TPU v7x, 32 devices: a whole 2x2x4 slice. The times are simulated.
32 devices in a mesh: strip: 2 (over x), sub: 16 (over z, y, core).
Axes of the slice: x: 2, y: 2, z: 4, core: 2. Of those that a mesh axis runs over, the one named last changes fastest.
Arguments:
- images: float32 [2, 64, 262144], P(None, None, ('strip', 'sub')), parts along dimension 2, may hold values from -6 to 6
- band_shift: int32 [32, 2, 2, 64, 64], P(('strip', 'sub')), parts along dimension 0, may hold values from 0 to 3
- tap_weights: float32 [32, 2, 2, 64, 4], P(('strip', 'sub')), parts along dimension 0, may hold values from -3 to 3
- phases: float32 [32, 2, 2, 64, 2], P(('strip', 'sub')), parts along dimension 0, may hold values from -3.140625 to 3.140625
- extent_map: int32 [32], P('strip'), parts along dimension 0, may hold values from 16 to 48, as said below
Outputs:
- packed: float32 [2, 64, 131072], P(None, None, ('strip', 'sub')), parts along dimension 2
There are 2 independent parts, one for each index of `strip`. A program takes and returns all parts, laid end to end along the dimension named above; each array names one. Nothing has to cross between parts.
Inputs may be any that keep to these rules, and one draw needn't show every extreme that they name: For every k, extent_map[2k] + extent_map[2k + 1] = 64.
All inputs are finite; a program needn't handle non-finite values.
Results may differ from a plain program's by a relative error of at most 0.0003.
Values sent between devices are 32-bit elements; how exact they have to be, the bound alone decides.
No kernel may reach another device: no remote copies, remote signals or barrier semaphores. Data moves between devices by JAX's collectives and lax.ppermute only.
A program may use at most 128 MiB of HBM per device.

v0:
```python
import functools

import jax
import jax.numpy as jnp
from jax import lax
from jax.experimental import pallas as pl
from jax.experimental.pallas import tpu as pltpu
from jax.sharding import PartitionSpec as P

BLK = 128
ROW = 32
QRT = 16
CHUNKS = (14, 10, 8)


class Sizes:
    def __init__(self, slots, total_rows):
        self.slots = slots
        self.total = total_rows
        self.right = slots + 1
        self.middle = slots + 2
        self.zero = slots + 3
        self.used = slots + 3
        self.cols = 3 * slots // 2 + 1


ANY = pl.BlockSpec(memory_space=pl.ANY)
SMEM = pl.BlockSpec(memory_space=pltpu.SMEM)
F32 = jnp.float32


def shape(*dims):
    return jax.ShapeDtypeStruct(dims, F32)


def call(body, ins, outs, scratch, flops, aliases=None):
    size = sum(4 * x.size for x in ins) + sum(4 * x.size for x in outs)
    return pl.pallas_call(
        body,
        out_shape=tuple(outs),
        in_specs=[SMEM] + [ANY] * (len(ins) - 1),
        out_specs=tuple([ANY] * len(outs)),
        scratch_shapes=scratch,
        input_output_aliases=aliases or {},
        compiler_params=pltpu.CompilerParams(vmem_limit_bytes=48 * 2**20),
        cost_estimate=pl.CostEstimate(flops=flops, bytes_accessed=size, transcendentals=0),
    )(*ins)


def place(extent_ref):
    pos = lax.axis_index("sub")
    top = lax.axis_size("sub").bit_length() - 2
    core = pos & 1
    side = (pos >> top) & 1
    even = pos - core
    return core, side, extent_ref[even], extent_ref[even ^ (1 << top)]


def copy_block(images_ref, dst, side, part, block, sem):
    rows = pl.ds(pl.multiple_of(part * 2 * QRT + side * QRT, QRT), QRT)
    lanes = pl.ds(pl.multiple_of(block * BLK, BLK), BLK)
    pltpu.make_async_copy(images_ref.at[:, rows, lanes], dst, sem).start()


def copy_slots(images_ref, dst_ref, base, side, extent, first, count, sem):
    def step(i, carry):
        slot = first + i
        part = (slot >= extent).astype(jnp.int32)
        copy_block(images_ref, dst_ref.at[base + i], side, part, slot - part * extent, sem)
        return carry

    lax.fori_loop(0, count, step, 0)


def copy_halo(images_ref, dst_ref, left_at, right_at, middle_at, side, extent, first, slots, sem):
    part = (first >= extent).astype(jnp.int32)
    block = jnp.maximum(first - part * extent - 1, 0)
    copy_block(images_ref, dst_ref.at[left_at], side, part, block, sem)
    last = first + slots - 1
    part = (last >= extent).astype(jnp.int32)
    copy_block(images_ref, dst_ref.at[right_at], side, part, last - part * extent + 1, sem)
    copy_block(images_ref, dst_ref.at[middle_at], side, 0, extent, sem)


def wait_whole(ref, sem):
    pltpu.make_async_copy(ref, ref, sem).wait()


def first_pack(sz, extent_ref, images_ref, same_ref, cross_ref, sems):
    core, side, _, extent = place(extent_ref)
    count = same_ref.shape[0]
    copy_slots(images_ref, same_ref, 0, 1 - side, extent, core * sz.slots, count, sems.at[0])
    copy_slots(images_ref, cross_ref, 0, 1 - side, extent, (1 - core) * sz.slots, count, sems.at[1])
    wait_whole(same_ref, sems.at[0])
    wait_whole(cross_ref, sems.at[1])


def rest_pack(sz, chunks, extent_ref, images_ref, par0_ref, par1_ref, *rest):
    outs, sems = rest[:-1], rest[-1]
    halo_same, halo_cross, mate, kept = outs[:4]
    core, side, own, other = place(extent_ref)
    slots = sz.slots
    n = 0
    for ref, window in ((halo_same, core), (halo_cross, 1 - core)):
        copy_halo(images_ref, ref, 0, 1, 2, 1 - side, other, window * slots, slots, sems.at[n])
        pltpu.make_async_copy(par0_ref.at[1 - side], ref.at[3], sems.at[n]).start()
        n += 1
    begin = chunks[0]
    for k, count in enumerate(chunks[1:]):
        for ref, window in ((outs[4 + 2 * k], core), (outs[5 + 2 * k], 1 - core)):
            copy_slots(images_ref, ref, 0, 1 - side, other, window * slots + begin, count, sems.at[n + 2])
            n += 1
        begin += count
    for at, ref, window in ((2, mate, 1 - core), (3, kept, core)):
        copy_slots(images_ref, ref, 1, side, own, window * slots, slots, sems.at[at])
        copy_halo(images_ref, ref, 0, sz.right, sz.middle, side, own, window * slots, slots, sems.at[at])
    pltpu.make_async_copy(par0_ref.at[side], mate.at[sz.used], sems.at[2]).start()
    pltpu.make_async_copy(par1_ref.at[0], mate.at[sz.used + 1], sems.at[2]).start()
    pltpu.make_async_copy(par1_ref.at[1], mate.at[sz.used + 2], sems.at[2]).start()
    for i, ref in enumerate(outs):
        wait_whole(ref, sems.at[i])


def build_tables(sz, par_ref, tab_ref, ltab_ref, groups, extent, first):
    lane = lax.broadcasted_iota(jnp.int32, (QRT, BLK), 1)
    even = first + lane - 1 < extent
    middle = lane == sz.middle
    even = jnp.logical_or(even, middle)
    block = jnp.where(even, first - 1 + lane, first - 1 + lane - extent)
    block = jnp.where(middle, extent, block).astype(F32)
    for group in range(groups):
        rows = [par_ref[p, pl.ds(group, QRT, stride=groups), :] for p in range(2)]
        for s in range(2):
            off = s * (BLK // 2)

            def column(c):
                return jnp.where(
                    even,
                    jnp.broadcast_to(rows[0][:, off + c : off + c + 1], (QRT, BLK)),
                    jnp.broadcast_to(rows[1][:, off + c : off + c + 1], (QRT, BLK)),
                )

            turn = lambda x, by: pltpu.roll(x, jnp.bitwise_and(by, BLK - 1), 1)
            shift = jnp.where(
                even, turn(rows[0], 1 - first - off), turn(rows[1], 1 - first + extent - off)
            )
            shift = jnp.where(middle, turn(rows[0], sz.middle - extent - off), shift)
            taps = [column(sz.cols + k) for k in range(4)]
            for o in range(-1, 6):
                weight = jnp.zeros((QRT, BLK), F32)
                for k in range(4):
                    if 0 <= o + 1 - k <= 3:
                        weight = weight + jnp.where(shift == float(o + 1 - k), taps[k], 0.0)
                tab_ref[s, group, o + 1] = weight
            angle = column(sz.cols + 4) + column(sz.cols + 5) * (block * (BLK / sz.total))
            tab_ref[s, group, 7] = jnp.cos(angle)
            tab_ref[s, group, 8] = jnp.sin(angle)
            for p in range(2):
                c = off + sz.cols + 5
                angle = jnp.broadcast_to(rows[p][:, c : c + 1], (QRT, BLK)) * (
                    lane.astype(F32) / sz.total
                )
                ltab_ref[p, s, group, 0] = jnp.cos(angle)
                ltab_ref[p, s, group, 1] = jnp.sin(angle)


def merge_block(load, tab_ref, ltab_ref, groups, x, before, after, part, h, store):
    lane = lax.broadcasted_iota(jnp.int32, (8, BLK), 1)
    pick = jnp.full((8, BLK), x, jnp.int32)
    rows = pl.ds(8 * h, 8)
    sums = [[None, None], [None, None]]
    for s in range(2):
        moved = []
        for ri in range(2):
            cur, prv, nxt = load(s, x, ri), load(s, before, ri), load(s, after, ri)
            views = [pltpu.roll(jnp.where(lane == BLK - 1, prv, cur), 1, 1), cur]
            for o in range(1, 6):
                views.append(pltpu.roll(jnp.where(lane < o, nxt, cur), BLK - o, 1))
            moved.append(views)
        for u in range(2):
            spread = [
                jnp.take_along_axis(tab_ref[s, groups[u], k, rows, :], pick, axis=1) for k in range(9)
            ]
            value = []
            for ri in range(2):
                total = spread[0] * moved[ri][0]
                for k in range(1, 7):
                    total = total + spread[k] * moved[ri][k]
                value.append(total)
            cl = ltab_ref[part, s, groups[u], 0, rows, :]
            sl = ltab_ref[part, s, groups[u], 1, rows, :]
            cosine = spread[7] * cl - spread[8] * sl
            sine = spread[8] * cl + spread[7] * sl
            real = cosine * value[0] - sine * value[1]
            imag = sine * value[0] + cosine * value[1]
            sums[u] = [real, imag] if s == 0 else [sums[u][0] + real, sums[u][1] + imag]
    for u in range(2):
        for ri in range(2):
            store(u, ri, sums[u][ri])


def level_one(sz, d_ref, f_ref, tab_ref, ltab_ref, x, before, after, part):
    for h in range(2):
        rows = lambda ri: pl.ds(QRT * ri + 8 * h, 8)

        def store(u, ri, value):
            f_ref[x, u, rows(ri), :] = value

        merge_block(
            lambda s, at, ri: d_ref[s, at, rows(ri), :],
            tab_ref, ltab_ref, (0, 1), x, before, after, part, h, store,
        )


def level_two(sz, f_ref, out_ref, at, tab_ref, ltab_ref, x, before, after, part):
    for u1 in range(2):
        for h in range(2):
            rows = pl.ds(8 * h, 8)

            def store(u, ri, value):
                out_ref[at, ri, pl.ds(32 * h + 2 * u1 + u, 8, stride=4), :] = value

            merge_block(
                lambda s, pos, ri: f_ref[s, pos, u1, pl.ds(QRT * ri + 8 * h, 8), :],
                tab_ref, ltab_ref, (2 * u1, 2 * u1 + 1), x, before, after, part, h, store,
            )


def neighbours(sz, slot, first, extent):
    where = first + slot
    before = jnp.where(jnp.logical_or(where == 0, where == extent), sz.zero, slot)
    after = jnp.where(where == extent - 1, sz.middle, slot + 2)
    return before, after, (where >= extent).astype(jnp.int32)


def edge_part(sz, slot, first, extent):
    return (first + slot >= extent).astype(jnp.int32)


def level_one_slots(sz, begin, end, first, extent, *refs):
    def step(slot, carry):
        before, after, part = neighbours(sz, slot, first, extent)
        level_one(sz, *refs, slot + 1, before, after, part)
        return carry

    lax.fori_loop(begin, end, step, 0)


def level_one_middle(sz, low, high, first, extent, *refs):
    before = jnp.clip(extent - first, low + 1, high)
    level_one(sz, *refs, sz.middle, before, sz.zero, 0)


def run_copies(copies, sems):
    handles = [pltpu.make_async_copy(src, dst, sems.at[i]) for i, (src, dst) in enumerate(copies)]
    for handle in handles:
        handle.start()
    for handle in handles:
        handle.wait()


def local_body(sz, extent_ref, kept, mate, par0, par1, own_f, tab2_out, ltab2_out,
               d, f, par1s, par2s, tab, ltab, tab2, ltab2, sems, out_sems):
    core, side, extent, _ = place(extent_ref)
    first = core * sz.slots
    used = sz.used
    run_copies(
        [
            (kept, d.at[core, pl.ds(0, used)]),
            (mate.at[pl.ds(0, used)], d.at[1 - core, pl.ds(0, used)]),
            (par0.at[side], par1s.at[core]),
            (mate.at[used], par1s.at[1 - core]),
            (par1, par2s.at[core]),
            (mate.at[used + 1], par2s.at[1 - core, pl.ds(0, ROW)]),
            (mate.at[used + 2], par2s.at[1 - core, pl.ds(ROW, ROW)]),
        ],
        sems,
    )
    for s in range(2):
        d[s, sz.zero] = jnp.zeros((ROW, BLK), F32)
    build_tables(sz, par1s, tab, ltab, 2, extent, first)
    build_tables(sz, par2s, tab2, ltab2, 4, extent, first)
    refs = (d, f, tab, ltab)
    level_one(sz, *refs, 0, 0, 1, edge_part(sz, 0, first, extent))
    level_one_slots(sz, 0, sz.slots, first, extent, *refs)
    level_one(sz, *refs, sz.right, sz.slots, sz.zero, edge_part(sz, sz.slots - 1, first, extent))
    level_one_middle(sz, 0, sz.slots, first, extent, *refs)
    run_copies([(f, own_f), (tab2, tab2_out), (ltab2, ltab2_out)], out_sems)


def other_tables_body(sz, extent_ref, halo_same, halo_cross, tab_out, ltab_out, pars, tab, ltab, sems):
    core, _, extent, _ = place(extent_ref)
    run_copies([(halo_same.at[3], pars.at[core]), (halo_cross.at[3], pars.at[1 - core])], sems)
    build_tables(sz, pars, tab, ltab, 2, extent, core * sz.slots)
    run_copies([(tab, tab_out), (ltab, ltab_out)], sems)


def main_body(sz, begin, count, passes, extent_ref, *rest):
    head, last = begin == 0, begin + count == sz.slots
    ins = list(rest)
    take = ins.pop
    same, cross, halo_same, halo_cross, own_f, tab1_in, ltab1_in, tab2_in, ltab2_in = ins[:9]
    ins = ins[9:]
    if not head:
        dtail_in, ftail_in, _ = ins[:3]
        ins = ins[3:]
    ins = ins[passes:]
    out = ins[0]
    ins = ins[1:]
    if not last:
        dtail_out, ftail_out = ins[:2]
        ins = ins[2:]
    ins = ins[passes:]
    d, f, tab1, ltab1, tab2, ltab2, o, sems, out_sem = ins
    core, _, extent, _ = place(extent_ref)
    side = place(extent_ref)[1]
    first = core * sz.slots
    end = begin + count
    mine, theirs = core, 1 - core
    low = 0 if head else begin - 2
    copies = [
        (same, d.at[mine, pl.ds(begin + 1, count)]),
        (cross, d.at[theirs, pl.ds(begin + 1, count)]),
        (halo_same.at[pl.ds(1, 2)], d.at[mine, pl.ds(sz.right, 2)]),
        (halo_cross.at[pl.ds(1, 2)], d.at[theirs, pl.ds(sz.right, 2)]),
        (tab1_in, tab1),
        (ltab1_in, ltab1),
        (tab2_in, tab2),
        (ltab2_in, ltab2),
    ]
    fl, fh = max(low - 1, -1) + 1, (end + 1 if last else end)
    copies.append((own_f.at[pl.ds(fl, fh - fl)], f.at[side, pl.ds(fl, fh - fl)]))
    copies.append((own_f.at[sz.middle], f.at[side, sz.middle]))
    if last:
        copies.append((own_f.at[sz.right], f.at[side, sz.right]))
    if head:
        copies.append((halo_same.at[0], d.at[mine, 0]))
        copies.append((halo_cross.at[0], d.at[theirs, 0]))
    else:
        copies.append((dtail_in, d.at[:, pl.ds(begin - 1, 2)]))
        copies.append((ftail_in, f.at[1 - side, pl.ds(begin - 2, 2)]))
    run_copies(copies, sems)
    for s in range(2):
        d[s, sz.zero] = jnp.zeros((ROW, BLK), F32)
        for u in range(2):
            f[s, sz.zero, u] = jnp.zeros((ROW, BLK), F32)
    refs = (d, f.at[1 - side], tab1, ltab1)
    if head:
        level_one(sz, *refs, 0, 0, 1, edge_part(sz, 0, first, extent))
    level_one_slots(sz, 0 if head else begin - 1, end if last else end - 1, first, extent, *refs)
    if last:
        level_one(sz, *refs, sz.right, sz.slots, sz.zero, edge_part(sz, sz.slots - 1, first, extent))
    level_one_middle(sz, low, end, first, extent, *refs)
    top = end if last else end - 2

    def step(slot, carry):
        before, after, part = neighbours(sz, slot, first, extent)
        level_two(sz, f, o, slot - low, tab2, ltab2, slot + 1, before, after, part)
        lanes = pl.ds(pl.multiple_of(slot * BLK, BLK), BLK)
        pltpu.make_async_copy(o.at[slot - low], out.at[:, :, lanes], out_sem).start()
        return carry

    lax.fori_loop(low, top, step, 0)
    if not last:
        run_copies(
            [(d.at[:, pl.ds(end - 1, 2)], dtail_out), (f.at[1 - side, pl.ds(end - 2, 2)], ftail_out)],
            sems,
        )
    pltpu.make_async_copy(o, o, out_sem).wait()


def per_device(images, band_shift, tap_weights, phases, extent_map):
    total_rows = images.shape[2]
    beams = images.shape[1]
    assert beams == 4 * QRT
    slots = total_rows // BLK // 2
    sz = Sizes(slots, total_rows)
    chunks = CHUNKS
    assert sum(chunks) == slots and sz.cols + 6 <= BLK // 2 and sz.zero < BLK
    size = lax.axis_size("sub")
    top = 1 << (size.bit_length() - 2)
    dma = pltpu.SemaphoreType.DMA
    swap = lambda x, by: lax.ppermute(x, "sub", [(i, i ^ by) for i in range(size)])
    block = lambda n: shape(n, 2, QRT, BLK)
    flat = lambda x: x.reshape(x.shape[0], ROW, BLK)

    same0, cross0 = call(
        functools.partial(first_pack, sz), [extent_map, images],
        [block(chunks[0])] * 2, [dma((2,))], 0,
    )
    got = [(flat(swap(same0, top)), flat(swap(cross0, top ^ 1)))]

    par = jnp.concatenate(
        [
            band_shift[0, :, :, :, : sz.cols].astype(F32),
            tap_weights[0],
            phases[0],
            jnp.zeros((2, 2, beams, BLK // 2 - sz.cols - 6), F32),
        ],
        axis=3,
    )
    par = jnp.concatenate([par[:, 0], par[:, 1]], axis=2)
    par0, par1 = (par[i].reshape(2, 2, QRT, BLK) for i in range(2))

    outs = [block(4)] * 2 + [block(sz.used + 3), block(sz.used)]
    for count in chunks[1:]:
        outs += [block(count)] * 2
    packed = call(
        functools.partial(rest_pack, sz, chunks), [extent_map, images, par0, par1],
        outs, [dma((len(outs),))], 0,
    )
    halo = [flat(swap(packed[0], top)), flat(swap(packed[1], top ^ 1))]
    mate = flat(swap(packed[2], 1))
    kept = flat(packed[3])
    got.append((flat(swap(packed[4], top)), flat(swap(packed[5], top ^ 1))))
    waiting = list(packed[6:])

    tabs1, ltabs1 = shape(2, 2, 9, QRT, BLK), shape(2, 2, 2, 2, QRT, BLK)
    tabs2, ltabs2 = shape(2, 4, 9, QRT, BLK), shape(2, 2, 4, 2, QRT, BLK)
    vm = lambda s: pltpu.VMEM(s.shape, F32)
    d_s, f_s = shape(2, sz.zero + 1, ROW, BLK), shape(sz.used, 2, ROW, BLK)
    own_f, tab2, ltab2 = call(
        functools.partial(local_body, sz),
        [extent_map, kept, mate, par0.reshape(2, ROW, BLK), par1.reshape(2 * ROW, BLK)],
        [f_s, tabs2, ltabs2],
        [vm(d_s), vm(f_s), vm(shape(2, ROW, BLK)), vm(shape(2, 2 * ROW, BLK)),
         vm(tabs1), vm(ltabs1), vm(tabs2), vm(ltabs2), dma((7,)), dma((3,))],
        10**8,
    )
    tab1, ltab1 = call(
        functools.partial(other_tables_body, sz), [extent_map] + halo, [tabs1, ltabs1],
        [vm(shape(2, ROW, BLK)), vm(tabs1), vm(ltabs1), dma((2,))], 10**6,
    )

    begin = 0
    out = None
    for k, count in enumerate(chunks):
        head, last = k == 0, k == len(chunks) - 1
        ins = [extent_map, *got[k], *halo, own_f, tab1, ltab1, tab2, ltab2]
        outs = [shape(2, beams, slots * BLK)]
        aliases = {}
        if not head:
            aliases[len(ins) + 2] = 0
            ins += [dtail, ftail, out]
        if not last:
            outs += [shape(2, 2, ROW, BLK), shape(2, 2, ROW, BLK)]
        passes = waiting[:2]
        waiting = waiting[2:]
        for x in passes:
            aliases[len(ins)] = len(outs)
            ins.append(x)
            outs.append(shape(*x.shape))
        low = 0 if head else begin - 2
        done = (begin + count if last else begin + count - 2) - low
        res = call(
            functools.partial(main_body, sz, begin, count, len(passes)), ins, outs,
            [vm(d_s), vm(shape(2, sz.zero + 1, 2, ROW, BLK)), vm(tabs1), vm(ltabs1), vm(tabs2), vm(ltabs2),
             vm(shape(done, 2, beams, BLK)), dma((14,)), dma],
            10**7 * count, aliases,
        )
        out = res[0]
        if not last:
            dtail, ftail = res[1:3]
        if passes:
            same, cross = res[-2:]
            got.append((flat(swap(same, top)), flat(swap(cross, top ^ 1))))
        begin += count
    return out


def solution(mesh):
    placed = (
        P(None, None, ("strip", "sub")),
        P(("strip", "sub"), None, None, None, None),
        P(("strip", "sub"), None, None, None, None),
        P(("strip", "sub"), None, None, None, None),
        P("strip"),
    )
    return jax.shard_map(
        per_device,
        mesh=mesh,
        in_specs=placed,
        out_specs=P(None, None, ("strip", "sub")),
        check_vma=False,
    )
```

profile of v0, /device:TPU:9, one launch (start us, length us, event | category | flops | bytes accessed | tf_op | source)
XLA Modules:
  0.0 88.3 jit_solution(14698113273177104984)
XLA Ops:
  0.0 0.9 %fusion = f32[2,2,64,49]{3,2,0,1:T(8,128)S(1)} fusion(s32[1,2,2,64,64]{4,3,2,1,0:T(8,128)} %param.6), kind=kLoop, calls=%fused_computation.2 | loop fusion | flops 12544 | bytes 115712 | tf_op jit(solution)/shard_map/convert_element_type | solution.py:395
  0.9 0.8 copy.11
  1.7 0.8 copy.12
  2.5 0.1 pad.5.clone
  2.6 0.1 maximum_maximum_fusion
  2.8 0.1 pad_maximum_fusion
  2.9 0.0 copy-start
  2.9 2.2 %copy-done = f32[2,64,8192]{2,1,0:T(8,128)S(1)} copy-done((f32[2,64,8192]{2,1,0:T(8,128)S(1)}, f32[2,64,8192]{2,1,0:T(8,128)}, u32[]{:S(2)}) %copy-start) | copy-done | bytes 4194328
  5.1 0.0 copy-start.1
  5.1 0.7 copy-done.1
  5.7 2.8 %shard_map.56 = (f32[4,2,16,128]{3,2,1,0:T(8,128)S(1)}, f32[4,2,16,128]{3,2,1,0:T(8,128)S(1)}, f32[38,2,16,128]{3,2,1,0:T(8,128)S(1)}, f32[35,2,16,128]{3,2,1,0:...) custom-call(s32[16]{0:T(128)S(1)} %copy-done.1, ...), custom_call_target="tpu_custom_call" | custom-call | bytes 6176832 | tf_op jit(solution)/shard_map/pallas_call | solution.py:38
  8.5 0.7 collective-permute-start.4
  9.2 1.0 %shard_map.55 = (f32[14,2,16,128]{3,2,1,0:T(8,128)S(1)}, f32[14,2,16,128]{3,2,1,0:T(8,128)S(1)}) custom-call(s32[16]{0:T(128)S(1)} %copy-done.1, f32[2,64,8192]{2,1,0:T(8,128)S(1)} %copy-done), custom_call_target="tpu_custom_call" | custom-call | bytes 4653120 | tf_op jit(solution)/shard_map/pallas_call | solution.py:38
  10.3 2.4 %collective-permute-start = (f32[14,2,16,128]{3,2,1,0:T(8,128)S(1)}, f32[14,2,16,128]{3,2,1,0:T(8,128)S(1)}, u32[]{:S(2)}, u32[]{:S(2)}) collective-permute-start(f32[14,2,16,128]{3,2,1,0:T(8,128)S(1)} %get-tuple-element.28), channel_id=1, source_target_pairs={{0,8},{1,9},{2,10},{3,11},{4,12},{5,13},{6,14},{7,15},{8,0},{9,1},... | collective-permute-start | bytes 688136 | tf_op jit(solution)/shard_map/ppermute | solution.py:383
  12.7 0.2 collective-permute-start.1
  12.9 2.3 %collective-permute-start.2 = (f32[4,2,16,128]{3,2,1,0:T(8,128)S(1)}, f32[4,2,16,128]{3,2,1,0:T(8,128)S(1)}, u32[]{:S(2)}, u32[]{:S(2)}) collective-permute-start(f32[4,2,16,128]{3,2,1,0:T(8,128)S(1)} %get-tuple-element.30), channel_id=1, source_target_pairs={{0,8},{1,9},{2,10},{3,11},{4,12},{5,13},{6,14},{7,15},{8,0},{9,1},... | collective-permute-start | bytes 196616 | tf_op jit(solution)/shard_map/ppermute | solution.py:383
  15.2 0.5 collective-permute-start.3
  15.7 21.2 %collective-permute-done.2 = f32[4,2,16,128]{3,2,1,0:T(8,128)S(1)} collective-permute-done((f32[4,2,16,128]{3,2,1,0:T(8,128)S(1)}, f32[4,2,16,128]{3,2,1,0:T(8,128)S(1)}, u32[]{:S(2)}, u32[]{:S(2)}) %collective-permute-start.2) | collective-permute-done | bytes 65568 | tf_op jit(solution)/shard_map/ppermute | solution.py:383
  36.9 3.1 %collective-permute-start.7 = (f32[10,2,16,128]{3,2,1,0:T(8,128)S(1)}, f32[10,2,16,128]{3,2,1,0:T(8,128)S(1)}, u32[]{:S(2)}, u32[]{:S(2)}) collective-permute-start(f32[10,2,16,128]{3,2,1,0:T(8,128)S(1)} %get-tuple-element.43), channel_id=1, source_target_pairs={{0,8},{1,9},{2,10},{3,11},{4,12},{5,13},{6,14},{7,15},{8,0},{9,1},... | collective-permute-start | bytes 491528 | tf_op jit(solution)/shard_map/ppermute | solution.py:383
  40.0 0.0 collective-permute-done.3
  40.0 8.7 %collective-permute-start.8 = (f32[10,2,16,128]{3,2,1,0:T(8,128)S(1)}, f32[10,2,16,128]{3,2,1,0:T(8,128)S(1)}, u32[]{:S(2)}, u32[]{:S(2)}) collective-permute-start(f32[10,2,16,128]{3,2,1,0:T(8,128)S(1)} %get-tuple-element.44), channel_id=1, source_target_pairs={{0,9},{1,8},{2,11},{3,10},{4,13},{5,12},{6,15},{7,14},{8,1},{9,0},... | collective-permute-start | bytes 491528 | tf_op jit(solution)/shard_map/ppermute | solution.py:383
  48.7 1.3 %shard_map.58 = (f32[2,2,9,16,128]{4,3,2,1,0:T(8,128)S(1)}, f32[2,2,2,2,16,128]{5,4,3,2,1,0:T(8,128)S(1)}) custom-call(s32[16]{0:T(128)S(1)} %copy-done.1, f32[4,32,128]{2,1,0:T(8,128)S(1)} %bitcast.22, f32[4,32,128]{2,1,0:T(8,128)S(1)} %bitcast.26), custom_call_target="tpu_custom_call" | custom-call | flops 1000000 | bytes 557120 | tf_op jit(solution)/shard_map/pallas_call | solution.py:38
  50.1 0.0 collective-permute-done.4
  50.1 9.6 %shard_map.57 = (f32[35,2,32,128]{3,2,1,0:T(8,128)S(1)}, f32[2,4,9,16,128]{4,3,2,1,0:T(8,128)S(1)}, f32[2,2,4,2,16,128]{5,4,3,2,1,0:T(8,128)S(1)}) custom-call(s32[16]{0:T(128)S(1)} %copy-done.1, f32[35,32,128]{2,1,0:T(8,128)S(1)} %bitcast.31, f32[38,32,128]{2,1,0:T(8,128)S(1)} %bitcast.30, f32[2,32,128]{2,1,0:T(8,128)S(1)} %bitcast.35, f32[64,128]{1,0:T(8,128)S(1)} %bitcast.33), custom_call_target="tpu_custom_call" | custom-call | flops 100000000 | bytes 3260480 | tf_op jit(solution)/shard_map/pallas_call | solution.py:38
  59.7 0.0 collective-permute-done
  59.7 0.0 collective-permute-done.1
  59.7 9.8 %shard_map.59 = (f32[2,64,4096]{2,1,0:T(8,128)}, f32[2,2,32,128]{3,2,1,0:T(8,128)S(1)}, f32[2,2,32,128]{3,2,1,0:T(8,128)S(1)}, f32[8,2,16,128]{3,2,1,0:T(8,128)S(1)}, f32[8,2,16,128]{3,2,1,0:T(8,128)S(1)}) custom-call(s32[16]{0:T(128)S(1)} %copy-done.1, f32[14,32,128]{2,1,0:T(8,128)S(1)} %bitcast.36, ...), custom_call_target="tpu_custom_call", output_to_operand_aliasing={{3}: (10, {}), {4}: (11, {})} | custom-call | flops 140000000 | bytes 5767232 | tf_op jit(solution)/shard_map/pallas_call | solution.py:38
  69.5 0.1 collective-permute-start.5
  69.5 2.6 %collective-permute-start.6 = (f32[8,2,16,128]{3,2,1,0:T(8,128)S(1)}, f32[8,2,16,128]{3,2,1,0:T(8,128)S(1)}, u32[]{:S(2)}, u32[]{:S(2)}) collective-permute-start(f32[8,2,16,128]{3,2,1,0:T(8,128)S(1)} %get-tuple-element.42), channel_id=1, source_target_pairs={{0,9},{1,8},{2,11},{3,10},{4,13},{5,12},{6,15},{7,14},{8,1},{9,0},... | collective-permute-start | bytes 393224 | tf_op jit(solution)/shard_map/ppermute | solution.py:383
  72.2 0.0 collective-permute-done.7
  72.2 0.0 collective-permute-done.8
  72.2 8.1 %shard_map.60 = (f32[2,64,4096]{2,1,0:T(8,128)}, f32[2,2,32,128]{3,2,1,0:T(8,128)S(1)}, f32[2,2,32,128]{3,2,1,0:T(8,128)S(1)}) custom-call(s32[16]{0:T(128)S(1)} %copy-done.1, f32[10,32,128]{2,1,0:T(8,128)S(1)} %bitcast.38, f32[10,32,128]{2,1,0:T(8,128)S(1)} %bitcast.39, f32[4,32,128]{2,1,0:T(8,128)S(1)} %bitcast.24, ...), custom_call_target="tpu_custom_call", output_to_operand_aliasing={{0}: (12, {})} | custom-call | flops 100000000 | bytes 7340096 | tf_op jit(solution)/shard_map/pallas_call | solution.py:38
  80.3 0.0 collective-permute-done.5
  80.3 0.0 collective-permute-done.6
  80.3 8.0 %shard_map.61 = f32[2,64,4096]{2,1,0:T(8,128)} custom-call(s32[16]{0:T(128)S(1)} %copy-done.1, f32[8,32,128]{2,1,0:T(8,128)S(1)} %bitcast.40, f32[8,32,128]{2,1,0:T(8,128)S(1)} %bitcast.41, f32[4,32,128]{2,1,0:T(8,128)S(1)} %bitcast.25, f32[4,32,128]{2,1,0:T(8,128)S(1)} %bitcast.29, ...), custom_call_target="tpu_custom_call", output_to_operand_aliasing={{}: (12, {})} | custom-call | flops 80000000 | bytes 7143488 | tf_op jit(solution)/shard_map/pallas_call | solution.py:38
  (2 shorter events, 0.0 us)
Async XLA Ops:
  2.9 2.2 %copy-start = (f32[2,64,8192]{2,1,0:T(8,128)S(1)}, f32[2,64,8192]{2,1,0:T(8,128)}, u32[]{:S(2)}) copy-start(f32[2,64,8192]{2,1,0:T(8,128)} %images_ref.3) | copy-start | bytes 12582916
  5.1 0.7 copy-start.1
  8.5 41.6 %collective-permute-start.4 = (f32[38,2,16,128]{3,2,1,0:T(8,128)S(1)}, f32[38,2,16,128]{3,2,1,0:T(8,128)S(1)}, u32[]{:S(2)}, u32[]{:S(2)}) collective-permute-start(f32[38,2,16,128]{3,2,1,0:T(8,128)S(1)} %get-tuple-element.33), channel_id=1, source_target_pairs={{0,1},{1,0},{2,3},{3,2},{4,5},{5,4},{6,7},{7,6},{8,9},{9,8},{10,11... | collective-permute-start | bytes 1867784 | tf_op jit(solution)/shard_map/ppermute | solution.py:383
  10.3 49.4 %collective-permute-start = (f32[14,2,16,128]{3,2,1,0:T(8,128)S(1)}, f32[14,2,16,128]{3,2,1,0:T(8,128)S(1)}, u32[]{:S(2)}, u32[]{:S(2)}) collective-permute-start(f32[14,2,16,128]{3,2,1,0:T(8,128)S(1)} %get-tuple-element.28), channel_id=1, source_target_pairs={{0,8},{1,9},{2,10},{3,11},{4,12},{5,13},{6,14},{7,15},{8,0},{9,1},... | collective-permute-start | bytes 688136 | tf_op jit(solution)/shard_map/ppermute | solution.py:383
  12.7 47.0 %collective-permute-start.1 = (f32[14,2,16,128]{3,2,1,0:T(8,128)S(1)}, f32[14,2,16,128]{3,2,1,0:T(8,128)S(1)}, u32[]{:S(2)}, u32[]{:S(2)}) collective-permute-start(f32[14,2,16,128]{3,2,1,0:T(8,128)S(1)} %get-tuple-element.29), channel_id=1, source_target_pairs={{0,9},{1,8},{2,11},{3,10},{4,13},{5,12},{6,15},{7,14},{8,1},{9,0},... | collective-permute-start | bytes 688136 | tf_op jit(solution)/shard_map/ppermute | solution.py:383
  12.9 24.0 %collective-permute-start.2 = (f32[4,2,16,128]{3,2,1,0:T(8,128)S(1)}, f32[4,2,16,128]{3,2,1,0:T(8,128)S(1)}, u32[]{:S(2)}, u32[]{:S(2)}) collective-permute-start(f32[4,2,16,128]{3,2,1,0:T(8,128)S(1)} %get-tuple-element.30), channel_id=1, source_target_pairs={{0,8},{1,9},{2,10},{3,11},{4,12},{5,13},{6,14},{7,15},{8,0},{9,1},... | collective-permute-start | bytes 196616 | tf_op jit(solution)/shard_map/ppermute | solution.py:383
  15.2 24.8 %collective-permute-start.3 = (f32[4,2,16,128]{3,2,1,0:T(8,128)S(1)}, f32[4,2,16,128]{3,2,1,0:T(8,128)S(1)}, u32[]{:S(2)}, u32[]{:S(2)}) collective-permute-start(f32[4,2,16,128]{3,2,1,0:T(8,128)S(1)} %get-tuple-element.31), channel_id=1, source_target_pairs={{0,9},{1,8},{2,11},{3,10},{4,13},{5,12},{6,15},{7,14},{8,1},{9,0},... | collective-permute-start | bytes 196616 | tf_op jit(solution)/shard_map/ppermute | solution.py:383
  36.9 35.3 %collective-permute-start.7 = (f32[10,2,16,128]{3,2,1,0:T(8,128)S(1)}, f32[10,2,16,128]{3,2,1,0:T(8,128)S(1)}, u32[]{:S(2)}, u32[]{:S(2)}) collective-permute-start(f32[10,2,16,128]{3,2,1,0:T(8,128)S(1)} %get-tuple-element.43), channel_id=1, source_target_pairs={{0,8},{1,9},{2,10},{3,11},{4,12},{5,13},{6,14},{7,15},{8,0},{9,1},... | collective-permute-start | bytes 491528 | tf_op jit(solution)/shard_map/ppermute | solution.py:383
  40.0 32.2 %collective-permute-start.8 = (f32[10,2,16,128]{3,2,1,0:T(8,128)S(1)}, f32[10,2,16,128]{3,2,1,0:T(8,128)S(1)}, u32[]{:S(2)}, u32[]{:S(2)}) collective-permute-start(f32[10,2,16,128]{3,2,1,0:T(8,128)S(1)} %get-tuple-element.44), channel_id=1, source_target_pairs={{0,9},{1,8},{2,11},{3,10},{4,13},{5,12},{6,15},{7,14},{8,1},{9,0},... | collective-permute-start | bytes 491528 | tf_op jit(solution)/shard_map/ppermute | solution.py:383
  69.5 10.9 %collective-permute-start.5 = (f32[8,2,16,128]{3,2,1,0:T(8,128)S(1)}, f32[8,2,16,128]{3,2,1,0:T(8,128)S(1)}, u32[]{:S(2)}, u32[]{:S(2)}) collective-permute-start(f32[8,2,16,128]{3,2,1,0:T(8,128)S(1)} %get-tuple-element.41), channel_id=1, source_target_pairs={{0,8},{1,9},{2,10},{3,11},{4,12},{5,13},{6,14},{7,15},{8,0},{9,1},... | collective-permute-start | bytes 393224 | tf_op jit(solution)/shard_map/ppermute | solution.py:383
  69.5 10.8 %collective-permute-start.6 = (f32[8,2,16,128]{3,2,1,0:T(8,128)S(1)}, f32[8,2,16,128]{3,2,1,0:T(8,128)S(1)}, u32[]{:S(2)}, u32[]{:S(2)}) collective-permute-start(f32[8,2,16,128]{3,2,1,0:T(8,128)S(1)} %get-tuple-element.42), channel_id=1, source_target_pairs={{0,9},{1,8},{2,11},{3,10},{4,13},{5,12},{6,15},{7,14},{8,1},{9,0},... | collective-permute-start | bytes 393224 | tf_op jit(solution)/shard_map/ppermute | solution.py:383
where the time goes:
time: 88.6 us; the launch traced here: 88.3 us
  Pallas kernels  40.6 us (46%)
  waiting for transfers between devices  21.3 us (24%)
  starting transfers between devices  20.6 us (23%)
  local copies, waits for them, and re-layouts  4.53 us (5%)
  other arithmetic  1.13 us (1%)
    pallas_call x7, Pallas kernels, call(): pl.pallas_call(body, out_shape=tuple(outs), in_specs=[SMEM] + [ANY] * (le...  40.6 us
    ppermute x9, waiting for transfers between devices, per_device(): lax.ppermute(x, 'sub', [(i, i ^ by) for i in range(size)])  21.3 us
    ppermute x9, starting transfers between devices, per_device(): lax.ppermute(x, 'sub', [(i, i ^ by) for i in range(size)])  20.6 us
    unnamed x6, local copies, waits for them, and re-layouts  4.44 us
  transfers between devices with their start and end apart: 9, of which 1 were waited for; matrix products, arithmetic and copies ran while one was open for 0% of the time, Pallas kernels for 34%

commit v1 on v0

v1 whole, which is shorter than its diff:
```python
import functools

import jax
import jax.numpy as jnp
from jax import lax
from jax.experimental import pallas as pl
from jax.experimental.pallas import tpu as pltpu
from jax.sharding import PartitionSpec as P

BLK = 128
QRT = 16
ROW = 2 * QRT
CHUNKS = (12, 14, 6)

REACH = 10
BASE = (24, 72)


class Sizes:
    def __init__(self, slots, total_rows):
        self.slots = slots
        self.total = total_rows
        self.right = slots + 1
        self.middle = slots + 2
        self.zero = slots + 3
        self.used = slots + 3


F32 = jnp.float32
ANY, HBM, VMEM, SMEM = pl.ANY, pltpu.HBM, pltpu.VMEM, pltpu.SMEM
DMA = pltpu.SemaphoreType.DMA


def shape(*dims):
    return jax.ShapeDtypeStruct(dims, F32)


def call(body, ins, outs, scratch, aliases=None, grant=32):
    return pl.pallas_call(
        body,
        out_shape=tuple(x for x, _ in outs),
        in_specs=[pl.BlockSpec(memory_space=m) for _, m in ins],
        out_specs=tuple(pl.BlockSpec(memory_space=m) for _, m in outs),
        scratch_shapes=scratch,
        input_output_aliases=aliases or {},
        compiler_params=pltpu.CompilerParams(vmem_limit_bytes=grant * 2**20),
        cost_estimate=pl.CostEstimate(flops=1, bytes_accessed=1, transcendentals=0),
    )(*(x for x, _ in ins))


def place(extent_ref):
    pos = lax.axis_index("sub")
    top = lax.axis_size("sub").bit_length() - 2
    core = pos & 1
    side = (pos >> top) & 1
    even = pos - core
    return core, side, extent_ref[even], extent_ref[even ^ (1 << top)]


def copy_block(images_ref, dst, side, part, block, sem):
    rows = pl.ds(pl.multiple_of(part * 2 * QRT + side * QRT, QRT), QRT)
    lanes = pl.ds(pl.multiple_of(block * BLK, BLK), BLK)
    pltpu.make_async_copy(images_ref.at[:, rows, lanes], dst, sem).start()


def copy_slots(images_ref, dst_ref, base, side, extent, first, count, sem):
    def step(i, carry):
        slot = first + i
        part = (slot >= extent).astype(jnp.int32)
        copy_block(images_ref, dst_ref.at[base + i], side, part, slot - part * extent, sem)
        return carry

    lax.fori_loop(0, count, step, 0)


def copy_halo(images_ref, dst_ref, left_at, right_at, middle_at, side, extent, first, slots, sem):
    part = (first >= extent).astype(jnp.int32)
    block = jnp.maximum(first - part * extent - 1, 0)
    copy_block(images_ref, dst_ref.at[left_at], side, part, block, sem)
    last = first + slots - 1
    part = (last >= extent).astype(jnp.int32)
    copy_block(images_ref, dst_ref.at[right_at], side, part, last - part * extent + 1, sem)
    copy_block(images_ref, dst_ref.at[middle_at], side, 0, extent, sem)


def wait_whole(ref, sem):
    pltpu.make_async_copy(ref, ref, sem).wait()


def run_copies(copies, sems):
    handles = [pltpu.make_async_copy(src, dst, sems.at[i]) for i, (src, dst) in enumerate(copies)]
    for handle in handles:
        handle.start()
    for handle in handles:
        handle.wait()


def pack_body(sz, chunks, extent_ref, images_ref, shift_ref, taps_ref, phase_ref, *rest):
    sends = 2 + 2 * len(chunks)
    outs = rest[:sends]
    mate, kept, own_par = outs[-2], outs[-1], rest[sends]
    moved_ref, turned_ref, shifts_ref, edges_ref, made_ref, sems, edge_sem, made_sem = rest[sends + 1 :]
    core, side, own, other = place(extent_ref)
    slots = sz.slots
    windows = (core * slots, (1 - core) * slots)
    for i in range(2):
        copy_halo(images_ref, edges_ref.at[i], 0, 1, 2, 1 - side, other, windows[i], slots, edge_sem)
    begin = 0
    for k, count in enumerate(chunks):
        for i in range(2):
            at = 2 * k + i
            copy_slots(images_ref, outs[at], 0, 1 - side, other, windows[i] + begin, count, sems.at[at])
        begin += count
    for at, ref, window in ((sends - 2, mate, windows[1]), (sends - 1, kept, windows[0])):
        copy_slots(images_ref, ref, 1, side, own, window, slots, sems.at[at])
        copy_halo(images_ref, ref, 0, sz.right, sz.middle, side, own, window, slots, sems.at[at])

    half = BLK // 2
    for l in range(2):
        moved_ref[...] = jnp.zeros((BLK, BLK), F32)
        for s in range(2):
            at = BASE[s] + sz.used
            moved_ref[at : at + 4, 0:half] = taps_ref[l, s]
            moved_ref[at + 4 : at + 6, 0:half] = phase_ref[l, s]
            shifts_ref[l, s] = jnp.zeros((half, BLK), F32)
            shifts_ref[l, s, :, 0:half] = shift_ref[l, s].astype(F32)
        turned_ref[l] = moved_ref[...].T[0:half]
    lane = lax.broadcasted_iota(jnp.int32, (ROW, BLK), 1)

    def parameters(l, row, first, extent):
        rows = pl.ds(pl.multiple_of(row, ROW), ROW)
        result = turned_ref[l, rows, :]
        for s in range(2):
            shifts = shifts_ref[l, s, rows, :]
            at = BASE[s]
            turn = lambda by: pltpu.roll(shifts, jnp.bitwise_and(by, BLK - 1), 1)
            inside = jnp.logical_and(lane >= at, lane < at + sz.middle)
            result = jnp.where(inside, turn(at + 1 - first + core * extent), result)
            result = jnp.where(lane == at + sz.middle, turn(at + sz.middle - extent), result)
        return result

    for i, level, row in ((0, 0, side * ROW), (1, 1, 0), (2, 1, ROW)):
        made_ref[2 + i] = parameters(level, row, windows[1], own).reshape(2, QRT, BLK)
        own_par[i] = parameters(level, row, windows[0], own)
    wait_whole(edges_ref, edge_sem)
    for i in range(2):
        left, right, middle = (edges_ref[i, n].reshape(ROW, BLK) for n in range(3))
        result = parameters(0, (1 - side) * ROW, windows[i], other)
        result = jnp.where(lane < 2 * REACH, pltpu.roll(middle, REACH, 1), result)
        result = jnp.where(lane < REACH, right, result)
        result = jnp.where(lane >= BLK - 2, left, result)
        made_ref[i] = result.reshape(2, QRT, BLK)
        pltpu.make_async_copy(made_ref.at[i], outs[i].at[chunks[0]], made_sem).start()
    pltpu.make_async_copy(made_ref.at[pl.ds(2, 3)], mate.at[pl.ds(sz.used, 3)], made_sem).start()
    wait_whole(made_ref, made_sem)
    for at, ref in enumerate(outs):
        if at < 2:
            ref = ref.at[pl.ds(0, chunks[0])]
        elif at == sends - 2:
            ref = ref.at[pl.ds(0, sz.used)]
        wait_whole(ref, sems.at[at])


def build_tables(sz, par_ref, tab_ref, ltab_ref, groups, extent, first):
    lane = lax.broadcasted_iota(jnp.int32, (QRT, BLK), 1)
    middle = lane == sz.middle
    even = jnp.logical_or(first + lane - 1 < extent, middle)
    block = jnp.where(even, first - 1 + lane, first - 1 + lane - extent)
    block = jnp.where(middle, extent, block).astype(F32)
    for group in range(groups):
        rows = [par_ref[p, pl.ds(group, QRT, stride=groups), :] for p in range(2)]
        for s in range(2):

            def spread(p, n):
                c = BASE[s] + sz.used + n
                return jnp.broadcast_to(rows[p][:, c : c + 1], (QRT, BLK))

            column = lambda n: jnp.where(even, spread(0, n), spread(1, n))
            shift = jnp.where(
                even,
                pltpu.roll(rows[0], BLK - BASE[s], 1),
                pltpu.roll(rows[1], BLK - BASE[s], 1),
            )
            taps = [column(k) for k in range(4)]
            for o in range(-1, 6):
                weight = jnp.zeros((QRT, BLK), F32)
                for k in range(4):
                    if 0 <= o + 1 - k <= 3:
                        weight = weight + jnp.where(shift == float(o + 1 - k), taps[k], 0.0)
                tab_ref[s, group, o + 1] = weight
            angle = column(4) + column(5) * (block * (BLK / sz.total))
            tab_ref[s, group, 7] = jnp.cos(angle)
            tab_ref[s, group, 8] = jnp.sin(angle)
            for p in range(2):
                angle = spread(p, 5) * (lane.astype(F32) / sz.total)
                ltab_ref[p, s, group, 0] = jnp.cos(angle)
                ltab_ref[p, s, group, 1] = jnp.sin(angle)


def gathered(tab_ref, ltab_ref, s, group, x, part, rows):
    pick = jnp.full((8, BLK), x, jnp.int32)
    spread = [jnp.take_along_axis(tab_ref[s, group, k, rows, :], pick, axis=1) for k in range(9)]
    cl = ltab_ref[part, s, group, 0, rows, :]
    sl = ltab_ref[part, s, group, 1, rows, :]
    cosine = spread[7] * cl - spread[8] * sl
    sine = spread[8] * cl + spread[7] * sl
    return spread[:7] + [cosine, sine]


def merge_block(sources, load, coef, sums, x, before, after, store):
    lane = lax.broadcasted_iota(jnp.int32, (8, BLK), 1)
    for s in sources:
        moved = []
        for ri in range(2):
            cur, prv, nxt = load(s, x, ri), load(s, before, ri), load(s, after, ri)
            views = [pltpu.roll(jnp.where(lane == BLK - 1, prv, cur), 1, 1), cur]
            for o in range(1, 6):
                views.append(pltpu.roll(jnp.where(lane < o, nxt, cur), BLK - o, 1))
            moved.append(views)
        for u in range(2):
            *weights, cosine, sine = coef(s, u)
            value = []
            for ri in range(2):
                total = weights[0] * moved[ri][0]
                for k in range(1, 7):
                    total = total + weights[k] * moved[ri][k]
                value.append(total)
            real = cosine * value[0] - sine * value[1]
            imag = sine * value[0] + cosine * value[1]
            sums[u] = [real, imag] if sums[u] is None else [sums[u][0] + real, sums[u][1] + imag]
    for u in range(2):
        for ri in range(2):
            store(u, ri, sums[u][ri])


def level_one(d_ref, f_ref, coef, x, before, after):
    for h in range(2):
        rows = lambda ri: pl.ds(QRT * ri + 8 * h, 8)

        def store(u, ri, value):
            f_ref[x, u, rows(ri), :] = value

        merge_block(
            (0, 1), lambda s, at, ri: d_ref[s, at, rows(ri), :],
            lambda s, u: coef(pl.ds(8 * h, 8), s, u), [None, None], x, before, after, store,
        )


def level_two(f_ref, coef, start, store, x, before, after):
    for u1 in range(2):
        for h in range(2):
            sums = [start(2 * u1 + u, h) for u in range(2)]
            merge_block(
                (0,), lambda s, at, ri: f_ref[at, u1, pl.ds(QRT * ri + 8 * h, 8), :],
                lambda s, u: coef(pl.ds(8 * h, 8), 2 * u1 + u), sums, x, before, after,
                lambda u, ri, value: store(2 * u1 + u, h, ri, value),
            )


def neighbours(sz, slot, first, extent):
    where = first + slot
    before = jnp.where(jnp.logical_or(where == 0, where == extent), sz.zero, slot)
    after = jnp.where(where == extent - 1, sz.middle, slot + 2)
    return before, after, (where >= extent).astype(jnp.int32)


def loop(begin, end, body):
    def step(slot, carry):
        body(slot)
        return carry

    lax.fori_loop(begin, end, step, 0)


def level_one_all(sz, d_ref, f_ref, coef_at, slots, left, right, low, high, first, extent):
    part_of = lambda slot: (first + slot >= extent).astype(jnp.int32)

    def body(slot):
        before, after, part = neighbours(sz, slot, first, extent)
        level_one(d_ref, f_ref, coef_at(slot + 1, part), slot + 1, before, after)

    if left:
        level_one(d_ref, f_ref, coef_at(0, part_of(0)), 0, 0, 1)
    loop(*slots, body)
    if right:
        part = part_of(sz.slots - 1)
        level_one(d_ref, f_ref, coef_at(sz.right, part), sz.right, sz.slots, sz.zero)
    before = jnp.clip(extent - first, low + 1, high)
    level_one(d_ref, f_ref, coef_at(sz.middle, 0), sz.middle, before, sz.zero)


def table_coef(tab, ltab):
    return lambda x, part: (lambda rows, s, u: gathered(tab, ltab, s, u, x, part, rows))


def local_body(sz, extent_ref, kept, mate, par, share_out, tab2_out, ltab2_out,
               d, f, par1s, par2s, tab, ltab, share, tab2, ltab2, sems, out_sems):
    core, side, extent, _ = place(extent_ref)
    first = core * sz.slots
    used = sz.used
    run_copies(
        [
            (kept, d.at[core, pl.ds(0, used)]),
            (mate.at[pl.ds(0, used)], d.at[1 - core, pl.ds(0, used)]),
            (par.at[0], par1s.at[core]),
            (par.at[1], par2s.at[core, pl.ds(0, ROW)]),
            (par.at[2], par2s.at[core, pl.ds(ROW, ROW)]),
            (mate.at[used], par1s.at[1 - core]),
            (mate.at[used + 1], par2s.at[1 - core, pl.ds(0, ROW)]),
            (mate.at[used + 2], par2s.at[1 - core, pl.ds(ROW, ROW)]),
        ],
        sems,
    )
    zeros = jnp.zeros((ROW, BLK), F32)
    for s in range(2):
        d[s, sz.zero] = zeros
        f[sz.zero, s] = zeros
    build_tables(sz, par1s, tab, ltab, 2, extent, first)
    build_tables(sz, par2s, tab2, ltab2, 4, extent, first)
    level_one_all(
        sz, d, f, table_coef(tab, ltab), (0, sz.slots), True, True, 0, sz.slots, first, extent
    )

    def body(slot):
        before, after, part = neighbours(sz, slot, first, extent)

        def store(u, h, ri, value):
            share[slot, ri, u, pl.ds(8 * h, 8), :] = value

        level_two(
            f, lambda rows, u: gathered(tab2, ltab2, side, u, slot + 1, part, rows),
            lambda u, h: None, store, slot + 1, before, after,
        )

    loop(0, sz.slots, body)
    run_copies([(share, share_out), (tab2, tab2_out), (ltab2, ltab2_out)], out_sems)


def other_tables_body(sz, begin, extent_ref, halo_same, halo_cross, tab2, ltab2,
                      tab_out, ltab_out, wide1_out, wide2_out, pars, tab, ltab, wide1, wide2, sems):
    core, side, extent, _ = place(extent_ref)
    first = core * sz.slots
    pars[core] = halo_same[halo_same.shape[0] - 1]
    pars[1 - core] = halo_cross[halo_cross.shape[0] - 1]
    build_tables(sz, pars, tab, ltab, 2, extent, first)
    rows = lambda h: pl.ds(8 * h, 8)

    def spread_one(j, x, part):
        for s in range(2):
            for u in range(2):
                for h in range(2):
                    for k, value in enumerate(gathered(tab, ltab, s, u, x, part, rows(h))):
                        wide1[j, s, u, k, rows(h), :] = value

    def body_one(slot):
        _, _, part = neighbours(sz, slot, first, extent)
        spread_one(slot - begin + 1, slot + 1, part)

    def body_two(slot):
        _, _, part = neighbours(sz, slot, first, extent)
        for u in range(4):
            for h in range(2):
                values = gathered(tab2, ltab2, 1 - side, u, slot + 1, part, rows(h))
                for k, value in enumerate(values):
                    wide2[slot - begin + 2, u, k, rows(h), :] = value

    loop(begin - 1, sz.slots, body_one)
    count = sz.slots - begin
    _, _, part = neighbours(sz, sz.slots - 1, first, extent)
    spread_one(count + 1, sz.right, part)
    spread_one(count + 2, sz.middle, 0)
    loop(begin - 2, sz.slots, body_two)
    run_copies([(tab, tab_out), (ltab, ltab_out), (wide1, wide1_out), (wide2, wide2_out)], sems)


def gate_body(*refs):
    pass


def main_body(sz, begin, count, extent_ref, *rest):
    head, last = begin == 0, begin + count == sz.slots
    ins = list(rest)

    def take(n):
        part = ins[:n]
        del ins[:n]
        return part

    same, cross, halo_same, halo_cross, share = take(5)
    tables = take(2 if last else 4)
    if not head:
        dtail_in, ftail_in, _ = take(3)
    (out,) = take(1)
    if not last:
        dtail_out, ftail_out = take(2)
    d, f, o, out_sem = ins
    core, side, extent, _ = place(extent_ref)
    first = core * sz.slots
    end = begin + count
    low = 0 if head else begin - 2
    zeros = jnp.zeros((ROW, BLK), F32)
    for mine, chunk, halo in ((core, same, halo_same), (1 - core, cross, halo_cross)):
        for i in range(count):
            d[mine, begin + 1 + i] = chunk[i]
        edge = halo[halo.shape[0] - 1]
        if head:
            d[mine, 0] = edge
        if last:
            d[mine, sz.right] = edge
        d[mine, sz.middle] = pltpu.roll(edge, BLK - REACH, 1)
    for s in range(2):
        d[s, sz.zero] = zeros
        f[sz.zero, s] = zeros
        if not head:
            for i in range(2):
                d[s, begin - 1 + i] = dtail_in[s, i]
                f[begin - 2 + i, s] = ftail_in[i, s]

    if last:
        wide1, wide2 = tables

        def coef_at(x, part):
            if isinstance(x, int):
                j = count + 1 if x == sz.right else count + 2
            else:
                j = x - begin
            return lambda rows, s, u: [wide1[j, s, u, k, rows, :] for k in range(9)]
    else:
        tab1, ltab1, tab2, ltab2 = tables
        coef_at = table_coef(tab1, ltab1)
    slots = (0 if head else begin - 1, end if last else end - 1)
    level_one_all(sz, d, f, coef_at, slots, head, last, low, end, first, extent)

    def body(slot):
        before, after, part = neighbours(sz, slot, first, extent)
        at = slot - low

        def store(u, h, ri, value):
            o[at, ri, pl.ds(32 * h + u, 8, stride=4), :] = value

        if last:
            coef = lambda rows, u: [wide2[at, u, k, rows, :] for k in range(9)]
        else:
            coef = lambda rows, u: gathered(tab2, ltab2, 1 - side, u, slot + 1, part, rows)
        level_two(
            f, coef, lambda u, h: [share[slot, ri, u, pl.ds(8 * h, 8), :] for ri in range(2)],
            store, slot + 1, before, after,
        )
        lanes = pl.ds(pl.multiple_of(slot * BLK, BLK), BLK)
        pltpu.make_async_copy(o.at[at], out.at[:, :, lanes], out_sem).start()

    loop(low, end if last else end - 2, body)
    if not last:
        for s in range(2):
            for i in range(2):
                dtail_out[s, i] = d[s, end - 1 + i]
                ftail_out[i, s] = f[end - 2 + i, s]
    wait_whole(o, out_sem)


def per_device(images, band_shift, tap_weights, phases, extent_map):
    total_rows = images.shape[2]
    beams = images.shape[1]
    slots = total_rows // BLK // 2
    sz = Sizes(slots, total_rows)
    chunks = CHUNKS
    assert beams == 4 * QRT and sum(chunks) == slots and len(chunks) == 3
    assert sz.used + 6 <= BASE[1] - BASE[0] and BASE[1] + sz.used + 6 <= BLK - 2
    size = lax.axis_size("sub")
    top = 1 << (size.bit_length() - 2)
    swap = lambda x, by: lax.ppermute(x, "sub", [(i, i ^ by) for i in range(size)])
    block = lambda n: (shape(n, 2, QRT, BLK), VMEM)
    flat = lambda x: x.reshape(x.shape[0], ROW, BLK)
    extents = (extent_map, SMEM)
    vm = lambda *dims: VMEM(dims, F32)

    outs = [block(chunks[0] + 1)] * 2
    for count in chunks[1:]:
        outs += [block(count)] * 2
    outs += [block(sz.used + 3), block(sz.used), (shape(3, ROW, BLK), VMEM)]
    half = BLK // 2
    packed = call(
        functools.partial(pack_body, sz, chunks),
        [
            extents,
            (images, HBM),
            (band_shift[0], VMEM),
            (tap_weights[0].transpose(0, 1, 3, 2), VMEM),
            (phases[0].transpose(0, 1, 3, 2), VMEM),
        ],
        outs,
        [vm(BLK, BLK), vm(2, half, BLK), vm(2, 2, half, BLK), vm(2, 3, 2, QRT, BLK),
         vm(5, 2, QRT, BLK), DMA((len(outs),)), DMA, DMA],
        grant=56,
    )
    send = lambda a, b: (flat(swap(a, top)), flat(swap(b, top ^ 1)))
    got = [send(*packed[0:2]), send(*packed[2:4])]
    mate, kept, own_par = flat(swap(packed[6], 1)), flat(packed[7]), packed[8]
    halo = [(x, VMEM) for x in got[0]]

    tabs1, ltabs1 = (2, 2, 9, QRT, BLK), (2, 2, 2, 2, QRT, BLK)
    tabs2, ltabs2 = (2, 4, 9, QRT, BLK), (2, 2, 4, 2, QRT, BLK)
    shares = (slots, 2, 4, QRT, BLK)
    d_s, f_s = (2, sz.zero + 1, ROW, BLK), (sz.zero + 1, 2, ROW, BLK)
    share, tab2, ltab2 = call(
        functools.partial(local_body, sz),
        [extents, (kept, ANY), (mate, ANY), (own_par, ANY)],
        [(shape(*shares), ANY), (shape(*tabs2), ANY), (shape(*ltabs2), ANY)],
        [vm(*d_s), vm(*f_s), vm(2, ROW, BLK), vm(2, 2 * ROW, BLK), vm(*tabs1), vm(*ltabs1),
         vm(*shares), vm(*tabs2), vm(*ltabs2), DMA((8,)), DMA((3,))],
    )
    count = chunks[-1]
    wides1, wides2 = (count + 3, 2, 2, 9, QRT, BLK), (count + 2, 4, 9, QRT, BLK)
    tab1, ltab1, wide1, wide2 = call(
        functools.partial(other_tables_body, sz, slots - count),
        [extents, *halo, (tab2, VMEM), (ltab2, VMEM)],
        [(shape(*s), ANY) for s in (tabs1, ltabs1, wides1, wides2)],
        [vm(2, ROW, BLK), vm(*tabs1), vm(*ltabs1), vm(*wides1), vm(*wides2), DMA((4,))],
    )

    waiting = [(x, ANY) for x in packed[4:6]]
    opened = call(
        gate_body, waiting + [(x, ANY) for x in got[0]] + [(share, ANY)],
        waiting, [], {0: 0, 1: 1},
    )
    got.append(send(*opened))

    begin = 0
    tail = [(shape(2, 2, ROW, BLK), VMEM)] * 2
    for k, count in enumerate(chunks):
        head, last = k == 0, k == len(chunks) - 1
        ins = [extents, *((x, VMEM) for x in got[k]), *halo, (share, VMEM)]
        if last:
            ins += [(wide1, VMEM), (wide2, VMEM)]
        else:
            ins += [(x, VMEM) for x in (tab1, ltab1, tab2, ltab2)]
        outs = [(shape(2, beams, slots * BLK), HBM)]
        aliases = {}
        if not head:
            aliases[len(ins) + 2] = 0
            ins += [(dtail, VMEM), (ftail, VMEM), (out, HBM)]
        if not last:
            outs += tail
        low = 0 if head else begin - 2
        done = (begin + count if last else begin + count - 2) - low
        res = call(
            functools.partial(main_body, sz, begin, count), ins, outs,
            [vm(*d_s), vm(*f_s), vm(done, 2, beams, BLK), DMA], aliases,
        )
        out = res[0]
        if not last:
            dtail, ftail = res[1:]
        begin += count
    return out


def solution(mesh):
    placed = (
        P(None, None, ("strip", "sub")),
        P(("strip", "sub"), None, None, None, None),
        P(("strip", "sub"), None, None, None, None),
        P(("strip", "sub"), None, None, None, None),
        P("strip"),
    )
    return jax.shard_map(
        per_device,
        mesh=mesh,
        in_specs=placed,
        out_specs=P(None, None, ("strip", "sub")),
        check_vma=False,
    )
```

time: 88.6 us -> 63.9 us (0.72)
  the two profiles are of different devices: /device:TPU:9 before, /device:TPU:1 now
where the time goes in v1:
time: 63.9 us; the launch traced here: 63.5 us
  Pallas kernels  42.1 us (66%)
  starting transfers between devices  9.55 us (15%)
  waiting for transfers between devices  9.02 us (14%)
  local copies, waits for them, and re-layouts  2.75 us (4%)
    pallas_call x7, Pallas kernels, call(): pl.pallas_call(body, out_shape=tuple((x for x, _ in outs)), in_specs=[pl....  42.1 us
    ppermute x7, starting transfers between devices, per_device(): lax.ppermute(x, 'sub', [(i, i ^ by) for i in range(size)])  9.55 us
    ppermute x7, waiting for transfers between devices, per_device(): lax.ppermute(x, 'sub', [(i, i ^ by) for i in range(size)])  9.02 us
    unnamed x8, local copies, waits for them, and re-layouts  2.75 us
  transfers between devices with their start and end apart: 7, of which 3 were waited for; matrix products, arithmetic and copies ran while one was open for 0% of the time, Pallas kernels for 52%

profile of v1, /device:TPU:1, one launch (start us, length us, event | category | flops | bytes accessed | tf_op | source)
XLA Modules:
  0.0 63.5 jit_solution(8790814948473655505)
XLA Ops:
  0.0 0.0 copy-start.3
  0.0 5.4 %shard_map.55 = (f32[13,2,16,128]{3,2,1,0:T(8,128)}, f32[13,2,16,128]{3,2,1,0:T(8,128)}, f32[14,2,16,128]{3,2,1,0:T(8,128)}, f32[14,2,16,128]{3,2,1,0:T(8,128)},...) custom-call(s32[16]{0:T(128)} %extent_ref.11, ...), custom_call_target="tpu_custom_call" | custom-call | flops 1 | bytes 1 | tf_op jit(solution)/shard_map/pallas_call | solution.py:39
  5.4 0.1 collective-permute-start.2
  5.5 3.8 %collective-permute-start = (f32[13,2,16,128]{3,2,1,0:T(8,128)}, f32[13,2,16,128]{3,2,1,0:T(8,128)S(1)}, u32[]{:S(2)}, u32[]{:S(2)}) collective-permute-start(f32[13,2,16,128]{3,2,1,0:T(8,128)} %get-tuple-element.31), channel_id=1, source_target_pairs={{0,8},{1,9},{2,10},{3,11},{4,12},{5,13},{6,14},{7,15},{8,0},{9,1},... | collective-permute-start | bytes 638984 | tf_op jit(solution)/shard_map/ppermute | solution.py:471
  9.3 0.0 collective-permute-start.1
  9.3 2.6 %collective-permute-start.5 = (f32[14,2,16,128]{3,2,1,0:T(8,128)}, f32[14,2,16,128]{3,2,1,0:T(8,128)S(1)}, u32[]{:S(2)}, u32[]{:S(2)}) collective-permute-start(f32[14,2,16,128]{3,2,1,0:T(8,128)} %get-tuple-element.43), channel_id=1, source_target_pairs={{0,8},{1,9},{2,10},{3,11},{4,12},{5,13},{6,14},{7,15},{8,0},{9,1},... | collective-permute-start | bytes 688136 | tf_op jit(solution)/shard_map/ppermute | solution.py:471
  11.9 0.3 collective-permute-start.6
  12.2 0.0 collective-permute-done.2
  12.3 0.0 copy-done.3
  12.3 0.0 copy-start
  12.3 1.1 %copy-done = f32[35,2,16,128]{3,2,1,0:T(8,128)S(1)} copy-done((f32[35,2,16,128]{3,2,1,0:T(8,128)S(1)}, f32[35,2,16,128]{3,2,1,0:T(8,128)}, u32[]{:S(2)}) %copy-start) | copy-done | bytes 573464
  13.3 0.0 copy-start.2
  13.3 0.8 %copy-done.2 = f32[3,32,128]{2,1,0:T(8,128)S(1)} copy-done((f32[3,32,128]{2,1,0:T(8,128)S(1)}, f32[3,32,128]{2,1,0:T(8,128)}, u32[]{:S(2)}) %copy-start.2) | copy-done | bytes 49176
  14.1 16.1 %shard_map.56 = (f32[32,2,4,16,128]{4,3,2,1,0:T(8,128)S(1)}, f32[2,4,9,16,128]{4,3,2,1,0:T(8,128)S(1)}, f32[2,2,4,2,16,128]{5,4,3,2,1,0:T(8,128)S(1)}) custom-call(s32[16]{0:T(128)S(1)} %copy-done.3, f32[35,32,128]{2,1,0:T(8,128)S(1)} %bitcast.28, f32[38,32,128]{2,1,0:T(8,128)S(1)} %bitcast.27, f32[3,32,128]{2,1,0:T(8,128)S(1)} %copy-done.2), custom_call_target="tpu_custom_call" | custom-call | flops 1 | bytes 1 | tf_op jit(solution)/shard_map/pallas_call | solution.py:39
  30.2 3.8 %collective-permute-done = f32[13,2,16,128]{3,2,1,0:T(8,128)S(1)} collective-permute-done((f32[13,2,16,128]{3,2,1,0:T(8,128)}, f32[13,2,16,128]{3,2,1,0:T(8,128)S(1)}, u32[]{:S(2)}, u32[]{:S(2)}) %collective-permute-start) | collective-permute-done | bytes 213024 | tf_op jit(solution)/shard_map/ppermute | solution.py:471
  34.0 4.8 %collective-permute-done.1 = f32[13,2,16,128]{3,2,1,0:T(8,128)S(1)} collective-permute-done((f32[13,2,16,128]{3,2,1,0:T(8,128)}, f32[13,2,16,128]{3,2,1,0:T(8,128)S(1)}, u32[]{:S(2)}, u32[]{:S(2)}) %collective-permute-start.1) | collective-permute-done | bytes 213024 | tf_op jit(solution)/shard_map/ppermute | solution.py:471
  38.8 0.0 copy-start.1
  38.8 0.9 %copy-done.1 = f32[6,2,16,128]{3,2,1,0:T(8,128)S(1)} copy-done((f32[6,2,16,128]{3,2,1,0:T(8,128)S(1)}, f32[6,2,16,128]{3,2,1,0:T(8,128)}, u32[]{:S(2)}) %copy-start.1) | copy-done | bytes 98328
  39.7 0.0 collective-permute-start.3
  39.7 2.7 %collective-permute-start.4 = (f32[6,2,16,128]{3,2,1,0:T(8,128)S(1)}, f32[6,2,16,128]{3,2,1,0:T(8,128)S(1)}, u32[]{:S(2)}, u32[]{:S(2)}) collective-permute-start(f32[6,2,16,128]{3,2,1,0:T(8,128)S(1)} %get-tuple-element.38), channel_id=1, source_target_pairs={{0,9},{1,8},{2,11},{3,10},{4,13},{5,12},{6,15},{7,14},{8,1},{9,0},... | collective-permute-start | bytes 294920 | tf_op jit(solution)/shard_map/ppermute | solution.py:471
  42.4 4.1 %shard_map.58 = (f32[2,2,9,16,128]{4,3,2,1,0:T(8,128)S(1)}, f32[2,2,2,2,16,128]{5,4,3,2,1,0:T(8,128)S(1)}, f32[9,2,2,9,16,128]{5,4,3,2,1,0:T(8,128)S(1)}, f32[8,4,9,16,128]{4,3,2,1,0:T(8,128)S(1)}) custom-call(s32[16]{0:T(128)S(1)} %copy-done.3, f32[13,32,128]{2,1,0:T(8,128)S(1)} %bitcast.16, f32[13,32,128]{2,1,0:T(8,128)S(1)} %bitcast.22, ...), custom_call_target="tpu_custom_call" | custom-call | flops 1 | bytes 1 | tf_op jit(solution)/shard_map/pallas_call | solution.py:39
  46.5 5.9 %shard_map.59 = (f32[2,64,4096]{2,1,0:T(8,128)}, f32[2,2,32,128]{3,2,1,0:T(8,128)S(1)}, f32[2,2,32,128]{3,2,1,0:T(8,128)S(1)}) custom-call(s32[16]{0:T(128)S(1)} %copy-done.3, f32[13,32,128]{2,1,0:T(8,128)S(1)} %bitcast.17, f32[13,32,128]{2,1,0:T(8,128)S(1)} %bitcast.23, f32[13,32,128]{2,1,0:T(8,128)S(1)} %bitcast.18, f32[13,32,128]{2,1,0:T(8,128)S(1)} %bitcast.24, ...), custom_call_target="tpu_custom_call" | custom-call | flops 1 | bytes 1 | tf_op jit(solution)/shard_map/pallas_call | solution.py:39
  52.4 0.0 collective-permute-done.5
  52.4 0.4 collective-permute-done.6
  52.8 7.2 %shard_map.60 = (f32[2,64,4096]{2,1,0:T(8,128)}, f32[2,2,32,128]{3,2,1,0:T(8,128)S(1)}, f32[2,2,32,128]{3,2,1,0:T(8,128)S(1)}) custom-call(s32[16]{0:T(128)S(1)} %copy-done.3, f32[14,32,128]{2,1,0:T(8,128)S(1)} %bitcast.29, f32[14,32,128]{2,1,0:T(8,128)S(1)} %bitcast.30, f32[13,32,128]{2,1,0:T(8,128)S(1)} %bitcast.19, ...), custom_call_target="tpu_custom_call", output_to_operand_aliasing={{0}: (12, {})} | custom-call | flops 1 | bytes 1 | tf_op jit(solution)/shard_map/pallas_call | solution.py:39
  60.1 0.0 collective-permute-done.3
  60.1 0.0 collective-permute-done.4
  60.1 3.4 %shard_map.61 = f32[2,64,4096]{2,1,0:T(8,128)} custom-call(s32[16]{0:T(128)S(1)} %copy-done.3, f32[6,32,128]{2,1,0:T(8,128)S(1)} %bitcast.31, f32[6,32,128]{2,1,0:T(8,128)S(1)} %bitcast.32, f32[13,32,128]{2,1,0:T(8,128)S(1)} %bitcast.20, f32[13,32,128]{2,1,0:T(8,128)S(1)} %bitcast.26, ...), custom_call_target="tpu_custom_call", output_to_operand_aliasing={{}: (10, {})} | custom-call | flops 1 | bytes 1 | tf_op jit(solution)/shard_map/pallas_call | solution.py:39
  (1 shorter events, 0.0 us)
Async XLA Ops:
  0.0 12.3 %copy-start.3 = (s32[16]{0:T(128)S(1)}, s32[16]{0:T(128)}, u32[]{:S(2)}) copy-start(s32[16]{0:T(128)} %extent_ref.11) | copy-start | bytes 196
  5.4 6.8 %collective-permute-start.2 = (f32[38,2,16,128]{3,2,1,0:T(8,128)}, f32[38,2,16,128]{3,2,1,0:T(8,128)S(1)}, u32[]{:S(2)}, u32[]{:S(2)}) collective-permute-start(f32[38,2,16,128]{3,2,1,0:T(8,128)} %get-tuple-element.34), channel_id=1, source_target_pairs={{0,1},{1,0},{2,3},{3,2},{4,5},{5,4},{6,7},{7,6},{8,9},{9,8},{10,11... | collective-permute-start | bytes 1867784 | tf_op jit(solution)/shard_map/ppermute | solution.py:471
  5.5 28.5 %collective-permute-start = (f32[13,2,16,128]{3,2,1,0:T(8,128)}, f32[13,2,16,128]{3,2,1,0:T(8,128)S(1)}, u32[]{:S(2)}, u32[]{:S(2)}) collective-permute-start(f32[13,2,16,128]{3,2,1,0:T(8,128)} %get-tuple-element.31), channel_id=1, source_target_pairs={{0,8},{1,9},{2,10},{3,11},{4,12},{5,13},{6,14},{7,15},{8,0},{9,1},... | collective-permute-start | bytes 638984 | tf_op jit(solution)/shard_map/ppermute | solution.py:471
  9.3 29.5 %collective-permute-start.1 = (f32[13,2,16,128]{3,2,1,0:T(8,128)}, f32[13,2,16,128]{3,2,1,0:T(8,128)S(1)}, u32[]{:S(2)}, u32[]{:S(2)}) collective-permute-start(f32[13,2,16,128]{3,2,1,0:T(8,128)} %get-tuple-element.32), channel_id=1, source_target_pairs={{0,9},{1,8},{2,11},{3,10},{4,13},{5,12},{6,15},{7,14},{8,1},{9,0},... | collective-permute-start | bytes 638984 | tf_op jit(solution)/shard_map/ppermute | solution.py:471
  9.3 43.1 %collective-permute-start.5 = (f32[14,2,16,128]{3,2,1,0:T(8,128)}, f32[14,2,16,128]{3,2,1,0:T(8,128)S(1)}, u32[]{:S(2)}, u32[]{:S(2)}) collective-permute-start(f32[14,2,16,128]{3,2,1,0:T(8,128)} %get-tuple-element.43), channel_id=1, source_target_pairs={{0,8},{1,9},{2,10},{3,11},{4,12},{5,13},{6,14},{7,15},{8,0},{9,1},... | collective-permute-start | bytes 688136 | tf_op jit(solution)/shard_map/ppermute | solution.py:471
  11.9 40.9 %collective-permute-start.6 = (f32[14,2,16,128]{3,2,1,0:T(8,128)}, f32[14,2,16,128]{3,2,1,0:T(8,128)S(1)}, u32[]{:S(2)}, u32[]{:S(2)}) collective-permute-start(f32[14,2,16,128]{3,2,1,0:T(8,128)} %get-tuple-element.44), channel_id=1, source_target_pairs={{0,9},{1,8},{2,11},{3,10},{4,13},{5,12},{6,15},{7,14},{8,1},{9,0},... | collective-permute-start | bytes 688136 | tf_op jit(solution)/shard_map/ppermute | solution.py:471
  12.3 1.1 %copy-start = (f32[35,2,16,128]{3,2,1,0:T(8,128)S(1)}, f32[35,2,16,128]{3,2,1,0:T(8,128)}, u32[]{:S(2)}) copy-start(f32[35,2,16,128]{3,2,1,0:T(8,128)} %get-tuple-element.33) | copy-start | bytes 1720324
  13.3 0.8 %copy-start.2 = (f32[3,32,128]{2,1,0:T(8,128)S(1)}, f32[3,32,128]{2,1,0:T(8,128)}, u32[]{:S(2)}) copy-start(f32[3,32,128]{2,1,0:T(8,128)} %get-tuple-element.35.par) | copy-start | bytes 147460
  38.8 0.9 %copy-start.1 = (f32[6,2,16,128]{3,2,1,0:T(8,128)S(1)}, f32[6,2,16,128]{3,2,1,0:T(8,128)}, u32[]{:S(2)}) copy-start(f32[6,2,16,128]{3,2,1,0:T(8,128)} %get-tuple-element.30.refs_1_) | copy-start | bytes 294916
  39.7 20.4 %collective-permute-start.3 = (f32[6,2,16,128]{3,2,1,0:T(8,128)}, f32[6,2,16,128]{3,2,1,0:T(8,128)S(1)}, u32[]{:S(2)}, u32[]{:S(2)}) collective-permute-start(f32[6,2,16,128]{3,2,1,0:T(8,128)} %get-tuple-element.37), channel_id=1, source_target_pairs={{0,8},{1,9},{2,10},{3,11},{4,12},{5,13},{6,14},{7,15},{8,0},{9,1},... | collective-permute-start | bytes 294920 | tf_op jit(solution)/shard_map/ppermute | solution.py:471
  39.7 20.4 %collective-permute-start.4 = (f32[6,2,16,128]{3,2,1,0:T(8,128)S(1)}, f32[6,2,16,128]{3,2,1,0:T(8,128)S(1)}, u32[]{:S(2)}, u32[]{:S(2)}) collective-permute-start(f32[6,2,16,128]{3,2,1,0:T(8,128)S(1)} %get-tuple-element.38), channel_id=1, source_target_pairs={{0,9},{1,8},{2,11},{3,10},{4,13},{5,12},{6,15},{7,14},{8,1},{9,0},... | collective-permute-start | bytes 294920 | tf_op jit(solution)/shard_map/ppermute | solution.py:471

commit v2 on v1

v2 whole, which is shorter than its diff:
```python
import functools

import jax
import jax.numpy as jnp
from jax import lax
from jax.experimental import pallas as pl
from jax.experimental.pallas import tpu as pltpu
from jax.sharding import PartitionSpec as P

BLK = 128
QRT = 16
ROW = 2 * QRT
CHUNKS = (8, 10, 8, 6)
HINT = 0.5
WIDE = 3

REACH = 10
BASE = (24, 72)


class Sizes:
    def __init__(self, slots, total_rows):
        self.slots = slots
        self.total = total_rows
        self.right = slots + 1
        self.middle = slots + 2
        self.zero = slots + 3
        self.used = slots + 3


F32 = jnp.float32
ANY, HBM, VMEM, SMEM = pl.ANY, pltpu.HBM, pltpu.VMEM, pltpu.SMEM
DMA = pltpu.SemaphoreType.DMA


def shape(*dims):
    return jax.ShapeDtypeStruct(dims, F32)


def call(body, ins, outs, scratch, aliases=None, grant=32, us=0):
    return pl.pallas_call(
        body,
        out_shape=tuple(x for x, _ in outs),
        in_specs=[pl.BlockSpec(memory_space=m) for _, m in ins],
        out_specs=tuple(pl.BlockSpec(memory_space=m) for _, m in outs),
        scratch_shapes=scratch,
        input_output_aliases=aliases or {},
        compiler_params=pltpu.CompilerParams(vmem_limit_bytes=grant * 2**20),
        cost_estimate=pl.CostEstimate(flops=int(us * 10**9) + 1, bytes_accessed=int(us * 3 * 10**6) + 1, transcendentals=0),
    )(*(x for x, _ in ins))


def place(extent_ref):
    pos = lax.axis_index("sub")
    top = lax.axis_size("sub").bit_length() - 2
    core = pos & 1
    side = (pos >> top) & 1
    even = pos - core
    return core, side, extent_ref[even], extent_ref[even ^ (1 << top)]


def wait_whole(ref, sem):
    pltpu.make_async_copy(ref, ref, sem).wait()


def run_copies(copies, sems):
    handles = [pltpu.make_async_copy(src, dst, sems.at[i]) for i, (src, dst) in enumerate(copies)]
    for handle in handles:
        handle.start()
    for handle in handles:
        handle.wait()


def pack_body(sz, chunks, extent_ref, images_ref, shift_ref, taps_ref, phase_ref, *rest):
    sends = 2 + 2 * len(chunks)
    homes, own_par = rest[:sends], rest[sends]
    outs = rest[sends + 1 : 2 * sends + 1]
    mate, kept = outs[-2:]
    field_ref, moved_ref, turned_ref, shifts_ref, raw_ref, pieces_ref, angles_ref, sems, out_sems = rest[2 * sends + 1 :]
    core, side, own, other = place(extent_ref)
    slots = sz.slots
    windows = (core * slots, (1 - core) * slots)
    lanes = field_ref.shape[-1]
    small = [(shift_ref, raw_ref), (taps_ref, pieces_ref), (phase_ref, angles_ref)]
    loads = [pltpu.make_async_copy(*pair, sems.at[4 + i]) for i, pair in enumerate(small)]
    for t, which in enumerate((1 - side, side)):
        for part in range(2):
            rows = pl.ds(pl.multiple_of(part * ROW + which * QRT, QRT), QRT)
            source = images_ref.at[:, rows, pl.ds(0, lanes)]
            loads.append(pltpu.make_async_copy(source, field_ref.at[t, part], sems.at[2 * t + part]))
    for load in loads:
        load.start()
    for load in loads[:3]:
        load.wait()
    stores = [pltpu.make_async_copy(outs[i], homes[i], out_sems.at[i]) for i in range(sends)]

    half = BLK // 2
    for l in range(2):
        moved_ref[...] = jnp.zeros((BLK, BLK), F32)
        for s in range(2):
            at = BASE[s] + sz.used
            moved_ref[at : at + 4, 0:half] = pieces_ref[l, s]
            moved_ref[at + 4 : at + 6, 0:half] = angles_ref[l, s]
            shifts_ref[l, s] = jnp.zeros((half, BLK), F32)
            shifts_ref[l, s, :, 0:half] = raw_ref[l, s].astype(F32)
        turned_ref[l] = moved_ref[...].T[0:half]
    lane = lax.broadcasted_iota(jnp.int32, (ROW, BLK), 1)

    def parameters(l, row, first, extent):
        rows = pl.ds(pl.multiple_of(row, ROW), ROW)
        result = turned_ref[l, rows, :]
        for s in range(2):
            shifts = shifts_ref[l, s, rows, :]
            at = BASE[s]
            turn = lambda by: pltpu.roll(shifts, jnp.bitwise_and(by, BLK - 1), 1)
            inside = jnp.logical_and(lane >= at, lane < at + sz.middle)
            result = jnp.where(inside, turn(at + 1 - first + core * extent), result)
            result = jnp.where(lane == at + sz.middle, turn(at + sz.middle - extent), result)
        return result

    def read(t, part, block):
        return field_ref[t, part, :, :, pl.ds(pl.multiple_of(block * BLK, BLK), BLK)]

    def packed(t, extent, slot):
        part = (slot >= extent).astype(jnp.int32)
        return read(t, part, slot - part * extent)

    def halo(t, extent, first):
        part = (first >= extent).astype(jnp.int32)
        left = read(t, part, jnp.maximum(first - part * extent - 1, 0))
        last = first + slots - 1
        part = (last >= extent).astype(jnp.int32)
        return left, read(t, part, last - part * extent + 1), read(t, 0, extent)

    for i, level, row in ((0, 0, side * ROW), (1, 1, 0), (2, 1, ROW)):
        mate[sz.used + i] = parameters(level, row, windows[1], own).reshape(2, QRT, BLK)
        own_par[i] = parameters(level, row, windows[0], own)
    for load in loads[3:5]:
        load.wait()
    for i in range(2):
        left, right, middle = (x.reshape(ROW, BLK) for x in halo(0, other, windows[i]))
        result = parameters(0, (1 - side) * ROW, windows[i], other)
        result = jnp.where(lane < 2 * REACH, pltpu.roll(middle, REACH, 1), result)
        result = jnp.where(lane < REACH, right, result)
        result = jnp.where(lane >= BLK - 2, left, result)
        outs[i][chunks[0]] = result.reshape(2, QRT, BLK)
        slot = windows[i]
        for k, count in enumerate(chunks):
            for j in range(count):
                outs[2 * k + i][j] = packed(0, other, slot)
                slot = slot + 1
            stores[2 * k + i].start()
    for load in loads[5:]:
        load.wait()
    for n, first in ((sends - 2, windows[1]), (sends - 1, windows[0])):
        ref = outs[n]
        ref[0], ref[sz.right], ref[sz.middle] = halo(1, own, first)
        for j in range(slots):
            ref[1 + j] = packed(1, own, first + j)
        stores[n].start()
    for store in stores:
        store.wait()


def build_tables(sz, par_ref, tab_ref, ltab_ref, groups, extent, first):
    lane = lax.broadcasted_iota(jnp.int32, (QRT, BLK), 1)
    middle = lane == sz.middle
    even = jnp.logical_or(first + lane - 1 < extent, middle)
    block = jnp.where(even, first - 1 + lane, first - 1 + lane - extent)
    block = jnp.where(middle, extent, block).astype(F32)
    for group in range(groups):
        rows = [par_ref[p, pl.ds(group, QRT, stride=groups), :] for p in range(2)]
        for s in range(2):

            def spread(p, n):
                c = BASE[s] + sz.used + n
                return jnp.broadcast_to(rows[p][:, c : c + 1], (QRT, BLK))

            column = lambda n: jnp.where(even, spread(0, n), spread(1, n))
            tab_ref[s, group, 0] = jnp.where(
                even,
                pltpu.roll(rows[0], BLK - BASE[s], 1),
                pltpu.roll(rows[1], BLK - BASE[s], 1),
            )
            angle = column(4) + column(5) * (block * (BLK / sz.total))
            tab_ref[s, group, 1] = jnp.cos(angle)
            tab_ref[s, group, 2] = jnp.sin(angle)
            for p in range(2):
                angle = spread(p, 5) * (lane.astype(F32) / sz.total)
                ltab_ref[p, s, group, 0] = jnp.cos(angle)
                ltab_ref[p, s, group, 1] = jnp.sin(angle)
                for k in range(4):
                    ltab_ref[p, s, group, 2 + k] = spread(p, k)


def gathered(tab_ref, ltab_ref, s, group, x, part, rows):
    pick = jnp.full((8, BLK), x, jnp.int32)
    shift, cb, sb = (
        jnp.take_along_axis(tab_ref[s, group, k, rows, :], pick, axis=1) for k in range(3)
    )
    cl, sl, *taps = (ltab_ref[part, s, group, k, rows, :] for k in range(6))
    two = shift > 1.5
    one = jnp.where(two, shift - 2.0, shift) > 0.5
    zero = jnp.zeros((8, BLK), F32)
    taps = [zero] + taps + [zero]
    taps = [zero] * 2 + [jnp.where(one, taps[k], taps[k + 1]) for k in range(5)] + [zero] * 2
    weights = [jnp.where(two, taps[k], taps[k + 2]) for k in range(7)]
    return weights + [cb * cl - sb * sl, sb * cl + cb * sl]


def merge_block(sources, load, coef, sums, x, before, after, store):
    lane = lax.broadcasted_iota(jnp.int32, (8, BLK), 1)
    for s in sources:
        moved = []
        for ri in range(2):
            cur, prv, nxt = load(s, x, ri), load(s, before, ri), load(s, after, ri)
            views = [pltpu.roll(jnp.where(lane == BLK - 1, prv, cur), 1, 1), cur]
            for o in range(1, 6):
                views.append(pltpu.roll(jnp.where(lane < o, nxt, cur), BLK - o, 1))
            moved.append(views)
        for u in range(2):
            *weights, cosine, sine = coef(s, u)
            value = []
            for ri in range(2):
                total = weights[0] * moved[ri][0]
                for k in range(1, 7):
                    total = total + weights[k] * moved[ri][k]
                value.append(total)
            real = cosine * value[0] - sine * value[1]
            imag = sine * value[0] + cosine * value[1]
            sums[u] = [real, imag] if sums[u] is None else [sums[u][0] + real, sums[u][1] + imag]
    for u in range(2):
        for ri in range(2):
            store(u, ri, sums[u][ri])


def level_one(d_ref, f_ref, coef, x, before, after):
    for h in range(2):
        rows = lambda ri: pl.ds(QRT * ri + 8 * h, 8)

        def store(u, ri, value):
            f_ref[x, u, rows(ri), :] = value

        merge_block(
            (0, 1), lambda s, at, ri: d_ref[s, at, rows(ri), :],
            lambda s, u: coef(pl.ds(8 * h, 8), s, u), [None, None], x, before, after, store,
        )


def level_two(f_ref, coef, start, store, x, before, after):
    for u1 in range(2):
        for h in range(2):
            sums = [start(2 * u1 + u, h) for u in range(2)]
            merge_block(
                (0,), lambda s, at, ri: f_ref[at, u1, pl.ds(QRT * ri + 8 * h, 8), :],
                lambda s, u: coef(pl.ds(8 * h, 8), 2 * u1 + u), sums, x, before, after,
                lambda u, ri, value: store(2 * u1 + u, h, ri, value),
            )


def neighbours(sz, slot, first, extent):
    where = first + slot
    before = jnp.where(jnp.logical_or(where == 0, where == extent), sz.zero, slot)
    after = jnp.where(where == extent - 1, sz.middle, slot + 2)
    return before, after, (where >= extent).astype(jnp.int32)


def loop(begin, end, body):
    def step(slot, carry):
        body(slot)
        return carry

    lax.fori_loop(begin, end, step, 0)


def level_one_all(sz, d_ref, f_ref, coef_at, slots, left, right, low, high, first, extent):
    part_of = lambda slot: (first + slot >= extent).astype(jnp.int32)

    def body(slot):
        before, after, part = neighbours(sz, slot, first, extent)
        level_one(d_ref, f_ref, coef_at(slot + 1, part), slot + 1, before, after)

    if left:
        level_one(d_ref, f_ref, coef_at(0, part_of(0)), 0, 0, 1)
    loop(*slots, body)
    if right:
        part = part_of(sz.slots - 1)
        level_one(d_ref, f_ref, coef_at(sz.right, part), sz.right, sz.slots, sz.zero)
    before = jnp.clip(extent - first, low + 1, high)
    level_one(d_ref, f_ref, coef_at(sz.middle, 0), sz.middle, before, sz.zero)


def table_coef(tab, ltab):
    return lambda x, part: (lambda rows, s, u: gathered(tab, ltab, s, u, x, part, rows))


def local_body(sz, extent_ref, kept, mate, par, f_out, tab2_out, ltab2_out,
               d, f, par1s, par2s, tab, ltab, tab2, ltab2, sems, out_sems):
    core, side, extent, _ = place(extent_ref)
    first = core * sz.slots
    used = sz.used
    run_copies(
        [
            (kept, d.at[core, pl.ds(0, used)]),
            (mate.at[pl.ds(0, used)], d.at[1 - core, pl.ds(0, used)]),
            (par.at[0], par1s.at[core]),
            (par.at[1], par2s.at[core, pl.ds(0, ROW)]),
            (par.at[2], par2s.at[core, pl.ds(ROW, ROW)]),
            (mate.at[used], par1s.at[1 - core]),
            (mate.at[used + 1], par2s.at[1 - core, pl.ds(0, ROW)]),
            (mate.at[used + 2], par2s.at[1 - core, pl.ds(ROW, ROW)]),
        ],
        sems,
    )
    zeros = jnp.zeros((ROW, BLK), F32)
    for s in range(2):
        d[s, sz.zero] = zeros
        f[sz.zero, s] = zeros
    build_tables(sz, par1s, tab, ltab, 2, extent, first)
    build_tables(sz, par2s, tab2, ltab2, 4, extent, first)
    level_one_all(
        sz, d, f, table_coef(tab, ltab), (0, sz.slots), True, True, 0, sz.slots, first, extent
    )
    run_copies([(f, f_out), (tab2, tab2_out), (ltab2, ltab2_out)], out_sems)


def share_body(sz, extent_ref, f, tab2, ltab2, _, share_out, share, sem):
    core, side, extent, _ = place(extent_ref)
    first = core * sz.slots

    def body(slot):
        before, after, part = neighbours(sz, slot, first, extent)

        def store(u, h, ri, value):
            share[slot, ri, u, pl.ds(8 * h, 8), :] = value

        level_two(
            f, lambda rows, u: gathered(tab2, ltab2, side, u, slot + 1, part, rows),
            lambda u, h: None, store, slot + 1, before, after,
        )

    loop(0, sz.slots, body)
    run_copies([(share, share_out)], sem)


def one_range(sz, begin, count):
    end = begin + count
    return (0 if begin == 0 else begin - 1), (end if end == sz.slots else end - 1)


def two_range(sz, begin, count):
    end = begin + count
    return (0 if begin == 0 else begin - 2), (end if end == sz.slots else end - 2)


def other_tables_body(sz, spans, extent_ref, halo_same, halo_cross, tab2, ltab2, tab, ltab, *rest):
    wides, pars = rest[:-1], rest[-1]
    core, side, extent, _ = place(extent_ref)
    first = core * sz.slots
    pars[core] = halo_same[halo_same.shape[0] - 1]
    pars[1 - core] = halo_cross[halo_cross.shape[0] - 1]
    build_tables(sz, pars, tab, ltab, 2, extent, first)
    rows = lambda h: pl.ds(8 * h, 8)
    for n, span in enumerate(spans):
        wide1, wide2 = wides[2 * n : 2 * n + 2]
        one, two = one_range(sz, *span), two_range(sz, *span)

        def spread_one(j, x, part):
            for s in range(2):
                for u in range(2):
                    for h in range(2):
                        values = gathered(tab, ltab, s, u, x, part, rows(h))
                        for k, value in enumerate(values):
                            wide1[j, s, u, k, rows(h), :] = value

        def body_one(slot):
            _, _, part = neighbours(sz, slot, first, extent)
            spread_one(slot - one[0], slot + 1, part)

        def body_two(slot):
            _, _, part = neighbours(sz, slot, first, extent)
            for u in range(4):
                for h in range(2):
                    values = gathered(tab2, ltab2, 1 - side, u, slot + 1, part, rows(h))
                    for k, value in enumerate(values):
                        wide2[slot - two[0], u, k, rows(h), :] = value

        loop(*one, body_one)
        _, _, part = neighbours(sz, sz.slots - 1, first, extent)
        count = one[1] - one[0]
        spread_one(count, sz.middle, 0)
        if one[1] == sz.slots:
            spread_one(count + 1, sz.right, part)
        loop(*two, body_two)


def gate_body(*refs):
    pass


def main_body(sz, begin, count, wide, extent_ref, *rest):
    head, last = begin == 0, begin + count == sz.slots
    ins = list(rest)

    def take(n):
        part = ins[:n]
        del ins[:n]
        return part

    same, cross, halo_same, halo_cross, share = take(5)
    tables = take(2 if wide else 4)
    if not head:
        dtail_in, ftail_in, _ = take(3)
    (out,) = take(1)
    if not last:
        dtail_out, ftail_out = take(2)
    d, f, o, out_sem = ins
    core, side, extent, _ = place(extent_ref)
    first = core * sz.slots
    end = begin + count
    low = 0 if head else begin - 2
    zeros = jnp.zeros((ROW, BLK), F32)
    for mine, chunk, halo in ((core, same, halo_same), (1 - core, cross, halo_cross)):
        for i in range(count):
            d[mine, begin + 1 + i] = chunk[i]
        edge = halo[halo.shape[0] - 1]
        if head:
            d[mine, 0] = edge
        if last:
            d[mine, sz.right] = edge
        d[mine, sz.middle] = pltpu.roll(edge, BLK - REACH, 1)
    for s in range(2):
        d[s, sz.zero] = zeros
        f[sz.zero, s] = zeros
        if not head:
            for i in range(2):
                d[s, begin - 1 + i] = dtail_in[s, i]
                f[begin - 2 + i, s] = ftail_in[i, s]

    slots = one_range(sz, begin, count)
    if wide:
        wide1, wide2 = tables

        def coef_at(x, part):
            if isinstance(x, int):
                j = slots[1] - slots[0] + (1 if x == sz.right else 0)
            else:
                j = x - 1 - slots[0]
            return lambda rows, s, u: [wide1[j, s, u, k, rows, :] for k in range(9)]
    else:
        tab1, ltab1, tab2, ltab2 = tables
        coef_at = table_coef(tab1, ltab1)
    level_one_all(sz, d, f, coef_at, slots, head, last, low, end, first, extent)

    def body(slot):
        before, after, part = neighbours(sz, slot, first, extent)
        at = slot - low

        def store(u, h, ri, value):
            o[at, ri, pl.ds(32 * h + u, 8, stride=4), :] = value

        if wide:
            coef = lambda rows, u: [wide2[at, u, k, rows, :] for k in range(9)]
        else:
            coef = lambda rows, u: gathered(tab2, ltab2, 1 - side, u, slot + 1, part, rows)
        level_two(
            f, coef, lambda u, h: [share[slot, ri, u, pl.ds(8 * h, 8), :] for ri in range(2)],
            store, slot + 1, before, after,
        )
        lanes = pl.ds(pl.multiple_of(slot * BLK, BLK), BLK)
        pltpu.make_async_copy(o.at[at], out.at[:, :, lanes], out_sem).start()

    loop(*two_range(sz, begin, count), body)
    if not last:
        for s in range(2):
            for i in range(2):
                dtail_out[s, i] = d[s, end - 1 + i]
                ftail_out[i, s] = f[end - 2 + i, s]
    wait_whole(o, out_sem)


def per_device(images, band_shift, tap_weights, phases, extent_map):
    total_rows = images.shape[2]
    beams = images.shape[1]
    slots = total_rows // BLK // 2
    sz = Sizes(slots, total_rows)
    chunks = CHUNKS
    assert beams == 4 * QRT and sum(chunks) == slots and len(chunks) > 2
    assert sz.used + 6 <= BASE[1] - BASE[0] and BASE[1] + sz.used + 6 <= BLK - 2
    size = lax.axis_size("sub")
    top = 1 << (size.bit_length() - 2)
    swap = lambda x, by: lax.ppermute(x, "sub", [(i, i ^ by) for i in range(size)])
    flat = lambda x: x.reshape(x.shape[0], ROW, BLK)
    extents = (extent_map, SMEM)
    vm = lambda *dims: VMEM(dims, F32)

    counts = [chunks[0] + 1] * 2
    for count in chunks[1:]:
        counts += [count] * 2
    counts += [sz.used + 3, sz.used]
    half = BLK // 2
    packed = call(
        functools.partial(pack_body, sz, chunks),
        [
            extents,
            (images, HBM),
            (band_shift[0], HBM),
            (tap_weights[0].transpose(0, 1, 3, 2), HBM),
            (phases[0].transpose(0, 1, 3, 2), HBM),
        ],
        [(shape(n, 2, QRT, BLK), ANY) for n in counts] + [(shape(3, ROW, BLK), VMEM)],
        [vm(n, 2, QRT, BLK) for n in counts]
        + [vm(2, 2, 2, QRT, (3 * slots // 2 + 1) * BLK), vm(BLK, BLK), vm(2, half, BLK),
           vm(2, 2, half, BLK), VMEM((2, 2, half, half), jnp.int32), vm(2, 2, 4, half),
           vm(2, 2, 2, half), DMA((7,)), DMA((len(counts),))],
        grant=56,
    )
    send = lambda a, b: (flat(swap(a, top)), flat(swap(b, top ^ 1)))
    def gate(waiting, needed):
        passed = [(x, ANY) for x in waiting]
        out = call(gate_body, passed + [(x, ANY) for x in needed], passed, [], {0: 0, 1: 1})
        return send(*out)

    got = [send(*packed[0:2])]
    last = len(chunks)
    mate, kept, own_par = flat(swap(packed[2 * last], 1)), flat(packed[2 * last + 1]), packed[-1]
    got.append(gate(packed[2:4], [mate]))
    halo = [(x, VMEM) for x in got[0]]

    tabs1, ltabs1 = (2, 2, 3, QRT, BLK), (2, 2, 2, 6, QRT, BLK)
    tabs2, ltabs2 = (2, 4, 3, QRT, BLK), (2, 2, 4, 6, QRT, BLK)
    shares = (slots, 2, 4, QRT, BLK)
    d_s, f_s = (2, sz.zero + 1, ROW, BLK), (sz.zero + 1, 2, ROW, BLK)
    own_f, tab2, ltab2 = call(
        functools.partial(local_body, sz),
        [extents, (kept, HBM), (mate, HBM), (own_par, HBM)],
        [(shape(*f_s), ANY), (shape(*tabs2), ANY), (shape(*ltabs2), ANY)],
        [vm(*d_s), vm(*f_s), vm(2, ROW, BLK), vm(2, 2 * ROW, BLK), vm(*tabs1), vm(*ltabs1),
         vm(*tabs2), vm(*ltabs2), DMA((8,)), DMA((3,))],
        us=10,
    )

    begins = [sum(chunks[:k]) for k in range(len(chunks))]
    spans = [(begins[k], chunks[k]) for k in range(WIDE, len(chunks))]
    outs = [tabs1, ltabs1]
    for span in spans:
        one, two = one_range(sz, *span), two_range(sz, *span)
        extra = 2 if one[1] == slots else 1
        outs += [(one[1] - one[0] + extra, 2, 2, 9, QRT, BLK), (two[1] - two[0], 4, 9, QRT, BLK)]
    got.append(gate(packed[4:6], [*got[0], own_f]))
    tab1, ltab1, *wides = call(
        functools.partial(other_tables_body, sz, spans),
        [extents, *halo, (tab2, VMEM), (ltab2, VMEM)],
        [(shape(*s), VMEM) for s in outs], [vm(2, ROW, BLK)], us=HINT,
    )
    (share,) = call(
        functools.partial(share_body, sz),
        [extents, (own_f, VMEM), (tab2, VMEM), (ltab2, VMEM), (tab1, ANY)],
        [(shape(*shares), ANY)], [vm(*shares), DMA((1,))], us=HINT,
    )

    tail = [(shape(2, 2, ROW, BLK), VMEM)] * 2
    out = None
    for k, count in enumerate(chunks):
        begin = begins[k]
        head, last = k == 0, k == len(chunks) - 1
        if k >= 1 and k + 2 < len(chunks):
            got.append(gate(packed[2 * k + 4 : 2 * k + 6], [*got[k], dtail]))
        ins = [extents, *((x, VMEM) for x in got[k]), *halo, (share, VMEM)]
        if k >= WIDE:
            ins += [(x, VMEM) for x in wides[2 * (k - WIDE) : 2 * (k - WIDE) + 2]]
        else:
            ins += [(x, VMEM) for x in (tab1, ltab1, tab2, ltab2)]
        outs = [(shape(2, beams, slots * BLK), HBM)]
        aliases = {}
        if not head:
            aliases[len(ins) + 2] = 0
            ins += [(dtail, VMEM), (ftail, VMEM), (out, HBM)]
        if not last:
            outs += tail
        low, top_slot = two_range(sz, begin, count)
        res = call(
            functools.partial(main_body, sz, begin, count, k >= WIDE), ins, outs,
            [vm(*d_s), vm(*f_s), vm(top_slot - low, 2, beams, BLK), DMA], aliases, us=HINT if head else 0.1,
        )
        out = res[0]
        if not last:
            dtail, ftail = res[1:]
    return out


def solution(mesh):
    placed = (
        P(None, None, ("strip", "sub")),
        P(("strip", "sub"), None, None, None, None),
        P(("strip", "sub"), None, None, None, None),
        P(("strip", "sub"), None, None, None, None),
        P("strip"),
    )
    return jax.shard_map(
        per_device,
        mesh=mesh,
        in_specs=placed,
        out_specs=P(None, None, ("strip", "sub")),
        check_vma=False,
    )
```

time: 63.9 us -> 59.9 us (0.937)
  Pallas kernels: 42.1 us -> 36.1 us
  starting transfers between devices: 9.55 us -> 12.2 us
  local copies, waits for them, and re-layouts: 2.75 us -> 1.88 us
    pallas_call x7 -> x11, Pallas kernels: 42.1 us -> 36.1 us  [call(): pl.pallas_call(body, out_shape=tuple((x for x, _ in outs)), in_specs=[pl....]
    ppermute x7 -> x9, starting transfers between devices: 9.55 us -> 12.2 us  [per_device(): lax.ppermute(x, 'sub', [(i, i ^ by) for i in range(size)])]
    unnamed x8 -> x14, local copies, waits for them, and re-layouts: 2.75 us -> 1.88 us
    ppermute x7 -> x9, waiting for transfers between devices: 9.02 us -> 9.14 us  [per_device(): lax.ppermute(x, 'sub', [(i, i ^ by) for i in range(size)])]
  transfers between devices with their start and end apart: 7 -> 9, of which waited for: 3 -> 3; matrix products, arithmetic and copies ran while one was open for 0% -> 0% of each run, Pallas kernels for 52% -> 47%
where the time goes in v2:
time: 59.9 us; the launch traced here: 59.4 us
  Pallas kernels  36.1 us (60%)
  starting transfers between devices  12.2 us (20%)
  waiting for transfers between devices  9.14 us (15%)
  local copies, waits for them, and re-layouts  1.88 us (3%)
    pallas_call x11, Pallas kernels, call(): pl.pallas_call(body, out_shape=tuple((x for x, _ in outs)), in_specs=[pl....  36.1 us
    ppermute x9, starting transfers between devices, per_device(): lax.ppermute(x, 'sub', [(i, i ^ by) for i in range(size)])  12.2 us
    ppermute x9, waiting for transfers between devices, per_device(): lax.ppermute(x, 'sub', [(i, i ^ by) for i in range(size)])  9.14 us
    unnamed x14, local copies, waits for them, and re-layouts  1.88 us
  transfers between devices with their start and end apart: 9, of which 3 were waited for; matrix products, arithmetic and copies ran while one was open for 0% of the time, Pallas kernels for 47%

profile of v2, /device:TPU:1, one launch (start us, length us, event | category | flops | bytes accessed | tf_op | source)
XLA Modules:
  0.0 59.4 jit_solution(11997257994141665724)
XLA Ops:
  0.0 0.0 copy-start.4
  0.0 4.7 %shard_map.55 = (f32[9,2,16,128]{3,2,1,0:T(8,128)}, f32[9,2,16,128]{3,2,1,0:T(8,128)}, f32[10,2,16,128]{3,2,1,0:T(8,128)}, f32[10,2,16,128]{3,2,1,0:T(8,128)}, f...) custom-call(s32[16]{0:T(128)} %extent_ref.15, ...), custom_call_target="tpu_custom_call" | custom-call | flops 1 | bytes 1 | tf_op jit(solution)/shard_map/pallas_call | solution.py:41
  4.7 0.1 collective-permute-start
  4.8 3.8 %collective-permute-start.3 = (f32[9,2,16,128]{3,2,1,0:T(8,128)}, f32[9,2,16,128]{3,2,1,0:T(8,128)S(1)}, u32[]{:S(2)}, u32[]{:S(2)}) collective-permute-start(f32[9,2,16,128]{3,2,1,0:T(8,128)} %get-tuple-element.45), channel_id=1, source_target_pairs={{0,8},{1,9},{2,10},{3,11},{4,12},{5,13},{6,14},{7,15},{8,0},{9,1},... | collective-permute-start | bytes 442376 | tf_op jit(solution)/shard_map/ppermute | solution.py:492
  8.6 0.0 collective-permute-start.4
  8.6 0.0 collective-permute-done
  8.6 2.6 %collective-permute-start.1 = (f32[10,2,16,128]{3,2,1,0:T(8,128)}, f32[10,2,16,128]{3,2,1,0:T(8,128)S(1)}, u32[]{:S(2)}, u32[]{:S(2)}) collective-permute-start(f32[10,2,16,128]{3,2,1,0:T(8,128)} %get-tuple-element.43), channel_id=1, source_target_pairs={{0,8},{1,9},{2,10},{3,11},{4,12},{5,13},{6,14},{7,15},{8,0},{9,1},... | collective-permute-start | bytes 491528 | tf_op jit(solution)/shard_map/ppermute | solution.py:492
  11.2 0.3 collective-permute-start.2
  11.5 0.0 copy-done.4
  11.5 0.0 copy-start.5
  11.5 1.1 %copy-done.5 = f32[35,2,16,128]{3,2,1,0:T(8,128)S(1)} copy-done((f32[35,2,16,128]{3,2,1,0:T(8,128)S(1)}, f32[35,2,16,128]{3,2,1,0:T(8,128)}, u32[]{:S(2)}) %copy-start.5) | copy-done | bytes 573464
  12.6 0.0 copy-start.6
  12.6 0.8 %copy-done.6 = f32[3,32,128]{2,1,0:T(8,128)S(1)} copy-done((f32[3,32,128]{2,1,0:T(8,128)S(1)}, f32[3,32,128]{2,1,0:T(8,128)}, u32[]{:S(2)}) %copy-start.6) | copy-done | bytes 49176
  13.4 0.0 copy-start
  13.4 0.0 copy-start.1
  13.4 7.9 %shard_map.57 = (f32[36,2,32,128]{3,2,1,0:T(8,128)S(1)}, f32[2,4,3,16,128]{4,3,2,1,0:T(8,128)S(1)}, f32[2,2,4,6,16,128]{5,4,3,2,1,0:T(8,128)S(1)}) custom-call(s32[16]{0:T(128)S(1)} %copy-done.4, f32[35,32,128]{2,1,0:T(8,128)S(1)} %bitcast.41, f32[38,32,128]{2,1,0:T(8,128)S(1)} %bitcast.36, f32[3,32,128]{2,1,0:T(8,128)S(1)} %copy-done.6), custom_call_target="tpu_custom_call" | custom-call | flops 10000000000 | bytes 30000000 | tf_op jit(solution)/shard_map/pallas_call | solution.py:41
  21.3 5.0 %collective-permute-done.3 = f32[9,2,16,128]{3,2,1,0:T(8,128)S(1)} collective-permute-done((f32[9,2,16,128]{3,2,1,0:T(8,128)}, f32[9,2,16,128]{3,2,1,0:T(8,128)S(1)}, u32[]{:S(2)}, u32[]{:S(2)}) %collective-permute-start.3) | collective-permute-done | bytes 147488 | tf_op jit(solution)/shard_map/ppermute | solution.py:492
  26.2 3.4 %collective-permute-done.4 = f32[9,2,16,128]{3,2,1,0:T(8,128)S(1)} collective-permute-done((f32[9,2,16,128]{3,2,1,0:T(8,128)}, f32[9,2,16,128]{3,2,1,0:T(8,128)S(1)}, u32[]{:S(2)}, u32[]{:S(2)}) %collective-permute-start.4) | collective-permute-done | bytes 147488 | tf_op jit(solution)/shard_map/ppermute | solution.py:492
  29.6 0.0 copy-done
  29.6 0.0 copy-done.1
  29.6 0.0 collective-permute-start.7
  29.6 2.7 %collective-permute-start.8 = (f32[8,2,16,128]{3,2,1,0:T(8,128)S(1)}, f32[8,2,16,128]{3,2,1,0:T(8,128)S(1)}, u32[]{:S(2)}, u32[]{:S(2)}) collective-permute-start(f32[8,2,16,128]{3,2,1,0:T(8,128)S(1)} %get-tuple-element.62), channel_id=1, source_target_pairs={{0,9},{1,8},{2,11},{3,10},{4,13},{5,12},{6,15},{7,14},{8,1},{9,0},... | collective-permute-start | bytes 393224 | tf_op jit(solution)/shard_map/ppermute | solution.py:492
  32.3 2.6 %shard_map.58 = (f32[2,2,3,16,128]{4,3,2,1,0:T(8,128)S(1)}, f32[2,2,2,6,16,128]{5,4,3,2,1,0:T(8,128)S(1)}, f32[9,2,2,9,16,128]{5,4,3,2,1,0:T(8,128)S(1)}, f32[8,4,9,16,128]{4,3,2,1,0:T(8,128)S(1)}) custom-call(s32[16]{0:T(128)S(1)} %copy-done.4, f32[9,32,128]{2,1,0:T(8,128)S(1)} %bitcast.18, f32[9,32,128]{2,1,0:T(8,128)S(1)} %bitcast.25, ...), custom_call_target="tpu_custom_call" | custom-call | flops 500000000 | bytes 1500001 | tf_op jit(solution)/shard_map/pallas_call | solution.py:41
  35.0 5.6 %shard_map.59.rest_4_ = f32[32,2,4,16,128]{4,3,2,1,0:T(8,128)S(1)} custom-call(s32[16]{0:T(128)S(1)} %copy-done.4, f32[36,2,32,128]{3,2,1,0:T(8,128)S(1)} %get-tuple-element.49.f.refs_4_, f32[2,4,3,16,128]{4,3,2,1,0:T(8,128)S(1)} %get-tuple-element.50.tab2.rest_7_, f32[2,2,4,6,16,128]{5,4,3,2,1,0:T(8,128)S(1)} %get-tuple-element.51.ltab2.rest_8_, ...), custom_call_target="tpu_custom_call" | custom-call | flops 500000000 | bytes 1500001 | tf_op jit(solution)/shard_map/pallas_call | solution.py:41
  40.6 0.0 copy-start.2
  40.6 0.0 copy-start.3
  40.6 3.5 %shard_map.60 = (f32[2,64,4096]{2,1,0:T(8,128)}, f32[2,2,32,128]{3,2,1,0:T(8,128)S(1)}, f32[2,2,32,128]{3,2,1,0:T(8,128)S(1)}) custom-call(s32[16]{0:T(128)S(1)} %copy-done.4, f32[9,32,128]{2,1,0:T(8,128)S(1)} %bitcast.19, f32[9,32,128]{2,1,0:T(8,128)S(1)} %bitcast.26, f32[9,32,128]{2,1,0:T(8,128)S(1)} %bitcast.20, f32[9,32,128]{2,1,0:T(8,128)S(1)} %bitcast.27, ...), custom_call_target="tpu_custom_call" | custom-call | flops 500000000 | bytes 1500001 | tf_op jit(solution)/shard_map/pallas_call | solution.py:41
  44.2 0.0 collective-permute-done.1
  44.2 0.0 collective-permute-done.2
  44.2 0.0 copy-done.2
  44.2 0.0 copy-done.3
  44.2 0.1 collective-permute-start.5
  44.3 2.6 %collective-permute-start.6 = (f32[6,2,16,128]{3,2,1,0:T(8,128)S(1)}, f32[6,2,16,128]{3,2,1,0:T(8,128)S(1)}, u32[]{:S(2)}, u32[]{:S(2)}) collective-permute-start(f32[6,2,16,128]{3,2,1,0:T(8,128)S(1)} %get-tuple-element.56), channel_id=1, source_target_pairs={{0,9},{1,8},{2,11},{3,10},{4,13},{5,12},{6,15},{7,14},{8,1},{9,0},... | collective-permute-start | bytes 294920 | tf_op jit(solution)/shard_map/ppermute | solution.py:492
  46.9 4.5 %shard_map.63 = (f32[2,64,4096]{2,1,0:T(8,128)}, f32[2,2,32,128]{3,2,1,0:T(8,128)S(1)}, f32[2,2,32,128]{3,2,1,0:T(8,128)S(1)}) custom-call(s32[16]{0:T(128)S(1)} %copy-done.4, f32[10,32,128]{2,1,0:T(8,128)S(1)} %bitcast.32, f32[10,32,128]{2,1,0:T(8,128)S(1)} %bitcast.34, f32[9,32,128]{2,1,0:T(8,128)S(1)} %bitcast.21, ...), custom_call_target="tpu_custom_call", output_to_operand_aliasing={{0}: (12, {})} | custom-call | flops 100000000 | bytes 300001 | tf_op jit(solution)/shard_map/pallas_call | solution.py:41
  51.4 0.0 collective-permute-done.7
  51.4 0.0 collective-permute-done.8
  51.4 3.9 %shard_map.64 = (f32[2,64,4096]{2,1,0:T(8,128)}, f32[2,2,32,128]{3,2,1,0:T(8,128)S(1)}, f32[2,2,32,128]{3,2,1,0:T(8,128)S(1)}) custom-call(s32[16]{0:T(128)S(1)} %copy-done.4, f32[8,32,128]{2,1,0:T(8,128)S(1)} %bitcast.37, f32[8,32,128]{2,1,0:T(8,128)S(1)} %bitcast.38, f32[9,32,128]{2,1,0:T(8,128)S(1)} %bitcast.22, ...), custom_call_target="tpu_custom_call", output_to_operand_aliasing={{0}: (12, {})} | custom-call | flops 100000000 | bytes 300001 | tf_op jit(solution)/shard_map/pallas_call | solution.py:41
  55.3 0.0 collective-permute-done.5
  55.3 0.8 %collective-permute-done.6 = f32[6,2,16,128]{3,2,1,0:T(8,128)S(1)} collective-permute-done((f32[6,2,16,128]{3,2,1,0:T(8,128)S(1)}, f32[6,2,16,128]{3,2,1,0:T(8,128)S(1)}, u32[]{:S(2)}, u32[]{:S(2)}) %collective-permute-start.6) | collective-permute-done | bytes 98336 | tf_op jit(solution)/shard_map/ppermute | solution.py:492
  56.1 3.4 %shard_map.65 = f32[2,64,4096]{2,1,0:T(8,128)} custom-call(s32[16]{0:T(128)S(1)} %copy-done.4, f32[6,32,128]{2,1,0:T(8,128)S(1)} %bitcast.39, f32[6,32,128]{2,1,0:T(8,128)S(1)} %bitcast.40, f32[9,32,128]{2,1,0:T(8,128)S(1)} %bitcast.23, f32[9,32,128]{2,1,0:T(8,128)S(1)} %bitcast.30, ...), custom_call_target="tpu_custom_call", output_to_operand_aliasing={{}: (10, {})} | custom-call | flops 100000000 | bytes 300001 | tf_op jit(solution)/shard_map/pallas_call | solution.py:41
  (3 shorter events, 0.0 us)
Async XLA Ops:
  0.0 11.5 %copy-start.4 = (s32[16]{0:T(128)S(1)}, s32[16]{0:T(128)}, u32[]{:S(2)}) copy-start(s32[16]{0:T(128)} %extent_ref.15) | copy-start | bytes 196
  4.7 3.9 %collective-permute-start = (f32[38,2,16,128]{3,2,1,0:T(8,128)}, f32[38,2,16,128]{3,2,1,0:T(8,128)S(1)}, u32[]{:S(2)}, u32[]{:S(2)}) collective-permute-start(f32[38,2,16,128]{3,2,1,0:T(8,128)} %get-tuple-element.42), channel_id=1, source_target_pairs={{0,1},{1,0},{2,3},{3,2},{4,5},{5,4},{6,7},{7,6},{8,9},{9,8},{10,11... | collective-permute-start | bytes 1867784 | tf_op jit(solution)/shard_map/ppermute | solution.py:492
  4.8 21.5 %collective-permute-start.3 = (f32[9,2,16,128]{3,2,1,0:T(8,128)}, f32[9,2,16,128]{3,2,1,0:T(8,128)S(1)}, u32[]{:S(2)}, u32[]{:S(2)}) collective-permute-start(f32[9,2,16,128]{3,2,1,0:T(8,128)} %get-tuple-element.45), channel_id=1, source_target_pairs={{0,8},{1,9},{2,10},{3,11},{4,12},{5,13},{6,14},{7,15},{8,0},{9,1},... | collective-permute-start | bytes 442376 | tf_op jit(solution)/shard_map/ppermute | solution.py:492
  8.6 21.1 %collective-permute-start.4 = (f32[9,2,16,128]{3,2,1,0:T(8,128)}, f32[9,2,16,128]{3,2,1,0:T(8,128)S(1)}, u32[]{:S(2)}, u32[]{:S(2)}) collective-permute-start(f32[9,2,16,128]{3,2,1,0:T(8,128)} %get-tuple-element.46), channel_id=1, source_target_pairs={{0,9},{1,8},{2,11},{3,10},{4,13},{5,12},{6,15},{7,14},{8,1},{9,0},... | collective-permute-start | bytes 442376 | tf_op jit(solution)/shard_map/ppermute | solution.py:492
  8.6 35.5 %collective-permute-start.1 = (f32[10,2,16,128]{3,2,1,0:T(8,128)}, f32[10,2,16,128]{3,2,1,0:T(8,128)S(1)}, u32[]{:S(2)}, u32[]{:S(2)}) collective-permute-start(f32[10,2,16,128]{3,2,1,0:T(8,128)} %get-tuple-element.43), channel_id=1, source_target_pairs={{0,8},{1,9},{2,10},{3,11},{4,12},{5,13},{6,14},{7,15},{8,0},{9,1},... | collective-permute-start | bytes 491528 | tf_op jit(solution)/shard_map/ppermute | solution.py:492
  11.2 33.0 %collective-permute-start.2 = (f32[10,2,16,128]{3,2,1,0:T(8,128)}, f32[10,2,16,128]{3,2,1,0:T(8,128)S(1)}, u32[]{:S(2)}, u32[]{:S(2)}) collective-permute-start(f32[10,2,16,128]{3,2,1,0:T(8,128)} %get-tuple-element.44), channel_id=1, source_target_pairs={{0,9},{1,8},{2,11},{3,10},{4,13},{5,12},{6,15},{7,14},{8,1},{9,0},... | collective-permute-start | bytes 491528 | tf_op jit(solution)/shard_map/ppermute | solution.py:492
  11.5 1.1 %copy-start.5 = (f32[35,2,16,128]{3,2,1,0:T(8,128)S(1)}, f32[35,2,16,128]{3,2,1,0:T(8,128)}, u32[]{:S(2)}) copy-start(f32[35,2,16,128]{3,2,1,0:T(8,128)} %get-tuple-element.47) | copy-start | bytes 1720324
  12.6 0.8 %copy-start.6 = (f32[3,32,128]{2,1,0:T(8,128)S(1)}, f32[3,32,128]{2,1,0:T(8,128)}, u32[]{:S(2)}) copy-start(f32[3,32,128]{2,1,0:T(8,128)} %get-tuple-element.48.par) | copy-start | bytes 147460
  13.4 16.3 %copy-start = (f32[8,2,16,128]{3,2,1,0:T(8,128)S(1)}, f32[8,2,16,128]{3,2,1,0:T(8,128)}, u32[]{:S(2)}) copy-start(f32[8,2,16,128]{3,2,1,0:T(8,128)} %get-tuple-element.59.refs_0_) | copy-start | bytes 393220
  13.4 16.3 %copy-start.1 = (f32[8,2,16,128]{3,2,1,0:T(8,128)S(1)}, f32[8,2,16,128]{3,2,1,0:T(8,128)}, u32[]{:S(2)}) copy-start(f32[8,2,16,128]{3,2,1,0:T(8,128)} %get-tuple-element.60.refs_1_) | copy-start | bytes 393220
  29.6 21.7 %collective-permute-start.7 = (f32[8,2,16,128]{3,2,1,0:T(8,128)S(1)}, f32[8,2,16,128]{3,2,1,0:T(8,128)S(1)}, u32[]{:S(2)}, u32[]{:S(2)}) collective-permute-start(f32[8,2,16,128]{3,2,1,0:T(8,128)S(1)} %get-tuple-element.61), channel_id=1, source_target_pairs={{0,8},{1,9},{2,10},{3,11},{4,12},{5,13},{6,14},{7,15},{8,0},{9,1},... | collective-permute-start | bytes 393224 | tf_op jit(solution)/shard_map/ppermute | solution.py:492
  29.6 21.7 %collective-permute-start.8 = (f32[8,2,16,128]{3,2,1,0:T(8,128)S(1)}, f32[8,2,16,128]{3,2,1,0:T(8,128)S(1)}, u32[]{:S(2)}, u32[]{:S(2)}) collective-permute-start(f32[8,2,16,128]{3,2,1,0:T(8,128)S(1)} %get-tuple-element.62), channel_id=1, source_target_pairs={{0,9},{1,8},{2,11},{3,10},{4,13},{5,12},{6,15},{7,14},{8,1},{9,0},... | collective-permute-start | bytes 393224 | tf_op jit(solution)/shard_map/ppermute | solution.py:492
  40.6 3.6 %copy-start.2 = (f32[6,2,16,128]{3,2,1,0:T(8,128)S(1)}, f32[6,2,16,128]{3,2,1,0:T(8,128)}, u32[]{:S(2)}) copy-start(f32[6,2,16,128]{3,2,1,0:T(8,128)} %get-tuple-element.38.refs_0_) | copy-start | bytes 294916
  40.6 3.6 %copy-start.3 = (f32[6,2,16,128]{3,2,1,0:T(8,128)S(1)}, f32[6,2,16,128]{3,2,1,0:T(8,128)}, u32[]{:S(2)}) copy-start(f32[6,2,16,128]{3,2,1,0:T(8,128)} %get-tuple-element.39.refs_1_) | copy-start | bytes 294916
  44.2 11.1 %collective-permute-start.5 = (f32[6,2,16,128]{3,2,1,0:T(8,128)S(1)}, f32[6,2,16,128]{3,2,1,0:T(8,128)S(1)}, u32[]{:S(2)}, u32[]{:S(2)}) collective-permute-start(f32[6,2,16,128]{3,2,1,0:T(8,128)S(1)} %get-tuple-element.55), channel_id=1, source_target_pairs={{0,8},{1,9},{2,10},{3,11},{4,12},{5,13},{6,14},{7,15},{8,0},{9,1},... | collective-permute-start | bytes 294920 | tf_op jit(solution)/shard_map/ppermute | solution.py:492
  44.3 11.8 %collective-permute-start.6 = (f32[6,2,16,128]{3,2,1,0:T(8,128)S(1)}, f32[6,2,16,128]{3,2,1,0:T(8,128)S(1)}, u32[]{:S(2)}, u32[]{:S(2)}) collective-permute-start(f32[6,2,16,128]{3,2,1,0:T(8,128)S(1)} %get-tuple-element.56), channel_id=1, source_target_pairs={{0,9},{1,8},{2,11},{3,10},{4,13},{5,12},{6,15},{7,14},{8,1},{9,0},... | collective-permute-start | bytes 294920 | tf_op jit(solution)/shard_map/ppermute | solution.py:492

commit v3 on v2

--- a/solution.py
+++ b/solution.py
@@ -10,9 +10,12 @@
 BLK = 128
 QRT = 16
 ROW = 2 * QRT
-CHUNKS = (8, 10, 8, 6)
-HINT = 0.5
-WIDE = 3
+CHUNKS = (19, 8, 5)
+HINT = 0
+LOCAL = 0
+MATES = 3
+GATED = True
+WIDE = 2
 
 REACH = 10
 BASE = (24, 72)
@@ -71,31 +74,43 @@
         handle.wait()
 
 
-def pack_body(sz, chunks, extent_ref, images_ref, shift_ref, taps_ref, phase_ref, *rest):
-    sends = 2 + 2 * len(chunks)
-    homes, own_par = rest[:sends], rest[sends]
-    outs = rest[sends + 1 : 2 * sends + 1]
-    mate, kept = outs[-2:]
-    field_ref, moved_ref, turned_ref, shifts_ref, raw_ref, pieces_ref, angles_ref, sems, out_sems = rest[2 * sends + 1 :]
-    core, side, own, other = place(extent_ref)
-    slots = sz.slots
-    windows = (core * slots, (1 - core) * slots)
-    lanes = field_ref.shape[-1]
-    small = [(shift_ref, raw_ref), (taps_ref, pieces_ref), (phase_ref, angles_ref)]
-    loads = [pltpu.make_async_copy(*pair, sems.at[4 + i]) for i, pair in enumerate(small)]
-    for t, which in enumerate((1 - side, side)):
-        for part in range(2):
-            rows = pl.ds(pl.multiple_of(part * ROW + which * QRT, QRT), QRT)
-            source = images_ref.at[:, rows, pl.ds(0, lanes)]
-            loads.append(pltpu.make_async_copy(source, field_ref.at[t, part], sems.at[2 * t + part]))
+def load_rows(images_ref, field_ref, side, sems):
+    loads = []
+    for part in range(2):
+        rows = pl.ds(pl.multiple_of(part * ROW + side * QRT, QRT), QRT)
+        source = images_ref.at[:, rows, pl.ds(0, field_ref.shape[-1])]
+        loads.append(pltpu.make_async_copy(source, field_ref.at[part], sems.at[part]))
+        loads[-1].start()
+    return loads
+
+
+def read_block(field_ref, part, block):
+    return field_ref[part, :, :, pl.ds(pl.multiple_of(block * BLK, BLK), BLK)]
+
+
+def slot_block(extent, slot):
+    part = (slot >= extent).astype(jnp.int32)
+    return part, slot - part * extent
+
+
+def halo_blocks(sz, extent, first):
+    part, block = slot_block(extent, first)
+    left = (part, jnp.maximum(block - 1, 0))
+    part, block = slot_block(extent, first + sz.slots - 1)
+    return left, (part, block + 1), (0, extent)
+
+
+def load_parameters(shift_ref, taps_ref, phase_ref, raw_ref, pieces_ref, angles_ref, sems):
+    pairs = [(shift_ref, raw_ref), (taps_ref, pieces_ref), (phase_ref, angles_ref)]
+    loads = [pltpu.make_async_copy(*pair, sems.at[i]) for i, pair in enumerate(pairs)]
     for load in loads:
         load.start()
-    for load in loads[:3]:
-        load.wait()
-    stores = [pltpu.make_async_copy(outs[i], homes[i], out_sems.at[i]) for i in range(sends)]
-
+    return loads
+
+
+def turn_parameters(sz, levels, raw_ref, pieces_ref, angles_ref, moved_ref, turned_ref, shifts_ref):
     half = BLK // 2
-    for l in range(2):
+    for l in levels:
         moved_ref[...] = jnp.zeros((BLK, BLK), F32)
         for s in range(2):
             at = BASE[s] + sz.used
@@ -104,60 +119,118 @@
             shifts_ref[l, s] = jnp.zeros((half, BLK), F32)
             shifts_ref[l, s, :, 0:half] = raw_ref[l, s].astype(F32)
         turned_ref[l] = moved_ref[...].T[0:half]
+
+
+def window_parameters(sz, turned_ref, shifts_ref, l, row, first, extent, core):
     lane = lax.broadcasted_iota(jnp.int32, (ROW, BLK), 1)
-
-    def parameters(l, row, first, extent):
-        rows = pl.ds(pl.multiple_of(row, ROW), ROW)
-        result = turned_ref[l, rows, :]
-        for s in range(2):
-            shifts = shifts_ref[l, s, rows, :]
-            at = BASE[s]
-            turn = lambda by: pltpu.roll(shifts, jnp.bitwise_and(by, BLK - 1), 1)
-            inside = jnp.logical_and(lane >= at, lane < at + sz.middle)
-            result = jnp.where(inside, turn(at + 1 - first + core * extent), result)
-            result = jnp.where(lane == at + sz.middle, turn(at + sz.middle - extent), result)
-        return result
-
-    def read(t, part, block):
-        return field_ref[t, part, :, :, pl.ds(pl.multiple_of(block * BLK, BLK), BLK)]
-
-    def packed(t, extent, slot):
-        part = (slot >= extent).astype(jnp.int32)
-        return read(t, part, slot - part * extent)
-
-    def halo(t, extent, first):
-        part = (first >= extent).astype(jnp.int32)
-        left = read(t, part, jnp.maximum(first - part * extent - 1, 0))
-        last = first + slots - 1
-        part = (last >= extent).astype(jnp.int32)
-        return left, read(t, part, last - part * extent + 1), read(t, 0, extent)
-
-    for i, level, row in ((0, 0, side * ROW), (1, 1, 0), (2, 1, ROW)):
-        mate[sz.used + i] = parameters(level, row, windows[1], own).reshape(2, QRT, BLK)
-        own_par[i] = parameters(level, row, windows[0], own)
-    for load in loads[3:5]:
+    rows = pl.ds(pl.multiple_of(row, ROW), ROW)
+    result = turned_ref[l, rows, :]
+    for s in range(2):
+        shifts = shifts_ref[l, s, rows, :]
+        at = BASE[s]
+        turn = lambda by: pltpu.roll(shifts, jnp.bitwise_and(by, BLK - 1), 1)
+        inside = jnp.logical_and(lane >= at, lane < at + sz.middle)
+        result = jnp.where(inside, turn(at + 1 - first + core * extent), result)
+        result = jnp.where(lane == at + sz.middle, turn(at + sz.middle - extent), result)
+    return result
+
+
+def head_body(sz, extent_ref, images_ref, shift_ref, taps_ref, phase_ref, same_ref, cross_ref,
+              mate_par, own_par,
+              piece_ref, edge_ref, moved_ref, turned_ref, shifts_ref, raw_ref, pieces_ref, angles_ref,
+              sems, par_sems):
+    core, side, own, other = place(extent_ref)
+    windows = (core * sz.slots, (1 - core) * sz.slots)
+    small = load_parameters(shift_ref, taps_ref, phase_ref, raw_ref, pieces_ref, angles_ref, par_sems)
+    count = piece_ref.shape[1] - 1
+
+    def fetch(part, block, dst, sem):
+        rows = pl.ds(pl.multiple_of(part * ROW + (1 - side) * QRT, QRT), QRT)
+        lanes = pl.ds(pl.multiple_of(block * BLK, BLK), BLK)
+        pltpu.make_async_copy(images_ref.at[:, rows, lanes], dst, sem).start()
+
+    for i in range(2):
+        for n, (part, block) in enumerate(halo_blocks(sz, other, windows[i])):
+            fetch(part, block, edge_ref.at[i, n], sems.at[0])
+    for i in range(2):
+        for j in range(count):
+            fetch(*slot_block(other, windows[i] + j), piece_ref.at[i, j], sems.at[1])
+    for load in small:
         load.wait()
+    turn_parameters(sz, (0,), raw_ref, pieces_ref, angles_ref, moved_ref, turned_ref, shifts_ref)
+    lane = lax.broadcasted_iota(jnp.int32, (ROW, BLK), 1)
+    results = [
+        window_parameters(sz, turned_ref, shifts_ref, 0, (1 - side) * ROW, windows[i], other, core)
+        for i in range(2)
+    ]
+    wait_whole(edge_ref, sems.at[0])
     for i in range(2):
-        left, right, middle = (x.reshape(ROW, BLK) for x in halo(0, other, windows[i]))
-        result = parameters(0, (1 - side) * ROW, windows[i], other)
-        result = jnp.where(lane < 2 * REACH, pltpu.roll(middle, REACH, 1), result)
+        left, right, middle = (edge_ref[i, n].reshape(ROW, BLK) for n in range(3))
+        result = jnp.where(lane < 2 * REACH, pltpu.roll(middle, REACH, 1), results[i])
         result = jnp.where(lane < REACH, right, result)
         result = jnp.where(lane >= BLK - 2, left, result)
-        outs[i][chunks[0]] = result.reshape(2, QRT, BLK)
-        slot = windows[i]
-        for k, count in enumerate(chunks):
+        piece_ref[i, count] = result.reshape(2, QRT, BLK)
+    wait_whole(piece_ref.at[:, pl.ds(0, count)], sems.at[1])
+    stores = [(piece_ref.at[0], same_ref), (piece_ref.at[1], cross_ref)]
+    stores = [pltpu.make_async_copy(*pair, sems.at[i]) for i, pair in enumerate(stores)]
+    for store in stores:
+        store.start()
+    turn_parameters(sz, (1,), raw_ref, pieces_ref, angles_ref, moved_ref, turned_ref, shifts_ref)
+    for i, level, row in ((0, 0, side * ROW), (1, 1, 0), (2, 1, ROW)):
+        made = [
+            window_parameters(sz, turned_ref, shifts_ref, level, row, first, own, core)
+            for first in windows
+        ]
+        own_par[i] = made[0]
+        mate_par[i] = made[1].reshape(2, QRT, BLK)
+    for store in stores:
+        store.wait()
+
+
+def near_body(sz, chunks, pieces, extent_ref, images_ref, par_ref, *rest):
+    *rest, far_ref, field_ref, far_sems, sems, out_sems = rest
+    sends = 2 * len(chunks) - 2
+    homes, outs = rest[: len(rest) // 2], rest[len(rest) // 2 :]
+    mates, kept = outs[sends:-1], outs[-1]
+    core, side, own, other = place(extent_ref)
+    windows = (core * sz.slots, (1 - core) * sz.slots)
+    far_loads = load_rows(images_ref, far_ref, 1 - side, far_sems)
+    loads = load_rows(images_ref, field_ref, side, sems)
+    length = mates[0].shape[0]
+    last_load = pltpu.make_async_copy(par_ref, mates[-1].at[pl.ds(length - 3, 3)], sems.at[2])
+    last_load.start()
+    stores = [pltpu.make_async_copy(outs[i], homes[i], out_sems.at[i]) for i in range(len(outs))]
+    for load in far_loads:
+        load.wait()
+    begin = chunks[0]
+    for k, count in enumerate(chunks[1:]):
+        for i in range(2):
             for j in range(count):
-                outs[2 * k + i][j] = packed(0, other, slot)
-                slot = slot + 1
+                where = slot_block(other, windows[i] + begin + j)
+                outs[2 * k + i][j] = read_block(far_ref, *where)
             stores[2 * k + i].start()
-    for load in loads[5:]:
+        begin += count
+    for load in loads:
         load.wait()
-    for n, first in ((sends - 2, windows[1]), (sends - 1, windows[0])):
-        ref = outs[n]
-        ref[0], ref[sz.right], ref[sz.middle] = halo(1, own, first)
-        for j in range(slots):
-            ref[1 + j] = packed(1, own, first + j)
-        stores[n].start()
+
+    def put(first, where):
+        for x, at in zip((0, sz.right, sz.middle), halo_blocks(sz, own, first)):
+            where(x, read_block(field_ref, *at))
+        for j in range(sz.slots):
+            where(1 + j, read_block(field_ref, *slot_block(own, first + j)))
+
+    def mate_at(x, value):
+        mates[x // length][x % length] = value
+
+    def kept_at(x, value):
+        kept[x] = value
+
+    put(windows[1], mate_at)
+    last_load.wait()
+    for store in stores[sends:-1]:
+        store.start()
+    put(windows[0], kept_at)
+    stores[-1].start()
     for store in stores:
         store.wait()
 
@@ -270,7 +343,7 @@
         body(slot)
         return carry
 
-    lax.fori_loop(begin, end, step, 0)
+    lax.fori_loop(begin, end, step, 0, unroll=4)
 
 
 def level_one_all(sz, d_ref, f_ref, coef_at, slots, left, right, low, high, first, extent):
@@ -294,24 +367,29 @@
     return lambda x, part: (lambda rows, s, u: gathered(tab, ltab, s, u, x, part, rows))
 
 
-def local_body(sz, extent_ref, kept, mate, par, f_out, tab2_out, ltab2_out,
-               d, f, par1s, par2s, tab, ltab, tab2, ltab2, sems, out_sems):
+def local_body(sz, pieces, extent_ref, kept, par, *rest):
+    mates = rest[:pieces]
+    (share_out, tab2_out, ltab2_out, d, f, par1s, par2s, tab, ltab, tab2, ltab2, share,
+     sems, out_sems) = rest[pieces:]
     core, side, extent, _ = place(extent_ref)
     first = core * sz.slots
     used = sz.used
-    run_copies(
-        [
-            (kept, d.at[core, pl.ds(0, used)]),
-            (mate.at[pl.ds(0, used)], d.at[1 - core, pl.ds(0, used)]),
-            (par.at[0], par1s.at[core]),
-            (par.at[1], par2s.at[core, pl.ds(0, ROW)]),
-            (par.at[2], par2s.at[core, pl.ds(ROW, ROW)]),
-            (mate.at[used], par1s.at[1 - core]),
-            (mate.at[used + 1], par2s.at[1 - core, pl.ds(0, ROW)]),
-            (mate.at[used + 2], par2s.at[1 - core, pl.ds(ROW, ROW)]),
-        ],
-        sems,
-    )
+    copies = [
+        (kept, d.at[core, pl.ds(0, used)]),
+        (par.at[0], par1s.at[core]),
+        (par.at[1], par2s.at[core, pl.ds(0, ROW)]),
+        (par.at[2], par2s.at[core, pl.ds(ROW, ROW)]),
+    ]
+    length = mates[0].shape[0]
+    for i, mate in enumerate(mates):
+        count = min(length, used - i * length)
+        copies.append((mate.at[pl.ds(0, count)], d.at[1 - core, pl.ds(i * length, count)]))
+    copies += [
+        (mates[-1].at[length - 3], par1s.at[1 - core]),
+        (mates[-1].at[length - 2], par2s.at[1 - core, pl.ds(0, ROW)]),
+        (mates[-1].at[length - 1], par2s.at[1 - core, pl.ds(ROW, ROW)]),
+    ]
+    run_copies(copies, sems)
     zeros = jnp.zeros((ROW, BLK), F32)
     for s in range(2):
         d[s, sz.zero] = zeros
@@ -321,13 +399,6 @@
     level_one_all(
         sz, d, f, table_coef(tab, ltab), (0, sz.slots), True, True, 0, sz.slots, first, extent
     )
-    run_copies([(f, f_out), (tab2, tab2_out), (ltab2, ltab2_out)], out_sems)
-
-
-def share_body(sz, extent_ref, f, tab2, ltab2, _, share_out, share, sem):
-    core, side, extent, _ = place(extent_ref)
-    first = core * sz.slots
-
     def body(slot):
         before, after, part = neighbours(sz, slot, first, extent)
 
@@ -340,7 +411,7 @@
         )
 
     loop(0, sz.slots, body)
-    run_copies([(share, share_out)], sem)
+    run_copies([(share, share_out), (tab2, tab2_out), (ltab2, ltab2_out)], out_sems)
 
 
 def one_range(sz, begin, count):
@@ -494,13 +565,12 @@
     extents = (extent_map, SMEM)
     vm = lambda *dims: VMEM(dims, F32)
 
-    counts = [chunks[0] + 1] * 2
-    for count in chunks[1:]:
-        counts += [count] * 2
-    counts += [sz.used + 3, sz.used]
     half = BLK // 2
-    packed = call(
-        functools.partial(pack_body, sz, chunks),
+    blocks = lambda n: (shape(n, 2, QRT, BLK), ANY)
+    lanes = (3 * slots // 2 + 1) * BLK
+    count = chunks[0] + 1
+    *first, mate_par, own_par = call(
+        functools.partial(head_body, sz),
         [
             extents,
             (images, HBM),
@@ -508,13 +578,23 @@
             (tap_weights[0].transpose(0, 1, 3, 2), HBM),
             (phases[0].transpose(0, 1, 3, 2), HBM),
         ],
-        [(shape(n, 2, QRT, BLK), ANY) for n in counts] + [(shape(3, ROW, BLK), VMEM)],
-        [vm(n, 2, QRT, BLK) for n in counts]
-        + [vm(2, 2, 2, QRT, (3 * slots // 2 + 1) * BLK), vm(BLK, BLK), vm(2, half, BLK),
-           vm(2, 2, half, BLK), VMEM((2, 2, half, half), jnp.int32), vm(2, 2, 4, half),
-           vm(2, 2, 2, half), DMA((7,)), DMA((len(counts),))],
+        [blocks(count)] * 2 + [(shape(3, 2, QRT, BLK), VMEM), (shape(3, ROW, BLK), VMEM)],
+        [vm(2, count, 2, QRT, BLK), vm(2, 3, 2, QRT, BLK), vm(BLK, BLK), vm(2, half, BLK),
+         vm(2, 2, half, BLK), VMEM((2, 2, half, half), jnp.int32), vm(2, 2, 4, half),
+         vm(2, 2, 2, half), DMA((2,)), DMA((3,))],
         grant=56,
     )
+    length = -(-(sz.used + 3) // MATES)
+    counts = [n for n in chunks[1:] for _ in range(2)] + [length] * MATES + [sz.used]
+    *packed, kept = call(
+        functools.partial(near_body, sz, chunks, MATES),
+        [extents, (images, HBM), (mate_par, ANY)], [blocks(n) for n in counts],
+        [vm(n, 2, QRT, BLK) for n in counts] + [vm(2, 2, QRT, lanes)] * 2
+        + [DMA((2,)), DMA((3,)), DMA((len(counts),))],
+        grant=56,
+    )
+    packed, mates = list(first) + packed[:-MATES], packed[-MATES:]
+    mates, kept = [flat(swap(x, 1)) for x in mates], flat(kept)
     send = lambda a, b: (flat(swap(a, top)), flat(swap(b, top ^ 1)))
     def gate(waiting, needed):
         passed = [(x, ANY) for x in waiting]
@@ -522,22 +602,20 @@
         return send(*out)
 
     got = [send(*packed[0:2])]
-    last = len(chunks)
-    mate, kept, own_par = flat(swap(packed[2 * last], 1)), flat(packed[2 * last + 1]), packed[-1]
-    got.append(gate(packed[2:4], [mate]))
+    got.append(gate(packed[2:4], mates) if GATED else send(*packed[2:4]))
     halo = [(x, VMEM) for x in got[0]]
 
     tabs1, ltabs1 = (2, 2, 3, QRT, BLK), (2, 2, 2, 6, QRT, BLK)
     tabs2, ltabs2 = (2, 4, 3, QRT, BLK), (2, 2, 4, 6, QRT, BLK)
     shares = (slots, 2, 4, QRT, BLK)
     d_s, f_s = (2, sz.zero + 1, ROW, BLK), (sz.zero + 1, 2, ROW, BLK)
-    own_f, tab2, ltab2 = call(
-        functools.partial(local_body, sz),
-        [extents, (kept, HBM), (mate, HBM), (own_par, HBM)],
-        [(shape(*f_s), ANY), (shape(*tabs2), ANY), (shape(*ltabs2), ANY)],
+    share, tab2, ltab2 = call(
+        functools.partial(local_body, sz, MATES),
+        [extents, (kept, HBM), (own_par, HBM)] + [(x, HBM) for x in mates],
+        [(shape(*shares), ANY), (shape(*tabs2), ANY), (shape(*ltabs2), ANY)],
         [vm(*d_s), vm(*f_s), vm(2, ROW, BLK), vm(2, 2 * ROW, BLK), vm(*tabs1), vm(*ltabs1),
-         vm(*tabs2), vm(*ltabs2), DMA((8,)), DMA((3,))],
-        us=10,
+         vm(*tabs2), vm(*ltabs2), vm(*shares), DMA((7 + MATES,)), DMA((3,))],
+        us=LOCAL,
     )
 
     begins = [sum(chunks[:k]) for k in range(len(chunks))]
@@ -547,18 +625,12 @@
         one, two = one_range(sz, *span), two_range(sz, *span)
         extra = 2 if one[1] == slots else 1
         outs += [(one[1] - one[0] + extra, 2, 2, 9, QRT, BLK), (two[1] - two[0], 4, 9, QRT, BLK)]
-    got.append(gate(packed[4:6], [*got[0], own_f]))
+    got.append(gate(packed[4:6], [*got[0], share]))
     tab1, ltab1, *wides = call(
         functools.partial(other_tables_body, sz, spans),
         [extents, *halo, (tab2, VMEM), (ltab2, VMEM)],
         [(shape(*s), VMEM) for s in outs], [vm(2, ROW, BLK)], us=HINT,
     )
-    (share,) = call(
-        functools.partial(share_body, sz),
-        [extents, (own_f, VMEM), (tab2, VMEM), (ltab2, VMEM), (tab1, ANY)],
-        [(shape(*shares), ANY)], [vm(*shares), DMA((1,))], us=HINT,
-    )
-
     tail = [(shape(2, 2, ROW, BLK), VMEM)] * 2
     out = None
     for k, count in enumerate(chunks):

time: 59.9 us -> 58.2 us (0.972)
  waiting for transfers between devices: 9.14 us -> 16.8 us
  Pallas kernels: 36.1 us -> 30.1 us
  starting transfers between devices: 12.2 us -> 9.12 us
  local copies, waits for them, and re-layouts: 1.88 us -> 1.08 us
    ppermute x9, waiting for transfers between devices: 9.14 us -> 16.8 us  [per_device(): lax.ppermute(x, 'sub', [(i, i ^ by) for i in range(size)])]
    pallas_call x11 -> x9, Pallas kernels: 36.1 us -> 30.1 us  [call(): pl.pallas_call(body, out_shape=tuple((x for x, _ in outs)), in_specs=[pl....]
    ppermute x9, starting transfers between devices: 12.2 us -> 9.12 us  [per_device(): lax.ppermute(x, 'sub', [(i, i ^ by) for i in range(size)])]
    unnamed x14 -> x10, local copies, waits for them, and re-layouts: 1.88 us -> 1.08 us
  transfers between devices with their start and end apart: 9 -> 9, of which waited for: 3 -> 6; matrix products, arithmetic and copies ran while one was open for 0% -> 0% of each run, Pallas kernels for 47% -> 42%
where the time goes in v3:
time: 58.2 us; the launch traced here: 57.2 us
  Pallas kernels  30.1 us (52%)
  waiting for transfers between devices  16.8 us (29%)
  starting transfers between devices  9.12 us (16%)
  local copies, waits for them, and re-layouts  1.08 us (2%)
    pallas_call x9, Pallas kernels, call(): pl.pallas_call(body, out_shape=tuple((x for x, _ in outs)), in_specs=[pl....  30.1 us
    ppermute x9, waiting for transfers between devices, per_device(): lax.ppermute(x, 'sub', [(i, i ^ by) for i in range(size)])  16.8 us
    ppermute x9, starting transfers between devices, per_device(): lax.ppermute(x, 'sub', [(i, i ^ by) for i in range(size)])  9.12 us
  transfers between devices with their start and end apart: 9, of which 6 were waited for; matrix products, arithmetic and copies ran while one was open for 0% of the time, Pallas kernels for 42%

profile of v3, /device:TPU:1, one launch (start us, length us, event | category | flops | bytes accessed | tf_op | source)
XLA Modules:
  0.0 57.2 jit_solution(11999496247390765841)
XLA Ops:
  0.0 3.5 %shard_map.55 = (f32[20,2,16,128]{3,2,1,0:T(8,128)}, f32[20,2,16,128]{3,2,1,0:T(8,128)}, f32[3,2,16,128]{3,2,1,0:T(8,128)}, f32[3,32,128]{2,1,0:T(8,128)}) custom-call(s32[16]{0:T(128)} %extent_ref.13, f32[2,64,8192]{2,1,0:T(8,128)} %images_ref.3, s32[2,2,64,64]{3,2,1,0:T(8,128)} %bitcast.40, f32[2,2,4,64]{3,2,1,0:T(4,128)} %bitcast.41, f32[2,2,2,64]{3,2,1,0:T(2,128)} %bitcast.42), custom_call_target="tpu_custom_call" | custom-call | flops 1 | bytes 1 | tf_op jit(solution)/shard_map/pallas_call | solution.py:44
  3.5 3.2 %collective-permute-start = (f32[20,2,16,128]{3,2,1,0:T(8,128)}, f32[20,2,16,128]{3,2,1,0:T(8,128)S(1)}, u32[]{:S(2)}, u32[]{:S(2)}) collective-permute-start(f32[20,2,16,128]{3,2,1,0:T(8,128)} %get-tuple-element.37), channel_id=1, source_target_pairs={{0,8},{1,9},{2,10},{3,11},{4,12},{5,13},{6,14},{7,15},{8,0},{9,1},... | collective-permute-start | bytes 983048 | tf_op jit(solution)/shard_map/ppermute | solution.py:563
  6.7 0.6 %collective-permute-start.1 = (f32[20,2,16,128]{3,2,1,0:T(8,128)}, f32[20,2,16,128]{3,2,1,0:T(8,128)S(1)}, u32[]{:S(2)}, u32[]{:S(2)}) collective-permute-start(f32[20,2,16,128]{3,2,1,0:T(8,128)} %get-tuple-element.38), channel_id=1, source_target_pairs={{0,9},{1,8},{2,11},{3,10},{4,13},{5,12},{6,15},{7,14},{8,1},{9,0},... | collective-permute-start | bytes 983048 | tf_op jit(solution)/shard_map/ppermute | solution.py:563
  7.3 0.0 copy-start.3
  7.3 0.0 copy-start.4
  7.3 3.9 %shard_map.56 = (f32[8,2,16,128]{3,2,1,0:T(8,128)}, f32[8,2,16,128]{3,2,1,0:T(8,128)}, f32[5,2,16,128]{3,2,1,0:T(8,128)}, f32[5,2,16,128]{3,2,1,0:T(8,128)}, f32...) custom-call(s32[16]{0:T(128)} %extent_ref.13, ...), custom_call_target="tpu_custom_call" | custom-call | flops 1 | bytes 1 | tf_op jit(solution)/shard_map/pallas_call | solution.py:44
  11.2 0.0 copy-start.1
  11.2 0.0 copy-start.2
  11.2 0.4 collective-permute-start.2
  11.6 0.2 collective-permute-start.3
  11.8 0.3 collective-permute-start.4
  12.1 0.8 %collective-permute-done.2 = f32[13,2,16,128]{3,2,1,0:T(8,128)S(1)} collective-permute-done((f32[13,2,16,128]{3,2,1,0:T(8,128)}, f32[13,2,16,128]{3,2,1,0:T(8,128)S(1)}, u32[]{:S(2)}, u32[]{:S(2)}) %collective-permute-start.2) | collective-permute-done | bytes 213024 | tf_op jit(solution)/shard_map/ppermute | solution.py:563
  13.0 0.3 collective-permute-done.3
  13.3 0.3 collective-permute-done.4
  13.6 2.6 %collective-permute-start.7 = (f32[8,2,16,128]{3,2,1,0:T(8,128)}, f32[8,2,16,128]{3,2,1,0:T(8,128)S(1)}, u32[]{:S(2)}, u32[]{:S(2)}) collective-permute-start(f32[8,2,16,128]{3,2,1,0:T(8,128)} %get-tuple-element.53), channel_id=1, source_target_pairs={{0,8},{1,9},{2,10},{3,11},{4,12},{5,13},{6,14},{7,15},{8,0},{9,1},... | collective-permute-start | bytes 393224 | tf_op jit(solution)/shard_map/ppermute | solution.py:563
  16.2 0.3 collective-permute-start.8
  16.4 0.0 copy-done.3
  16.5 0.0 copy-done.4
  16.5 0.0 copy-start
  16.5 1.1 %copy-done = f32[35,2,16,128]{3,2,1,0:T(8,128)S(1)} copy-done((f32[35,2,16,128]{3,2,1,0:T(8,128)S(1)}, f32[35,2,16,128]{3,2,1,0:T(8,128)}, u32[]{:S(2)}) %copy-start) | copy-done | bytes 573464
  17.5 9.9 %shard_map.57 = (f32[32,2,4,16,128]{4,3,2,1,0:T(8,128)S(1)}, f32[2,4,3,16,128]{4,3,2,1,0:T(8,128)S(1)}, f32[2,2,4,6,16,128]{5,4,3,2,1,0:T(8,128)S(1)}) custom-call(s32[16]{0:T(128)S(1)} %copy-done.4, f32[35,32,128]{2,1,0:T(8,128)S(1)} %bitcast.35, f32[3,32,128]{2,1,0:T(8,128)S(1)} %copy-done.3, f32[13,32,128]{2,1,0:T(8,128)S(1)} %bitcast.30, ...), custom_call_target="tpu_custom_call" | custom-call | flops 1 | bytes 1 | tf_op jit(solution)/shard_map/pallas_call | solution.py:44
  27.5 6.5 %collective-permute-done = f32[20,2,16,128]{3,2,1,0:T(8,128)S(1)} collective-permute-done((f32[20,2,16,128]{3,2,1,0:T(8,128)}, f32[20,2,16,128]{3,2,1,0:T(8,128)S(1)}, u32[]{:S(2)}, u32[]{:S(2)}) %collective-permute-start) | collective-permute-done | bytes 327712 | tf_op jit(solution)/shard_map/ppermute | solution.py:563
  34.0 8.4 %collective-permute-done.1 = f32[20,2,16,128]{3,2,1,0:T(8,128)S(1)} collective-permute-done((f32[20,2,16,128]{3,2,1,0:T(8,128)}, f32[20,2,16,128]{3,2,1,0:T(8,128)S(1)}, u32[]{:S(2)}, u32[]{:S(2)}) %collective-permute-start.1) | collective-permute-done | bytes 327712 | tf_op jit(solution)/shard_map/ppermute | solution.py:563
  42.4 0.0 copy-done.1
  42.4 0.0 copy-done.2
  42.4 0.0 collective-permute-start.5
  42.4 1.5 %collective-permute-start.6 = (f32[5,2,16,128]{3,2,1,0:T(8,128)S(1)}, f32[5,2,16,128]{3,2,1,0:T(8,128)S(1)}, u32[]{:S(2)}, u32[]{:S(2)}) collective-permute-start(f32[5,2,16,128]{3,2,1,0:T(8,128)S(1)} %get-tuple-element.46), channel_id=1, source_target_pairs={{0,9},{1,8},{2,11},{3,10},{4,13},{5,12},{6,15},{7,14},{8,1},{9,0},... | collective-permute-start | bytes 245768 | tf_op jit(solution)/shard_map/ppermute | solution.py:563
  43.9 1.9 %shard_map.59 = (f32[2,2,3,16,128]{4,3,2,1,0:T(8,128)S(1)}, f32[2,2,2,6,16,128]{5,4,3,2,1,0:T(8,128)S(1)}, f32[8,2,2,9,16,128]{5,4,3,2,1,0:T(8,128)S(1)}, f32[7,4,9,16,128]{4,3,2,1,0:T(8,128)S(1)}) custom-call(s32[16]{0:T(128)S(1)} %copy-done.4, f32[20,32,128]{2,1,0:T(8,128)S(1)} %bitcast.18, f32[20,32,128]{2,1,0:T(8,128)S(1)} %bitcast.24, ...), custom_call_target="tpu_custom_call" | custom-call | flops 1 | bytes 1 | tf_op jit(solution)/shard_map/pallas_call | solution.py:44
  45.8 5.3 %shard_map.61 = (f32[2,64,4096]{2,1,0:T(8,128)}, f32[2,2,32,128]{3,2,1,0:T(8,128)S(1)}, f32[2,2,32,128]{3,2,1,0:T(8,128)S(1)}) custom-call(s32[16]{0:T(128)S(1)} %copy-done.4, f32[20,32,128]{2,1,0:T(8,128)S(1)} %bitcast.19, f32[20,32,128]{2,1,0:T(8,128)S(1)} %bitcast.25, f32[20,32,128]{2,1,0:T(8,128)S(1)} %bitcast.20, f32[20,32,128]{2,1,0:T(8,128)S(1)} %bitcast.26, ...), custom_call_target="tpu_custom_call" | custom-call | flops 1 | bytes 1 | tf_op jit(solution)/shard_map/pallas_call | solution.py:44
  51.1 0.0 collective-permute-done.7
  51.1 0.4 collective-permute-done.8
  51.5 3.0 %shard_map.62 = (f32[2,64,4096]{2,1,0:T(8,128)}, f32[2,2,32,128]{3,2,1,0:T(8,128)S(1)}, f32[2,2,32,128]{3,2,1,0:T(8,128)S(1)}) custom-call(s32[16]{0:T(128)S(1)} %copy-done.4, f32[8,32,128]{2,1,0:T(8,128)S(1)} %bitcast.36, f32[8,32,128]{2,1,0:T(8,128)S(1)} %bitcast.37, f32[20,32,128]{2,1,0:T(8,128)S(1)} %bitcast.21, ...), custom_call_target="tpu_custom_call", output_to_operand_aliasing={{0}: (12, {})} | custom-call | flops 100000000 | bytes 300001 | tf_op jit(solution)/shard_map/pallas_call | solution.py:44
  54.5 0.0 collective-permute-done.5
  54.5 0.0 collective-permute-done.6
  54.5 2.6 %shard_map.63 = f32[2,64,4096]{2,1,0:T(8,128)} custom-call(s32[16]{0:T(128)S(1)} %copy-done.4, f32[5,32,128]{2,1,0:T(8,128)S(1)} %bitcast.38, f32[5,32,128]{2,1,0:T(8,128)S(1)} %bitcast.39, f32[20,32,128]{2,1,0:T(8,128)S(1)} %bitcast.22, f32[20,32,128]{2,1,0:T(8,128)S(1)} %bitcast.28, ...), custom_call_target="tpu_custom_call", output_to_operand_aliasing={{}: (10, {})} | custom-call | flops 100000000 | bytes 300001 | tf_op jit(solution)/shard_map/pallas_call | solution.py:44
  (2 shorter events, 0.0 us)
Async XLA Ops:
  3.5 30.5 %collective-permute-start = (f32[20,2,16,128]{3,2,1,0:T(8,128)}, f32[20,2,16,128]{3,2,1,0:T(8,128)S(1)}, u32[]{:S(2)}, u32[]{:S(2)}) collective-permute-start(f32[20,2,16,128]{3,2,1,0:T(8,128)} %get-tuple-element.37), channel_id=1, source_target_pairs={{0,8},{1,9},{2,10},{3,11},{4,12},{5,13},{6,14},{7,15},{8,0},{9,1},... | collective-permute-start | bytes 983048 | tf_op jit(solution)/shard_map/ppermute | solution.py:563
  6.7 35.7 %collective-permute-start.1 = (f32[20,2,16,128]{3,2,1,0:T(8,128)}, f32[20,2,16,128]{3,2,1,0:T(8,128)S(1)}, u32[]{:S(2)}, u32[]{:S(2)}) collective-permute-start(f32[20,2,16,128]{3,2,1,0:T(8,128)} %get-tuple-element.38), channel_id=1, source_target_pairs={{0,9},{1,8},{2,11},{3,10},{4,13},{5,12},{6,15},{7,14},{8,1},{9,0},... | collective-permute-start | bytes 983048 | tf_op jit(solution)/shard_map/ppermute | solution.py:563
  7.3 9.1 %copy-start.3 = (f32[3,32,128]{2,1,0:T(8,128)S(1)}, f32[3,32,128]{2,1,0:T(8,128)}, u32[]{:S(2)}) copy-start(f32[3,32,128]{2,1,0:T(8,128)} %get-tuple-element.40.par) | copy-start | bytes 147460
  7.3 9.1 %copy-start.4 = (s32[16]{0:T(128)S(1)}, s32[16]{0:T(128)}, u32[]{:S(2)}) copy-start(s32[16]{0:T(128)} %extent_ref.13) | copy-start | bytes 196
  11.2 31.1 %copy-start.1 = (f32[5,2,16,128]{3,2,1,0:T(8,128)S(1)}, f32[5,2,16,128]{3,2,1,0:T(8,128)}, u32[]{:S(2)}) copy-start(f32[5,2,16,128]{3,2,1,0:T(8,128)} %get-tuple-element.35.refs_0_) | copy-start | bytes 245764
  11.2 31.1 %copy-start.2 = (f32[5,2,16,128]{3,2,1,0:T(8,128)S(1)}, f32[5,2,16,128]{3,2,1,0:T(8,128)}, u32[]{:S(2)}) copy-start(f32[5,2,16,128]{3,2,1,0:T(8,128)} %get-tuple-element.36.refs_1_) | copy-start | bytes 245764
  11.2 1.7 %collective-permute-start.2 = (f32[13,2,16,128]{3,2,1,0:T(8,128)}, f32[13,2,16,128]{3,2,1,0:T(8,128)S(1)}, u32[]{:S(2)}, u32[]{:S(2)}) collective-permute-start(f32[13,2,16,128]{3,2,1,0:T(8,128)} %get-tuple-element.41), channel_id=1, source_target_pairs={{0,1},{1,0},{2,3},{3,2},{4,5},{5,4},{6,7},{7,6},{8,9},{9,8},{10,11... | collective-permute-start | bytes 638984 | tf_op jit(solution)/shard_map/ppermute | solution.py:563
  11.6 1.7 %collective-permute-start.3 = (f32[13,2,16,128]{3,2,1,0:T(8,128)}, f32[13,2,16,128]{3,2,1,0:T(8,128)S(1)}, u32[]{:S(2)}, u32[]{:S(2)}) collective-permute-start(f32[13,2,16,128]{3,2,1,0:T(8,128)} %get-tuple-element.42), channel_id=1, source_target_pairs={{0,1},{1,0},{2,3},{3,2},{4,5},{5,4},{6,7},{7,6},{8,9},{9,8},{10,11... | collective-permute-start | bytes 638984 | tf_op jit(solution)/shard_map/ppermute | solution.py:563
  11.8 1.8 %collective-permute-start.4 = (f32[13,2,16,128]{3,2,1,0:T(8,128)}, f32[13,2,16,128]{3,2,1,0:T(8,128)S(1)}, u32[]{:S(2)}, u32[]{:S(2)}) collective-permute-start(f32[13,2,16,128]{3,2,1,0:T(8,128)} %get-tuple-element.43), channel_id=1, source_target_pairs={{0,1},{1,0},{2,3},{3,2},{4,5},{5,4},{6,7},{7,6},{8,9},{9,8},{10,11... | collective-permute-start | bytes 638984 | tf_op jit(solution)/shard_map/ppermute | solution.py:563
  13.6 37.5 %collective-permute-start.7 = (f32[8,2,16,128]{3,2,1,0:T(8,128)}, f32[8,2,16,128]{3,2,1,0:T(8,128)S(1)}, u32[]{:S(2)}, u32[]{:S(2)}) collective-permute-start(f32[8,2,16,128]{3,2,1,0:T(8,128)} %get-tuple-element.53), channel_id=1, source_target_pairs={{0,8},{1,9},{2,10},{3,11},{4,12},{5,13},{6,14},{7,15},{8,0},{9,1},... | collective-permute-start | bytes 393224 | tf_op jit(solution)/shard_map/ppermute | solution.py:563
  16.2 35.3 %collective-permute-start.8 = (f32[8,2,16,128]{3,2,1,0:T(8,128)}, f32[8,2,16,128]{3,2,1,0:T(8,128)S(1)}, u32[]{:S(2)}, u32[]{:S(2)}) collective-permute-start(f32[8,2,16,128]{3,2,1,0:T(8,128)} %get-tuple-element.54), channel_id=1, source_target_pairs={{0,9},{1,8},{2,11},{3,10},{4,13},{5,12},{6,15},{7,14},{8,1},{9,0},... | collective-permute-start | bytes 393224 | tf_op jit(solution)/shard_map/ppermute | solution.py:563
  16.5 1.1 %copy-start = (f32[35,2,16,128]{3,2,1,0:T(8,128)S(1)}, f32[35,2,16,128]{3,2,1,0:T(8,128)}, u32[]{:S(2)}) copy-start(f32[35,2,16,128]{3,2,1,0:T(8,128)} %get-tuple-element.39) | copy-start | bytes 1720324
  42.4 12.2 %collective-permute-start.5 = (f32[5,2,16,128]{3,2,1,0:T(8,128)S(1)}, f32[5,2,16,128]{3,2,1,0:T(8,128)S(1)}, u32[]{:S(2)}, u32[]{:S(2)}) collective-permute-start(f32[5,2,16,128]{3,2,1,0:T(8,128)S(1)} %get-tuple-element.45), channel_id=1, source_target_pairs={{0,8},{1,9},{2,10},{3,11},{4,12},{5,13},{6,14},{7,15},{8,0},{9,1},... | collective-permute-start | bytes 245768 | tf_op jit(solution)/shard_map/ppermute | solution.py:563
  42.4 12.2 %collective-permute-start.6 = (f32[5,2,16,128]{3,2,1,0:T(8,128)S(1)}, f32[5,2,16,128]{3,2,1,0:T(8,128)S(1)}, u32[]{:S(2)}, u32[]{:S(2)}) collective-permute-start(f32[5,2,16,128]{3,2,1,0:T(8,128)S(1)} %get-tuple-element.46), channel_id=1, source_target_pairs={{0,9},{1,8},{2,11},{3,10},{4,13},{5,12},{6,15},{7,14},{8,1},{9,0},... | collective-permute-start | bytes 245768 | tf_op jit(solution)/shard_map/ppermute | solution.py:563

commit v4 on v3

--- a/solution.py
+++ b/solution.py
@@ -10,7 +10,7 @@
 BLK = 128
 QRT = 16
 ROW = 2 * QRT
-CHUNKS = (19, 8, 5)
+CHUNKS = (18, 9, 5)
 HINT = 0
 LOCAL = 0
 MATES = 3
@@ -136,10 +136,9 @@
 
 
 def head_body(sz, extent_ref, images_ref, shift_ref, taps_ref, phase_ref, same_ref, cross_ref,
-              mate_par, own_par,
               piece_ref, edge_ref, moved_ref, turned_ref, shifts_ref, raw_ref, pieces_ref, angles_ref,
               sems, par_sems):
-    core, side, own, other = place(extent_ref)
+    core, side, _, other = place(extent_ref)
     windows = (core * sz.slots, (1 - core) * sz.slots)
     small = load_parameters(shift_ref, taps_ref, phase_ref, raw_ref, pieces_ref, angles_ref, par_sems)
     count = piece_ref.shape[1] - 1
@@ -175,30 +174,23 @@
     stores = [pltpu.make_async_copy(*pair, sems.at[i]) for i, pair in enumerate(stores)]
     for store in stores:
         store.start()
-    turn_parameters(sz, (1,), raw_ref, pieces_ref, angles_ref, moved_ref, turned_ref, shifts_ref)
-    for i, level, row in ((0, 0, side * ROW), (1, 1, 0), (2, 1, ROW)):
-        made = [
-            window_parameters(sz, turned_ref, shifts_ref, level, row, first, own, core)
-            for first in windows
-        ]
-        own_par[i] = made[0]
-        mate_par[i] = made[1].reshape(2, QRT, BLK)
     for store in stores:
         store.wait()
 
 
-def near_body(sz, chunks, pieces, extent_ref, images_ref, par_ref, *rest):
-    *rest, far_ref, field_ref, far_sems, sems, out_sems = rest
+def near_body(sz, chunks, extent_ref, images_ref, shift_ref, taps_ref, phase_ref, _, *rest):
+    (*rest, far_ref, field_ref, moved_ref, turned_ref, shifts_ref, raw_ref, pieces_ref, angles_ref,
+     far_sems, sems, par_sems, out_sems) = rest
     sends = 2 * len(chunks) - 2
-    homes, outs = rest[: len(rest) // 2], rest[len(rest) // 2 :]
+    total = (len(rest) - 1) // 2
+    homes, own_par, outs = rest[:total], rest[total], rest[total + 1 :]
     mates, kept = outs[sends:-1], outs[-1]
     core, side, own, other = place(extent_ref)
     windows = (core * sz.slots, (1 - core) * sz.slots)
     far_loads = load_rows(images_ref, far_ref, 1 - side, far_sems)
     loads = load_rows(images_ref, field_ref, side, sems)
     length = mates[0].shape[0]
-    last_load = pltpu.make_async_copy(par_ref, mates[-1].at[pl.ds(length - 3, 3)], sems.at[2])
-    last_load.start()
+    small = load_parameters(shift_ref, taps_ref, phase_ref, raw_ref, pieces_ref, angles_ref, par_sems)
     stores = [pltpu.make_async_copy(outs[i], homes[i], out_sems.at[i]) for i in range(len(outs))]
     for load in far_loads:
         load.wait()
@@ -210,6 +202,16 @@
                 outs[2 * k + i][j] = read_block(far_ref, *where)
             stores[2 * k + i].start()
         begin += count
+    for load in small:
+        load.wait()
+    turn_parameters(sz, (0, 1), raw_ref, pieces_ref, angles_ref, moved_ref, turned_ref, shifts_ref)
+    for i, level, row in ((0, 0, side * ROW), (1, 1, 0), (2, 1, ROW)):
+        made = [
+            window_parameters(sz, turned_ref, shifts_ref, level, row, first, own, core)
+            for first in windows
+        ]
+        own_par[i] = made[0]
+        mates[-1][length - 3 + i] = made[1].reshape(2, QRT, BLK)
     for load in loads:
         load.wait()
 
@@ -226,7 +228,6 @@
         kept[x] = value
 
     put(windows[1], mate_at)
-    last_load.wait()
     for store in stores[sends:-1]:
         store.start()
     put(windows[0], kept_at)
@@ -569,28 +570,26 @@
     blocks = lambda n: (shape(n, 2, QRT, BLK), ANY)
     lanes = (3 * slots // 2 + 1) * BLK
     count = chunks[0] + 1
-    *first, mate_par, own_par = call(
-        functools.partial(head_body, sz),
-        [
-            extents,
-            (images, HBM),
-            (band_shift[0], HBM),
-            (tap_weights[0].transpose(0, 1, 3, 2), HBM),
-            (phases[0].transpose(0, 1, 3, 2), HBM),
-        ],
-        [blocks(count)] * 2 + [(shape(3, 2, QRT, BLK), VMEM), (shape(3, ROW, BLK), VMEM)],
-        [vm(2, count, 2, QRT, BLK), vm(2, 3, 2, QRT, BLK), vm(BLK, BLK), vm(2, half, BLK),
-         vm(2, 2, half, BLK), VMEM((2, 2, half, half), jnp.int32), vm(2, 2, 4, half),
-         vm(2, 2, 2, half), DMA((2,)), DMA((3,))],
+    parameters = [
+        (band_shift[0], HBM),
+        (tap_weights[0].transpose(0, 1, 3, 2), HBM),
+        (phases[0].transpose(0, 1, 3, 2), HBM),
+    ]
+    room = [vm(BLK, BLK), vm(2, half, BLK), vm(2, 2, half, BLK), VMEM((2, 2, half, half), jnp.int32),
+            vm(2, 2, 4, half), vm(2, 2, 2, half)]
+    first = call(
+        functools.partial(head_body, sz), [extents, (images, HBM)] + parameters, [blocks(count)] * 2,
+        [vm(2, count, 2, QRT, BLK), vm(2, 3, 2, QRT, BLK)] + room + [DMA((2,)), DMA((3,))],
         grant=56,
     )
     length = -(-(sz.used + 3) // MATES)
     counts = [n for n in chunks[1:] for _ in range(2)] + [length] * MATES + [sz.used]
-    *packed, kept = call(
-        functools.partial(near_body, sz, chunks, MATES),
-        [extents, (images, HBM), (mate_par, ANY)], [blocks(n) for n in counts],
-        [vm(n, 2, QRT, BLK) for n in counts] + [vm(2, 2, QRT, lanes)] * 2
-        + [DMA((2,)), DMA((3,)), DMA((len(counts),))],
+    *packed, kept, own_par = call(
+        functools.partial(near_body, sz, chunks),
+        [extents, (images, HBM)] + parameters + [(first[0], ANY)],
+        [blocks(n) for n in counts] + [(shape(3, ROW, BLK), VMEM)],
+        [vm(n, 2, QRT, BLK) for n in counts] + [vm(2, 2, QRT, lanes)] * 2 + room
+        + [DMA((2,)), DMA((2,)), DMA((3,)), DMA((len(counts),))],
         grant=56,
     )
     packed, mates = list(first) + packed[:-MATES], packed[-MATES:]

time: 58.2 us -> 57.2 us (0.983); the launches traced: 57.2 us -> 56.9 us
  waiting for transfers between devices: 16.8 us -> 12.7 us
  starting transfers between devices: 9.12 us -> 12.1 us
  local copies, waits for them, and re-layouts: 1.08 us -> 1.87 us
    ppermute x9, waiting for transfers between devices: 16.8 us -> 12.7 us  [per_device(): lax.ppermute(x, 'sub', [(i, i ^ by) for i in range(size)])]
    ppermute x9, starting transfers between devices: 9.12 us -> 12.1 us  [per_device(): lax.ppermute(x, 'sub', [(i, i ^ by) for i in range(size)])]
    unnamed x10, local copies, waits for them, and re-layouts: 1.08 us -> 1.87 us
  transfers between devices with their start and end apart: 9 -> 9, of which waited for: 6 -> 5; matrix products, arithmetic and copies ran while one was open for 0% -> 0% of each run, Pallas kernels for 42% -> 43%
where the time goes in v4:
time: 57.2 us; the launch traced here: 56.9 us
  Pallas kernels  30.1 us (53%)
  waiting for transfers between devices  12.7 us (22%)
  starting transfers between devices  12.1 us (21%)
  local copies, waits for them, and re-layouts  1.87 us (3%)
    pallas_call x9, Pallas kernels, call(): pl.pallas_call(body, out_shape=tuple((x for x, _ in outs)), in_specs=[pl....  30.1 us
    ppermute x9, waiting for transfers between devices, per_device(): lax.ppermute(x, 'sub', [(i, i ^ by) for i in range(size)])  12.7 us
    ppermute x9, starting transfers between devices, per_device(): lax.ppermute(x, 'sub', [(i, i ^ by) for i in range(size)])  12.1 us
    unnamed x10, local copies, waits for them, and re-layouts  1.87 us
  transfers between devices with their start and end apart: 9, of which 5 were waited for; matrix products, arithmetic and copies ran while one was open for 0% of the time, Pallas kernels for 43%

profile of v4, /device:TPU:1, one launch (start us, length us, event | category | flops | bytes accessed | tf_op | source)
XLA Modules:
  0.0 56.9 jit_solution(4731752055970945981)
XLA Ops:
  0.0 2.8 %shard_map.55 = (f32[19,2,16,128]{3,2,1,0:T(8,128)}, f32[19,2,16,128]{3,2,1,0:T(8,128)}) custom-call(s32[16]{0:T(128)} %extent_ref.13, f32[2,64,8192]{2,1,0:T(8,128)} %images_ref.3, s32[2,2,64,64]{3,2,1,0:T(8,128)} %bitcast.40, f32[2,2,4,64]{3,2,1,0:T(4,128)} %bitcast.42, f32[2,2,2,64]{3,2,1,0:T(2,128)} %bitcast.44), custom_call_target="tpu_custom_call" | custom-call | flops 1 | bytes 1 | tf_op jit(solution)/shard_map/pallas_call | solution.py:44
  2.8 3.8 %collective-permute-start.1 = (f32[19,2,16,128]{3,2,1,0:T(8,128)}, f32[19,2,16,128]{3,2,1,0:T(8,128)S(1)}, u32[]{:S(2)}, u32[]{:S(2)}) collective-permute-start(f32[19,2,16,128]{3,2,1,0:T(8,128)} %get-tuple-element.36), channel_id=1, source_target_pairs={{0,9},{1,8},{2,11},{3,10},{4,13},{5,12},{6,15},{7,14},{8,1},{9,0},... | collective-permute-start | bytes 933896 | tf_op jit(solution)/shard_map/ppermute | solution.py:564
  6.5 0.0 copy-start.4
  6.5 0.0 collective-permute-start
  6.5 4.7 %shard_map.56 = (f32[9,2,16,128]{3,2,1,0:T(8,128)}, f32[9,2,16,128]{3,2,1,0:T(8,128)}, f32[5,2,16,128]{3,2,1,0:T(8,128)}, f32[5,2,16,128]{3,2,1,0:T(8,128)}, f32...) custom-call(s32[16]{0:T(128)} %extent_ref.13, ...), custom_call_target="tpu_custom_call" | custom-call | flops 1 | bytes 1 | tf_op jit(solution)/shard_map/pallas_call | solution.py:44
  11.3 0.0 copy-start.1
  11.3 0.0 copy-start.2
  11.3 0.4 collective-permute-start.2
  11.7 0.2 collective-permute-start.3
  11.9 0.3 collective-permute-start.4
  12.2 0.8 %collective-permute-done.2 = f32[13,2,16,128]{3,2,1,0:T(8,128)S(1)} collective-permute-done((f32[13,2,16,128]{3,2,1,0:T(8,128)}, f32[13,2,16,128]{3,2,1,0:T(8,128)S(1)}, u32[]{:S(2)}, u32[]{:S(2)}) %collective-permute-start.2) | collective-permute-done | bytes 213024 | tf_op jit(solution)/shard_map/ppermute | solution.py:564
  13.0 0.3 collective-permute-done.3
  13.4 0.3 collective-permute-done.4
  13.7 2.2 %collective-permute-start.7 = (f32[9,2,16,128]{3,2,1,0:T(8,128)}, f32[9,2,16,128]{3,2,1,0:T(8,128)S(1)}, u32[]{:S(2)}, u32[]{:S(2)}) collective-permute-start(f32[9,2,16,128]{3,2,1,0:T(8,128)} %get-tuple-element.51), channel_id=1, source_target_pairs={{0,8},{1,9},{2,10},{3,11},{4,12},{5,13},{6,14},{7,15},{8,0},{9,1},... | collective-permute-start | bytes 442376 | tf_op jit(solution)/shard_map/ppermute | solution.py:564
  15.9 0.6 %collective-permute-start.8 = (f32[9,2,16,128]{3,2,1,0:T(8,128)}, f32[9,2,16,128]{3,2,1,0:T(8,128)S(1)}, u32[]{:S(2)}, u32[]{:S(2)}) collective-permute-start(f32[9,2,16,128]{3,2,1,0:T(8,128)} %get-tuple-element.52), channel_id=1, source_target_pairs={{0,9},{1,8},{2,11},{3,10},{4,13},{5,12},{6,15},{7,14},{8,1},{9,0},... | collective-permute-start | bytes 442376 | tf_op jit(solution)/shard_map/ppermute | solution.py:564
  16.5 0.0 copy-done.4
  16.5 0.0 copy-start
  16.5 1.1 %copy-done = f32[35,2,16,128]{3,2,1,0:T(8,128)S(1)} copy-done((f32[35,2,16,128]{3,2,1,0:T(8,128)S(1)}, f32[35,2,16,128]{3,2,1,0:T(8,128)}, u32[]{:S(2)}) %copy-start) | copy-done | bytes 573464
  17.6 0.0 copy-start.3
  17.6 0.8 %copy-done.3 = f32[3,32,128]{2,1,0:T(8,128)S(1)} copy-done((f32[3,32,128]{2,1,0:T(8,128)S(1)}, f32[3,32,128]{2,1,0:T(8,128)}, u32[]{:S(2)}) %copy-start.3) | copy-done | bytes 49176
  18.4 9.9 %shard_map.57 = (f32[32,2,4,16,128]{4,3,2,1,0:T(8,128)S(1)}, f32[2,4,3,16,128]{4,3,2,1,0:T(8,128)S(1)}, f32[2,2,4,6,16,128]{5,4,3,2,1,0:T(8,128)S(1)}) custom-call(s32[16]{0:T(128)S(1)} %copy-done.4, f32[35,32,128]{2,1,0:T(8,128)S(1)} %bitcast.35, f32[3,32,128]{2,1,0:T(8,128)S(1)} %copy-done.3, f32[13,32,128]{2,1,0:T(8,128)S(1)} %bitcast.30, ...), custom_call_target="tpu_custom_call" | custom-call | flops 1 | bytes 1 | tf_op jit(solution)/shard_map/pallas_call | solution.py:44
  28.3 6.0 %collective-permute-done.1 = f32[19,2,16,128]{3,2,1,0:T(8,128)S(1)} collective-permute-done((f32[19,2,16,128]{3,2,1,0:T(8,128)}, f32[19,2,16,128]{3,2,1,0:T(8,128)S(1)}, u32[]{:S(2)}, u32[]{:S(2)}) %collective-permute-start.1) | collective-permute-done | bytes 311328 | tf_op jit(solution)/shard_map/ppermute | solution.py:564
  34.3 5.3 %collective-permute-done = f32[19,2,16,128]{3,2,1,0:T(8,128)S(1)} collective-permute-done((f32[19,2,16,128]{3,2,1,0:T(8,128)}, f32[19,2,16,128]{3,2,1,0:T(8,128)S(1)}, u32[]{:S(2)}, u32[]{:S(2)}) %collective-permute-start) | collective-permute-done | bytes 311328 | tf_op jit(solution)/shard_map/ppermute | solution.py:564
  39.6 0.0 copy-done.1
  39.6 0.0 copy-done.2
  39.6 0.0 collective-permute-start.5
  39.6 4.6 %collective-permute-start.6 = (f32[5,2,16,128]{3,2,1,0:T(8,128)S(1)}, f32[5,2,16,128]{3,2,1,0:T(8,128)S(1)}, u32[]{:S(2)}, u32[]{:S(2)}) collective-permute-start(f32[5,2,16,128]{3,2,1,0:T(8,128)S(1)} %get-tuple-element.44), channel_id=1, source_target_pairs={{0,9},{1,8},{2,11},{3,10},{4,13},{5,12},{6,15},{7,14},{8,1},{9,0},... | collective-permute-start | bytes 245768 | tf_op jit(solution)/shard_map/ppermute | solution.py:564
  44.2 1.9 %shard_map.59 = (f32[2,2,3,16,128]{4,3,2,1,0:T(8,128)S(1)}, f32[2,2,2,6,16,128]{5,4,3,2,1,0:T(8,128)S(1)}, f32[8,2,2,9,16,128]{5,4,3,2,1,0:T(8,128)S(1)}, f32[7,4,9,16,128]{4,3,2,1,0:T(8,128)S(1)}) custom-call(s32[16]{0:T(128)S(1)} %copy-done.4, f32[19,32,128]{2,1,0:T(8,128)S(1)} %bitcast.24, f32[19,32,128]{2,1,0:T(8,128)S(1)} %bitcast.18, ...), custom_call_target="tpu_custom_call" | custom-call | flops 1 | bytes 1 | tf_op jit(solution)/shard_map/pallas_call | solution.py:44
  46.1 4.9 %shard_map.61 = (f32[2,64,4096]{2,1,0:T(8,128)}, f32[2,2,32,128]{3,2,1,0:T(8,128)S(1)}, f32[2,2,32,128]{3,2,1,0:T(8,128)S(1)}) custom-call(s32[16]{0:T(128)S(1)} %copy-done.4, f32[19,32,128]{2,1,0:T(8,128)S(1)} %bitcast.25, f32[19,32,128]{2,1,0:T(8,128)S(1)} %bitcast.19, f32[19,32,128]{2,1,0:T(8,128)S(1)} %bitcast.26, f32[19,32,128]{2,1,0:T(8,128)S(1)} %bitcast.20, ...), custom_call_target="tpu_custom_call" | custom-call | flops 1 | bytes 1 | tf_op jit(solution)/shard_map/pallas_call | solution.py:44
  51.0 0.0 collective-permute-done.7
  51.0 0.0 collective-permute-done.8
  51.0 3.3 %shard_map.62 = (f32[2,64,4096]{2,1,0:T(8,128)}, f32[2,2,32,128]{3,2,1,0:T(8,128)S(1)}, f32[2,2,32,128]{3,2,1,0:T(8,128)S(1)}) custom-call(s32[16]{0:T(128)S(1)} %copy-done.4, f32[9,32,128]{2,1,0:T(8,128)S(1)} %bitcast.36, f32[9,32,128]{2,1,0:T(8,128)S(1)} %bitcast.37, f32[19,32,128]{2,1,0:T(8,128)S(1)} %bitcast.27, ...), custom_call_target="tpu_custom_call", output_to_operand_aliasing={{0}: (12, {})} | custom-call | flops 100000000 | bytes 300001 | tf_op jit(solution)/shard_map/pallas_call | solution.py:44
  54.2 0.0 collective-permute-done.5
  54.3 0.0 collective-permute-done.6
  54.3 2.6 %shard_map.63 = f32[2,64,4096]{2,1,0:T(8,128)} custom-call(s32[16]{0:T(128)S(1)} %copy-done.4, f32[5,32,128]{2,1,0:T(8,128)S(1)} %bitcast.38, f32[5,32,128]{2,1,0:T(8,128)S(1)} %bitcast.39, f32[19,32,128]{2,1,0:T(8,128)S(1)} %bitcast.28, f32[19,32,128]{2,1,0:T(8,128)S(1)} %bitcast.22, ...), custom_call_target="tpu_custom_call", output_to_operand_aliasing={{}: (10, {})} | custom-call | flops 100000000 | bytes 300001 | tf_op jit(solution)/shard_map/pallas_call | solution.py:44
  (2 shorter events, 0.0 us)
Async XLA Ops:
  2.8 31.5 %collective-permute-start.1 = (f32[19,2,16,128]{3,2,1,0:T(8,128)}, f32[19,2,16,128]{3,2,1,0:T(8,128)S(1)}, u32[]{:S(2)}, u32[]{:S(2)}) collective-permute-start(f32[19,2,16,128]{3,2,1,0:T(8,128)} %get-tuple-element.36), channel_id=1, source_target_pairs={{0,9},{1,8},{2,11},{3,10},{4,13},{5,12},{6,15},{7,14},{8,1},{9,0},... | collective-permute-start | bytes 933896 | tf_op jit(solution)/shard_map/ppermute | solution.py:564
  6.5 10.0 %copy-start.4 = (s32[16]{0:T(128)S(1)}, s32[16]{0:T(128)}, u32[]{:S(2)}) copy-start(s32[16]{0:T(128)} %extent_ref.13) | copy-start | bytes 196
  6.5 33.1 %collective-permute-start = (f32[19,2,16,128]{3,2,1,0:T(8,128)}, f32[19,2,16,128]{3,2,1,0:T(8,128)S(1)}, u32[]{:S(2)}, u32[]{:S(2)}) collective-permute-start(f32[19,2,16,128]{3,2,1,0:T(8,128)} %get-tuple-element.33._), channel_id=1, source_target_pairs={{0,8},{1,9},{2,10},{3,11},{4,12},{5,13},{6,14},{7,15},{8,0},{9,1},... | collective-permute-start | bytes 933896 | tf_op jit(solution)/shard_map/ppermute | solution.py:564
  11.3 28.3 %copy-start.1 = (f32[5,2,16,128]{3,2,1,0:T(8,128)S(1)}, f32[5,2,16,128]{3,2,1,0:T(8,128)}, u32[]{:S(2)}) copy-start(f32[5,2,16,128]{3,2,1,0:T(8,128)} %get-tuple-element.34.refs_0_) | copy-start | bytes 245764
  11.3 28.3 %copy-start.2 = (f32[5,2,16,128]{3,2,1,0:T(8,128)S(1)}, f32[5,2,16,128]{3,2,1,0:T(8,128)}, u32[]{:S(2)}) copy-start(f32[5,2,16,128]{3,2,1,0:T(8,128)} %get-tuple-element.35.refs_1_) | copy-start | bytes 245764
  11.3 1.7 %collective-permute-start.2 = (f32[13,2,16,128]{3,2,1,0:T(8,128)}, f32[13,2,16,128]{3,2,1,0:T(8,128)S(1)}, u32[]{:S(2)}, u32[]{:S(2)}) collective-permute-start(f32[13,2,16,128]{3,2,1,0:T(8,128)} %get-tuple-element.39), channel_id=1, source_target_pairs={{0,1},{1,0},{2,3},{3,2},{4,5},{5,4},{6,7},{7,6},{8,9},{9,8},{10,11... | collective-permute-start | bytes 638984 | tf_op jit(solution)/shard_map/ppermute | solution.py:564
  11.7 1.7 %collective-permute-start.3 = (f32[13,2,16,128]{3,2,1,0:T(8,128)}, f32[13,2,16,128]{3,2,1,0:T(8,128)S(1)}, u32[]{:S(2)}, u32[]{:S(2)}) collective-permute-start(f32[13,2,16,128]{3,2,1,0:T(8,128)} %get-tuple-element.40), channel_id=1, source_target_pairs={{0,1},{1,0},{2,3},{3,2},{4,5},{5,4},{6,7},{7,6},{8,9},{9,8},{10,11... | collective-permute-start | bytes 638984 | tf_op jit(solution)/shard_map/ppermute | solution.py:564
  11.9 1.8 %collective-permute-start.4 = (f32[13,2,16,128]{3,2,1,0:T(8,128)}, f32[13,2,16,128]{3,2,1,0:T(8,128)S(1)}, u32[]{:S(2)}, u32[]{:S(2)}) collective-permute-start(f32[13,2,16,128]{3,2,1,0:T(8,128)} %get-tuple-element.41), channel_id=1, source_target_pairs={{0,1},{1,0},{2,3},{3,2},{4,5},{5,4},{6,7},{7,6},{8,9},{9,8},{10,11... | collective-permute-start | bytes 638984 | tf_op jit(solution)/shard_map/ppermute | solution.py:564
  13.7 37.3 %collective-permute-start.7 = (f32[9,2,16,128]{3,2,1,0:T(8,128)}, f32[9,2,16,128]{3,2,1,0:T(8,128)S(1)}, u32[]{:S(2)}, u32[]{:S(2)}) collective-permute-start(f32[9,2,16,128]{3,2,1,0:T(8,128)} %get-tuple-element.51), channel_id=1, source_target_pairs={{0,8},{1,9},{2,10},{3,11},{4,12},{5,13},{6,14},{7,15},{8,0},{9,1},... | collective-permute-start | bytes 442376 | tf_op jit(solution)/shard_map/ppermute | solution.py:564
  15.9 35.1 %collective-permute-start.8 = (f32[9,2,16,128]{3,2,1,0:T(8,128)}, f32[9,2,16,128]{3,2,1,0:T(8,128)S(1)}, u32[]{:S(2)}, u32[]{:S(2)}) collective-permute-start(f32[9,2,16,128]{3,2,1,0:T(8,128)} %get-tuple-element.52), channel_id=1, source_target_pairs={{0,9},{1,8},{2,11},{3,10},{4,13},{5,12},{6,15},{7,14},{8,1},{9,0},... | collective-permute-start | bytes 442376 | tf_op jit(solution)/shard_map/ppermute | solution.py:564
  16.5 1.1 %copy-start = (f32[35,2,16,128]{3,2,1,0:T(8,128)S(1)}, f32[35,2,16,128]{3,2,1,0:T(8,128)}, u32[]{:S(2)}) copy-start(f32[35,2,16,128]{3,2,1,0:T(8,128)} %get-tuple-element.37) | copy-start | bytes 1720324
  17.6 0.8 %copy-start.3 = (f32[3,32,128]{2,1,0:T(8,128)S(1)}, f32[3,32,128]{2,1,0:T(8,128)}, u32[]{:S(2)}) copy-start(f32[3,32,128]{2,1,0:T(8,128)} %get-tuple-element.38.par) | copy-start | bytes 147460
  39.6 14.6 %collective-permute-start.5 = (f32[5,2,16,128]{3,2,1,0:T(8,128)S(1)}, f32[5,2,16,128]{3,2,1,0:T(8,128)S(1)}, u32[]{:S(2)}, u32[]{:S(2)}) collective-permute-start(f32[5,2,16,128]{3,2,1,0:T(8,128)S(1)} %get-tuple-element.43), channel_id=1, source_target_pairs={{0,8},{1,9},{2,10},{3,11},{4,12},{5,13},{6,14},{7,15},{8,0},{9,1},... | collective-permute-start | bytes 245768 | tf_op jit(solution)/shard_map/ppermute | solution.py:564
  39.6 14.6 %collective-permute-start.6 = (f32[5,2,16,128]{3,2,1,0:T(8,128)S(1)}, f32[5,2,16,128]{3,2,1,0:T(8,128)S(1)}, u32[]{:S(2)}, u32[]{:S(2)}) collective-permute-start(f32[5,2,16,128]{3,2,1,0:T(8,128)S(1)} %get-tuple-element.44), channel_id=1, source_target_pairs={{0,9},{1,8},{2,11},{3,10},{4,13},{5,12},{6,15},{7,14},{8,1},{9,0},... | collective-permute-start | bytes 245768 | tf_op jit(solution)/shard_map/ppermute | solution.py:564

commit v5 on v4

--- a/solution.py
+++ b/solution.py
@@ -137,7 +137,7 @@
 
 def head_body(sz, extent_ref, images_ref, shift_ref, taps_ref, phase_ref, same_ref, cross_ref,
               piece_ref, edge_ref, moved_ref, turned_ref, shifts_ref, raw_ref, pieces_ref, angles_ref,
-              sems, par_sems):
+              sems, par_sems, out_sems):
     core, side, _, other = place(extent_ref)
     windows = (core * sz.slots, (1 - core) * sz.slots)
     small = load_parameters(shift_ref, taps_ref, phase_ref, raw_ref, pieces_ref, angles_ref, par_sems)
@@ -154,26 +154,31 @@
     for i in range(2):
         for j in range(count):
             fetch(*slot_block(other, windows[i] + j), piece_ref.at[i, j], sems.at[1])
+    homes = (same_ref, cross_ref)
+    stores = []
+
+    def put(i, blocks):
+        source, target = piece_ref.at[i, blocks], homes[i].at[blocks]
+        stores.append(pltpu.make_async_copy(source, target, out_sems.at[len(stores)]))
+        stores[-1].start()
+
+    wait_whole(piece_ref.at[:, pl.ds(0, count)], sems.at[1])
+    for i in range(2):
+        put(i, pl.ds(0, count))
     for load in small:
         load.wait()
     turn_parameters(sz, (0,), raw_ref, pieces_ref, angles_ref, moved_ref, turned_ref, shifts_ref)
     lane = lax.broadcasted_iota(jnp.int32, (ROW, BLK), 1)
-    results = [
-        window_parameters(sz, turned_ref, shifts_ref, 0, (1 - side) * ROW, windows[i], other, core)
-        for i in range(2)
-    ]
     wait_whole(edge_ref, sems.at[0])
     for i in range(2):
         left, right, middle = (edge_ref[i, n].reshape(ROW, BLK) for n in range(3))
-        result = jnp.where(lane < 2 * REACH, pltpu.roll(middle, REACH, 1), results[i])
+        row = (1 - side) * ROW
+        result = window_parameters(sz, turned_ref, shifts_ref, 0, row, windows[i], other, core)
+        result = jnp.where(lane < 2 * REACH, pltpu.roll(middle, REACH, 1), result)
         result = jnp.where(lane < REACH, right, result)
         result = jnp.where(lane >= BLK - 2, left, result)
         piece_ref[i, count] = result.reshape(2, QRT, BLK)
-    wait_whole(piece_ref.at[:, pl.ds(0, count)], sems.at[1])
-    stores = [(piece_ref.at[0], same_ref), (piece_ref.at[1], cross_ref)]
-    stores = [pltpu.make_async_copy(*pair, sems.at[i]) for i, pair in enumerate(stores)]
-    for store in stores:
-        store.start()
+        put(i, pl.ds(count, 1))
     for store in stores:
         store.wait()
 
@@ -360,8 +365,11 @@
     if right:
         part = part_of(sz.slots - 1)
         level_one(d_ref, f_ref, coef_at(sz.right, part), sz.right, sz.slots, sz.zero)
-    before = jnp.clip(extent - first, low + 1, high)
-    level_one(d_ref, f_ref, coef_at(sz.middle, 0), sz.middle, before, sz.zero)
+    before = extent - first
+
+    @pl.when(jnp.logical_and(before > low, before <= high))
+    def _():
+        level_one(d_ref, f_ref, coef_at(sz.middle, 0), sz.middle, before, sz.zero)
 
 
 def table_coef(tab, ltab):
@@ -579,7 +587,8 @@
             vm(2, 2, 4, half), vm(2, 2, 2, half)]
     first = call(
         functools.partial(head_body, sz), [extents, (images, HBM)] + parameters, [blocks(count)] * 2,
-        [vm(2, count, 2, QRT, BLK), vm(2, 3, 2, QRT, BLK)] + room + [DMA((2,)), DMA((3,))],
+        [vm(2, count, 2, QRT, BLK), vm(2, 3, 2, QRT, BLK)] + room
+        + [DMA((2,)), DMA((3,)), DMA((4,))],
         grant=56,
     )
     length = -(-(sz.used + 3) // MATES)

time: 57.2 us -> 57 us (level)
  no operation moved by 1% of the time
where the time goes in v5:
time: 57 us; the launch traced here: 56.7 us
  Pallas kernels  29.8 us (52%)
  waiting for transfers between devices  12.8 us (22%)
  starting transfers between devices  12.1 us (21%)
  local copies, waits for them, and re-layouts  1.87 us (3%)
    pallas_call x9, Pallas kernels, call(): pl.pallas_call(body, out_shape=tuple((x for x, _ in outs)), in_specs=[pl....  29.8 us
    ppermute x9, waiting for transfers between devices, per_device(): lax.ppermute(x, 'sub', [(i, i ^ by) for i in range(size)])  12.8 us
    ppermute x9, starting transfers between devices, per_device(): lax.ppermute(x, 'sub', [(i, i ^ by) for i in range(size)])  12.1 us
    unnamed x10, local copies, waits for them, and re-layouts  1.87 us
  transfers between devices with their start and end apart: 9, of which 5 were waited for; matrix products, arithmetic and copies ran while one was open for 0% of the time, Pallas kernels for 43%

profile of v5, /device:TPU:1, one launch (start us, length us, event | category | flops | bytes accessed | tf_op | source)
XLA Modules:
  0.0 56.7 jit_solution(14710176628875422203)
XLA Ops:
  0.0 2.8 %shard_map.55 = (f32[19,2,16,128]{3,2,1,0:T(8,128)}, f32[19,2,16,128]{3,2,1,0:T(8,128)}) custom-call(s32[16]{0:T(128)} %extent_ref.13, f32[2,64,8192]{2,1,0:T(8,128)} %images_ref.3, s32[2,2,64,64]{3,2,1,0:T(8,128)} %bitcast.40, f32[2,2,4,64]{3,2,1,0:T(4,128)} %bitcast.42, f32[2,2,2,64]{3,2,1,0:T(2,128)} %bitcast.44), custom_call_target="tpu_custom_call" | custom-call | flops 1 | bytes 1 | tf_op jit(solution)/shard_map/pallas_call | solution.py:44
  2.8 3.8 %collective-permute-start.1 = (f32[19,2,16,128]{3,2,1,0:T(8,128)}, f32[19,2,16,128]{3,2,1,0:T(8,128)S(1)}, u32[]{:S(2)}, u32[]{:S(2)}) collective-permute-start(f32[19,2,16,128]{3,2,1,0:T(8,128)} %get-tuple-element.36), channel_id=1, source_target_pairs={{0,9},{1,8},{2,11},{3,10},{4,13},{5,12},{6,15},{7,14},{8,1},{9,0},... | collective-permute-start | bytes 933896 | tf_op jit(solution)/shard_map/ppermute | solution.py:572
  6.6 0.0 copy-start.4
  6.6 0.0 collective-permute-start
  6.6 4.7 %shard_map.56 = (f32[9,2,16,128]{3,2,1,0:T(8,128)}, f32[9,2,16,128]{3,2,1,0:T(8,128)}, f32[5,2,16,128]{3,2,1,0:T(8,128)}, f32[5,2,16,128]{3,2,1,0:T(8,128)}, f32...) custom-call(s32[16]{0:T(128)} %extent_ref.13, ...), custom_call_target="tpu_custom_call" | custom-call | flops 1 | bytes 1 | tf_op jit(solution)/shard_map/pallas_call | solution.py:44
  11.3 0.0 copy-start.1
  11.3 0.0 copy-start.2
  11.3 0.4 collective-permute-start.2
  11.7 0.2 collective-permute-start.3
  11.9 0.3 collective-permute-start.4
  12.3 0.8 %collective-permute-done.2 = f32[13,2,16,128]{3,2,1,0:T(8,128)S(1)} collective-permute-done((f32[13,2,16,128]{3,2,1,0:T(8,128)}, f32[13,2,16,128]{3,2,1,0:T(8,128)S(1)}, u32[]{:S(2)}, u32[]{:S(2)}) %collective-permute-start.2) | collective-permute-done | bytes 213024 | tf_op jit(solution)/shard_map/ppermute | solution.py:572
  13.1 0.3 collective-permute-done.3
  13.4 0.3 collective-permute-done.4
  13.7 2.2 %collective-permute-start.7 = (f32[9,2,16,128]{3,2,1,0:T(8,128)}, f32[9,2,16,128]{3,2,1,0:T(8,128)S(1)}, u32[]{:S(2)}, u32[]{:S(2)}) collective-permute-start(f32[9,2,16,128]{3,2,1,0:T(8,128)} %get-tuple-element.51), channel_id=1, source_target_pairs={{0,8},{1,9},{2,10},{3,11},{4,12},{5,13},{6,14},{7,15},{8,0},{9,1},... | collective-permute-start | bytes 442376 | tf_op jit(solution)/shard_map/ppermute | solution.py:572
  15.9 0.6 %collective-permute-start.8 = (f32[9,2,16,128]{3,2,1,0:T(8,128)}, f32[9,2,16,128]{3,2,1,0:T(8,128)S(1)}, u32[]{:S(2)}, u32[]{:S(2)}) collective-permute-start(f32[9,2,16,128]{3,2,1,0:T(8,128)} %get-tuple-element.52), channel_id=1, source_target_pairs={{0,9},{1,8},{2,11},{3,10},{4,13},{5,12},{6,15},{7,14},{8,1},{9,0},... | collective-permute-start | bytes 442376 | tf_op jit(solution)/shard_map/ppermute | solution.py:572
  16.6 0.0 copy-done.4
  16.6 0.0 copy-start
  16.6 1.1 %copy-done = f32[35,2,16,128]{3,2,1,0:T(8,128)S(1)} copy-done((f32[35,2,16,128]{3,2,1,0:T(8,128)S(1)}, f32[35,2,16,128]{3,2,1,0:T(8,128)}, u32[]{:S(2)}) %copy-start) | copy-done | bytes 573464
  17.6 0.0 copy-start.3
  17.6 0.8 %copy-done.3 = f32[3,32,128]{2,1,0:T(8,128)S(1)} copy-done((f32[3,32,128]{2,1,0:T(8,128)S(1)}, f32[3,32,128]{2,1,0:T(8,128)}, u32[]{:S(2)}) %copy-start.3) | copy-done | bytes 49176
  18.4 9.9 %shard_map.57 = (f32[32,2,4,16,128]{4,3,2,1,0:T(8,128)S(1)}, f32[2,4,3,16,128]{4,3,2,1,0:T(8,128)S(1)}, f32[2,2,4,6,16,128]{5,4,3,2,1,0:T(8,128)S(1)}) custom-call(s32[16]{0:T(128)S(1)} %copy-done.4, f32[35,32,128]{2,1,0:T(8,128)S(1)} %bitcast.35, f32[3,32,128]{2,1,0:T(8,128)S(1)} %copy-done.3, f32[13,32,128]{2,1,0:T(8,128)S(1)} %bitcast.30, ...), custom_call_target="tpu_custom_call" | custom-call | flops 1 | bytes 1 | tf_op jit(solution)/shard_map/pallas_call | solution.py:44
  28.3 6.0 %collective-permute-done.1 = f32[19,2,16,128]{3,2,1,0:T(8,128)S(1)} collective-permute-done((f32[19,2,16,128]{3,2,1,0:T(8,128)}, f32[19,2,16,128]{3,2,1,0:T(8,128)S(1)}, u32[]{:S(2)}, u32[]{:S(2)}) %collective-permute-start.1) | collective-permute-done | bytes 311328 | tf_op jit(solution)/shard_map/ppermute | solution.py:572
  34.3 5.3 %collective-permute-done = f32[19,2,16,128]{3,2,1,0:T(8,128)S(1)} collective-permute-done((f32[19,2,16,128]{3,2,1,0:T(8,128)}, f32[19,2,16,128]{3,2,1,0:T(8,128)S(1)}, u32[]{:S(2)}, u32[]{:S(2)}) %collective-permute-start) | collective-permute-done | bytes 311328 | tf_op jit(solution)/shard_map/ppermute | solution.py:572
  39.6 0.0 copy-done.1
  39.6 0.0 copy-done.2
  39.6 0.0 collective-permute-start.5
  39.7 4.6 %collective-permute-start.6 = (f32[5,2,16,128]{3,2,1,0:T(8,128)S(1)}, f32[5,2,16,128]{3,2,1,0:T(8,128)S(1)}, u32[]{:S(2)}, u32[]{:S(2)}) collective-permute-start(f32[5,2,16,128]{3,2,1,0:T(8,128)S(1)} %get-tuple-element.44), channel_id=1, source_target_pairs={{0,9},{1,8},{2,11},{3,10},{4,13},{5,12},{6,15},{7,14},{8,1},{9,0},... | collective-permute-start | bytes 245768 | tf_op jit(solution)/shard_map/ppermute | solution.py:572
  44.2 1.9 %shard_map.59 = (f32[2,2,3,16,128]{4,3,2,1,0:T(8,128)S(1)}, f32[2,2,2,6,16,128]{5,4,3,2,1,0:T(8,128)S(1)}, f32[8,2,2,9,16,128]{5,4,3,2,1,0:T(8,128)S(1)}, f32[7,4,9,16,128]{4,3,2,1,0:T(8,128)S(1)}) custom-call(s32[16]{0:T(128)S(1)} %copy-done.4, f32[19,32,128]{2,1,0:T(8,128)S(1)} %bitcast.24, f32[19,32,128]{2,1,0:T(8,128)S(1)} %bitcast.18, ...), custom_call_target="tpu_custom_call" | custom-call | flops 1 | bytes 1 | tf_op jit(solution)/shard_map/pallas_call | solution.py:44
  46.1 4.8 %shard_map.61 = (f32[2,64,4096]{2,1,0:T(8,128)}, f32[2,2,32,128]{3,2,1,0:T(8,128)S(1)}, f32[2,2,32,128]{3,2,1,0:T(8,128)S(1)}) custom-call(s32[16]{0:T(128)S(1)} %copy-done.4, f32[19,32,128]{2,1,0:T(8,128)S(1)} %bitcast.25, f32[19,32,128]{2,1,0:T(8,128)S(1)} %bitcast.19, f32[19,32,128]{2,1,0:T(8,128)S(1)} %bitcast.26, f32[19,32,128]{2,1,0:T(8,128)S(1)} %bitcast.20, ...), custom_call_target="tpu_custom_call" | custom-call | flops 1 | bytes 1 | tf_op jit(solution)/shard_map/pallas_call | solution.py:44
  50.9 0.0 collective-permute-done.7
  50.9 0.0 collective-permute-done.8
  50.9 3.2 %shard_map.62 = (f32[2,64,4096]{2,1,0:T(8,128)}, f32[2,2,32,128]{3,2,1,0:T(8,128)S(1)}, f32[2,2,32,128]{3,2,1,0:T(8,128)S(1)}) custom-call(s32[16]{0:T(128)S(1)} %copy-done.4, f32[9,32,128]{2,1,0:T(8,128)S(1)} %bitcast.36, f32[9,32,128]{2,1,0:T(8,128)S(1)} %bitcast.37, f32[19,32,128]{2,1,0:T(8,128)S(1)} %bitcast.27, ...), custom_call_target="tpu_custom_call", output_to_operand_aliasing={{0}: (12, {})} | custom-call | flops 100000000 | bytes 300001 | tf_op jit(solution)/shard_map/pallas_call | solution.py:44
  54.1 0.0 collective-permute-done.5
  54.1 0.0 collective-permute-done.6
  54.1 2.6 %shard_map.63 = f32[2,64,4096]{2,1,0:T(8,128)} custom-call(s32[16]{0:T(128)S(1)} %copy-done.4, f32[5,32,128]{2,1,0:T(8,128)S(1)} %bitcast.38, f32[5,32,128]{2,1,0:T(8,128)S(1)} %bitcast.39, f32[19,32,128]{2,1,0:T(8,128)S(1)} %bitcast.28, f32[19,32,128]{2,1,0:T(8,128)S(1)} %bitcast.22, ...), custom_call_target="tpu_custom_call", output_to_operand_aliasing={{}: (10, {})} | custom-call | flops 100000000 | bytes 300001 | tf_op jit(solution)/shard_map/pallas_call | solution.py:44
  (2 shorter events, 0.0 us)
Async XLA Ops:
  2.8 31.5 %collective-permute-start.1 = (f32[19,2,16,128]{3,2,1,0:T(8,128)}, f32[19,2,16,128]{3,2,1,0:T(8,128)S(1)}, u32[]{:S(2)}, u32[]{:S(2)}) collective-permute-start(f32[19,2,16,128]{3,2,1,0:T(8,128)} %get-tuple-element.36), channel_id=1, source_target_pairs={{0,9},{1,8},{2,11},{3,10},{4,13},{5,12},{6,15},{7,14},{8,1},{9,0},... | collective-permute-start | bytes 933896 | tf_op jit(solution)/shard_map/ppermute | solution.py:572
  6.6 10.0 %copy-start.4 = (s32[16]{0:T(128)S(1)}, s32[16]{0:T(128)}, u32[]{:S(2)}) copy-start(s32[16]{0:T(128)} %extent_ref.13) | copy-start | bytes 196
  6.6 33.1 %collective-permute-start = (f32[19,2,16,128]{3,2,1,0:T(8,128)}, f32[19,2,16,128]{3,2,1,0:T(8,128)S(1)}, u32[]{:S(2)}, u32[]{:S(2)}) collective-permute-start(f32[19,2,16,128]{3,2,1,0:T(8,128)} %get-tuple-element.33._), channel_id=1, source_target_pairs={{0,8},{1,9},{2,10},{3,11},{4,12},{5,13},{6,14},{7,15},{8,0},{9,1},... | collective-permute-start | bytes 933896 | tf_op jit(solution)/shard_map/ppermute | solution.py:572
  11.3 28.3 %copy-start.1 = (f32[5,2,16,128]{3,2,1,0:T(8,128)S(1)}, f32[5,2,16,128]{3,2,1,0:T(8,128)}, u32[]{:S(2)}) copy-start(f32[5,2,16,128]{3,2,1,0:T(8,128)} %get-tuple-element.34.refs_0_) | copy-start | bytes 245764
  11.3 28.3 %copy-start.2 = (f32[5,2,16,128]{3,2,1,0:T(8,128)S(1)}, f32[5,2,16,128]{3,2,1,0:T(8,128)}, u32[]{:S(2)}) copy-start(f32[5,2,16,128]{3,2,1,0:T(8,128)} %get-tuple-element.35.refs_1_) | copy-start | bytes 245764
  11.3 1.7 %collective-permute-start.2 = (f32[13,2,16,128]{3,2,1,0:T(8,128)}, f32[13,2,16,128]{3,2,1,0:T(8,128)S(1)}, u32[]{:S(2)}, u32[]{:S(2)}) collective-permute-start(f32[13,2,16,128]{3,2,1,0:T(8,128)} %get-tuple-element.39), channel_id=1, source_target_pairs={{0,1},{1,0},{2,3},{3,2},{4,5},{5,4},{6,7},{7,6},{8,9},{9,8},{10,11... | collective-permute-start | bytes 638984 | tf_op jit(solution)/shard_map/ppermute | solution.py:572
  11.7 1.7 %collective-permute-start.3 = (f32[13,2,16,128]{3,2,1,0:T(8,128)}, f32[13,2,16,128]{3,2,1,0:T(8,128)S(1)}, u32[]{:S(2)}, u32[]{:S(2)}) collective-permute-start(f32[13,2,16,128]{3,2,1,0:T(8,128)} %get-tuple-element.40), channel_id=1, source_target_pairs={{0,1},{1,0},{2,3},{3,2},{4,5},{5,4},{6,7},{7,6},{8,9},{9,8},{10,11... | collective-permute-start | bytes 638984 | tf_op jit(solution)/shard_map/ppermute | solution.py:572
  11.9 1.8 %collective-permute-start.4 = (f32[13,2,16,128]{3,2,1,0:T(8,128)}, f32[13,2,16,128]{3,2,1,0:T(8,128)S(1)}, u32[]{:S(2)}, u32[]{:S(2)}) collective-permute-start(f32[13,2,16,128]{3,2,1,0:T(8,128)} %get-tuple-element.41), channel_id=1, source_target_pairs={{0,1},{1,0},{2,3},{3,2},{4,5},{5,4},{6,7},{7,6},{8,9},{9,8},{10,11... | collective-permute-start | bytes 638984 | tf_op jit(solution)/shard_map/ppermute | solution.py:572
  13.7 37.2 %collective-permute-start.7 = (f32[9,2,16,128]{3,2,1,0:T(8,128)}, f32[9,2,16,128]{3,2,1,0:T(8,128)S(1)}, u32[]{:S(2)}, u32[]{:S(2)}) collective-permute-start(f32[9,2,16,128]{3,2,1,0:T(8,128)} %get-tuple-element.51), channel_id=1, source_target_pairs={{0,8},{1,9},{2,10},{3,11},{4,12},{5,13},{6,14},{7,15},{8,0},{9,1},... | collective-permute-start | bytes 442376 | tf_op jit(solution)/shard_map/ppermute | solution.py:572
  15.9 35.0 %collective-permute-start.8 = (f32[9,2,16,128]{3,2,1,0:T(8,128)}, f32[9,2,16,128]{3,2,1,0:T(8,128)S(1)}, u32[]{:S(2)}, u32[]{:S(2)}) collective-permute-start(f32[9,2,16,128]{3,2,1,0:T(8,128)} %get-tuple-element.52), channel_id=1, source_target_pairs={{0,9},{1,8},{2,11},{3,10},{4,13},{5,12},{6,15},{7,14},{8,1},{9,0},... | collective-permute-start | bytes 442376 | tf_op jit(solution)/shard_map/ppermute | solution.py:572
  16.6 1.1 %copy-start = (f32[35,2,16,128]{3,2,1,0:T(8,128)S(1)}, f32[35,2,16,128]{3,2,1,0:T(8,128)}, u32[]{:S(2)}) copy-start(f32[35,2,16,128]{3,2,1,0:T(8,128)} %get-tuple-element.37) | copy-start | bytes 1720324
  17.6 0.8 %copy-start.3 = (f32[3,32,128]{2,1,0:T(8,128)S(1)}, f32[3,32,128]{2,1,0:T(8,128)}, u32[]{:S(2)}) copy-start(f32[3,32,128]{2,1,0:T(8,128)} %get-tuple-element.38.par) | copy-start | bytes 147460
  39.6 14.5 %collective-permute-start.5 = (f32[5,2,16,128]{3,2,1,0:T(8,128)S(1)}, f32[5,2,16,128]{3,2,1,0:T(8,128)S(1)}, u32[]{:S(2)}, u32[]{:S(2)}) collective-permute-start(f32[5,2,16,128]{3,2,1,0:T(8,128)S(1)} %get-tuple-element.43), channel_id=1, source_target_pairs={{0,8},{1,9},{2,10},{3,11},{4,12},{5,13},{6,14},{7,15},{8,0},{9,1},... | collective-permute-start | bytes 245768 | tf_op jit(solution)/shard_map/ppermute | solution.py:572
  39.7 14.5 %collective-permute-start.6 = (f32[5,2,16,128]{3,2,1,0:T(8,128)S(1)}, f32[5,2,16,128]{3,2,1,0:T(8,128)S(1)}, u32[]{:S(2)}, u32[]{:S(2)}) collective-permute-start(f32[5,2,16,128]{3,2,1,0:T(8,128)S(1)} %get-tuple-element.44), channel_id=1, source_target_pairs={{0,9},{1,8},{2,11},{3,10},{4,13},{5,12},{6,15},{7,14},{8,1},{9,0},... | collective-permute-start | bytes 245768 | tf_op jit(solution)/shard_map/ppermute | solution.py:572

commit v6 on v5

--- a/solution.py
+++ b/solution.py
@@ -349,7 +349,7 @@
         body(slot)
         return carry
 
-    lax.fori_loop(begin, end, step, 0, unroll=4)
+    lax.fori_loop(begin, end, step, 0, unroll=3 if (end - begin) % 3 == 0 else 4)
 
 
 def level_one_all(sz, d_ref, f_ref, coef_at, slots, left, right, low, high, first, extent):

time: 57 us -> 56.9 us (level)
  no operation moved by 1% of the time
where the time goes in v6:
time: 56.9 us; the launch traced here: 56.6 us
  Pallas kernels  29.7 us (52%)
  waiting for transfers between devices  12.8 us (22%)
  starting transfers between devices  12.1 us (21%)
  local copies, waits for them, and re-layouts  1.87 us (3%)
    pallas_call x9, Pallas kernels, call(): pl.pallas_call(body, out_shape=tuple((x for x, _ in outs)), in_specs=[pl....  29.7 us
    ppermute x9, waiting for transfers between devices, per_device(): lax.ppermute(x, 'sub', [(i, i ^ by) for i in range(size)])  12.8 us
    ppermute x9, starting transfers between devices, per_device(): lax.ppermute(x, 'sub', [(i, i ^ by) for i in range(size)])  12.1 us
    unnamed x10, local copies, waits for them, and re-layouts  1.87 us
  transfers between devices with their start and end apart: 9, of which 5 were waited for; matrix products, arithmetic and copies ran while one was open for 0% of the time, Pallas kernels for 43%

profile of v6, /device:TPU:1, one launch (start us, length us, event | category | flops | bytes accessed | tf_op | source)
XLA Modules:
  0.0 56.6 jit_solution(4531158240714783127)
XLA Ops:
  0.0 2.8 %shard_map.55 = (f32[19,2,16,128]{3,2,1,0:T(8,128)}, f32[19,2,16,128]{3,2,1,0:T(8,128)}) custom-call(s32[16]{0:T(128)} %extent_ref.13, f32[2,64,8192]{2,1,0:T(8,128)} %images_ref.3, s32[2,2,64,64]{3,2,1,0:T(8,128)} %bitcast.40, f32[2,2,4,64]{3,2,1,0:T(4,128)} %bitcast.42, f32[2,2,2,64]{3,2,1,0:T(2,128)} %bitcast.44), custom_call_target="tpu_custom_call" | custom-call | flops 1 | bytes 1 | tf_op jit(solution)/shard_map/pallas_call | solution.py:44
  2.8 3.8 %collective-permute-start.1 = (f32[19,2,16,128]{3,2,1,0:T(8,128)}, f32[19,2,16,128]{3,2,1,0:T(8,128)S(1)}, u32[]{:S(2)}, u32[]{:S(2)}) collective-permute-start(f32[19,2,16,128]{3,2,1,0:T(8,128)} %get-tuple-element.36), channel_id=1, source_target_pairs={{0,9},{1,8},{2,11},{3,10},{4,13},{5,12},{6,15},{7,14},{8,1},{9,0},... | collective-permute-start | bytes 933896 | tf_op jit(solution)/shard_map/ppermute | solution.py:572
  6.6 0.0 copy-start.4
  6.6 0.0 collective-permute-start
  6.6 4.7 %shard_map.56 = (f32[9,2,16,128]{3,2,1,0:T(8,128)}, f32[9,2,16,128]{3,2,1,0:T(8,128)}, f32[5,2,16,128]{3,2,1,0:T(8,128)}, f32[5,2,16,128]{3,2,1,0:T(8,128)}, f32...) custom-call(s32[16]{0:T(128)} %extent_ref.13, ...), custom_call_target="tpu_custom_call" | custom-call | flops 1 | bytes 1 | tf_op jit(solution)/shard_map/pallas_call | solution.py:44
  11.3 0.0 copy-start.1
  11.3 0.0 copy-start.2
  11.3 0.4 collective-permute-start.2
  11.7 0.2 collective-permute-start.3
  11.9 0.3 collective-permute-start.4
  12.3 0.8 %collective-permute-done.2 = f32[13,2,16,128]{3,2,1,0:T(8,128)S(1)} collective-permute-done((f32[13,2,16,128]{3,2,1,0:T(8,128)}, f32[13,2,16,128]{3,2,1,0:T(8,128)S(1)}, u32[]{:S(2)}, u32[]{:S(2)}) %collective-permute-start.2) | collective-permute-done | bytes 213024 | tf_op jit(solution)/shard_map/ppermute | solution.py:572
  13.1 0.3 collective-permute-done.3
  13.4 0.3 collective-permute-done.4
  13.7 2.2 %collective-permute-start.7 = (f32[9,2,16,128]{3,2,1,0:T(8,128)}, f32[9,2,16,128]{3,2,1,0:T(8,128)S(1)}, u32[]{:S(2)}, u32[]{:S(2)}) collective-permute-start(f32[9,2,16,128]{3,2,1,0:T(8,128)} %get-tuple-element.51), channel_id=1, source_target_pairs={{0,8},{1,9},{2,10},{3,11},{4,12},{5,13},{6,14},{7,15},{8,0},{9,1},... | collective-permute-start | bytes 442376 | tf_op jit(solution)/shard_map/ppermute | solution.py:572
  15.9 0.6 %collective-permute-start.8 = (f32[9,2,16,128]{3,2,1,0:T(8,128)}, f32[9,2,16,128]{3,2,1,0:T(8,128)S(1)}, u32[]{:S(2)}, u32[]{:S(2)}) collective-permute-start(f32[9,2,16,128]{3,2,1,0:T(8,128)} %get-tuple-element.52), channel_id=1, source_target_pairs={{0,9},{1,8},{2,11},{3,10},{4,13},{5,12},{6,15},{7,14},{8,1},{9,0},... | collective-permute-start | bytes 442376 | tf_op jit(solution)/shard_map/ppermute | solution.py:572
  16.6 0.0 copy-done.4
  16.6 0.0 copy-start
  16.6 1.1 %copy-done = f32[35,2,16,128]{3,2,1,0:T(8,128)S(1)} copy-done((f32[35,2,16,128]{3,2,1,0:T(8,128)S(1)}, f32[35,2,16,128]{3,2,1,0:T(8,128)}, u32[]{:S(2)}) %copy-start) | copy-done | bytes 573464
  17.6 0.0 copy-start.3
  17.6 0.8 %copy-done.3 = f32[3,32,128]{2,1,0:T(8,128)S(1)} copy-done((f32[3,32,128]{2,1,0:T(8,128)S(1)}, f32[3,32,128]{2,1,0:T(8,128)}, u32[]{:S(2)}) %copy-start.3) | copy-done | bytes 49176
  18.4 9.9 %shard_map.57 = (f32[32,2,4,16,128]{4,3,2,1,0:T(8,128)S(1)}, f32[2,4,3,16,128]{4,3,2,1,0:T(8,128)S(1)}, f32[2,2,4,6,16,128]{5,4,3,2,1,0:T(8,128)S(1)}) custom-call(s32[16]{0:T(128)S(1)} %copy-done.4, f32[35,32,128]{2,1,0:T(8,128)S(1)} %bitcast.35, f32[3,32,128]{2,1,0:T(8,128)S(1)} %copy-done.3, f32[13,32,128]{2,1,0:T(8,128)S(1)} %bitcast.30, ...), custom_call_target="tpu_custom_call" | custom-call | flops 1 | bytes 1 | tf_op jit(solution)/shard_map/pallas_call | solution.py:44
  28.3 6.0 %collective-permute-done.1 = f32[19,2,16,128]{3,2,1,0:T(8,128)S(1)} collective-permute-done((f32[19,2,16,128]{3,2,1,0:T(8,128)}, f32[19,2,16,128]{3,2,1,0:T(8,128)S(1)}, u32[]{:S(2)}, u32[]{:S(2)}) %collective-permute-start.1) | collective-permute-done | bytes 311328 | tf_op jit(solution)/shard_map/ppermute | solution.py:572
  34.3 5.3 %collective-permute-done = f32[19,2,16,128]{3,2,1,0:T(8,128)S(1)} collective-permute-done((f32[19,2,16,128]{3,2,1,0:T(8,128)}, f32[19,2,16,128]{3,2,1,0:T(8,128)S(1)}, u32[]{:S(2)}, u32[]{:S(2)}) %collective-permute-start) | collective-permute-done | bytes 311328 | tf_op jit(solution)/shard_map/ppermute | solution.py:572
  39.6 0.0 copy-done.1
  39.6 0.0 copy-done.2
  39.6 0.0 collective-permute-start.5
  39.7 4.6 %collective-permute-start.6 = (f32[5,2,16,128]{3,2,1,0:T(8,128)S(1)}, f32[5,2,16,128]{3,2,1,0:T(8,128)S(1)}, u32[]{:S(2)}, u32[]{:S(2)}) collective-permute-start(f32[5,2,16,128]{3,2,1,0:T(8,128)S(1)} %get-tuple-element.44), channel_id=1, source_target_pairs={{0,9},{1,8},{2,11},{3,10},{4,13},{5,12},{6,15},{7,14},{8,1},{9,0},... | collective-permute-start | bytes 245768 | tf_op jit(solution)/shard_map/ppermute | solution.py:572
  44.2 1.8 %shard_map.59 = (f32[2,2,3,16,128]{4,3,2,1,0:T(8,128)S(1)}, f32[2,2,2,6,16,128]{5,4,3,2,1,0:T(8,128)S(1)}, f32[8,2,2,9,16,128]{5,4,3,2,1,0:T(8,128)S(1)}, f32[7,4,9,16,128]{4,3,2,1,0:T(8,128)S(1)}) custom-call(s32[16]{0:T(128)S(1)} %copy-done.4, f32[19,32,128]{2,1,0:T(8,128)S(1)} %bitcast.24, f32[19,32,128]{2,1,0:T(8,128)S(1)} %bitcast.18, ...), custom_call_target="tpu_custom_call" | custom-call | flops 1 | bytes 1 | tf_op jit(solution)/shard_map/pallas_call | solution.py:44
  46.1 4.8 %shard_map.61 = (f32[2,64,4096]{2,1,0:T(8,128)}, f32[2,2,32,128]{3,2,1,0:T(8,128)S(1)}, f32[2,2,32,128]{3,2,1,0:T(8,128)S(1)}) custom-call(s32[16]{0:T(128)S(1)} %copy-done.4, f32[19,32,128]{2,1,0:T(8,128)S(1)} %bitcast.25, f32[19,32,128]{2,1,0:T(8,128)S(1)} %bitcast.19, f32[19,32,128]{2,1,0:T(8,128)S(1)} %bitcast.26, f32[19,32,128]{2,1,0:T(8,128)S(1)} %bitcast.20, ...), custom_call_target="tpu_custom_call" | custom-call | flops 1 | bytes 1 | tf_op jit(solution)/shard_map/pallas_call | solution.py:44
  50.9 0.0 collective-permute-done.7
  50.9 0.0 collective-permute-done.8
  50.9 3.2 %shard_map.62 = (f32[2,64,4096]{2,1,0:T(8,128)}, f32[2,2,32,128]{3,2,1,0:T(8,128)S(1)}, f32[2,2,32,128]{3,2,1,0:T(8,128)S(1)}) custom-call(s32[16]{0:T(128)S(1)} %copy-done.4, f32[9,32,128]{2,1,0:T(8,128)S(1)} %bitcast.36, f32[9,32,128]{2,1,0:T(8,128)S(1)} %bitcast.37, f32[19,32,128]{2,1,0:T(8,128)S(1)} %bitcast.27, ...), custom_call_target="tpu_custom_call", output_to_operand_aliasing={{0}: (12, {})} | custom-call | flops 100000000 | bytes 300001 | tf_op jit(solution)/shard_map/pallas_call | solution.py:44
  54.1 0.0 collective-permute-done.5
  54.1 0.0 collective-permute-done.6
  54.1 2.5 %shard_map.63 = f32[2,64,4096]{2,1,0:T(8,128)} custom-call(s32[16]{0:T(128)S(1)} %copy-done.4, f32[5,32,128]{2,1,0:T(8,128)S(1)} %bitcast.38, f32[5,32,128]{2,1,0:T(8,128)S(1)} %bitcast.39, f32[19,32,128]{2,1,0:T(8,128)S(1)} %bitcast.28, f32[19,32,128]{2,1,0:T(8,128)S(1)} %bitcast.22, ...), custom_call_target="tpu_custom_call", output_to_operand_aliasing={{}: (10, {})} | custom-call | flops 100000000 | bytes 300001 | tf_op jit(solution)/shard_map/pallas_call | solution.py:44
  (2 shorter events, 0.0 us)
Async XLA Ops:
  2.8 31.5 %collective-permute-start.1 = (f32[19,2,16,128]{3,2,1,0:T(8,128)}, f32[19,2,16,128]{3,2,1,0:T(8,128)S(1)}, u32[]{:S(2)}, u32[]{:S(2)}) collective-permute-start(f32[19,2,16,128]{3,2,1,0:T(8,128)} %get-tuple-element.36), channel_id=1, source_target_pairs={{0,9},{1,8},{2,11},{3,10},{4,13},{5,12},{6,15},{7,14},{8,1},{9,0},... | collective-permute-start | bytes 933896 | tf_op jit(solution)/shard_map/ppermute | solution.py:572
  6.6 10.0 %copy-start.4 = (s32[16]{0:T(128)S(1)}, s32[16]{0:T(128)}, u32[]{:S(2)}) copy-start(s32[16]{0:T(128)} %extent_ref.13) | copy-start | bytes 196
  6.6 33.1 %collective-permute-start = (f32[19,2,16,128]{3,2,1,0:T(8,128)}, f32[19,2,16,128]{3,2,1,0:T(8,128)S(1)}, u32[]{:S(2)}, u32[]{:S(2)}) collective-permute-start(f32[19,2,16,128]{3,2,1,0:T(8,128)} %get-tuple-element.33._), channel_id=1, source_target_pairs={{0,8},{1,9},{2,10},{3,11},{4,12},{5,13},{6,14},{7,15},{8,0},{9,1},... | collective-permute-start | bytes 933896 | tf_op jit(solution)/shard_map/ppermute | solution.py:572
  11.3 28.3 %copy-start.1 = (f32[5,2,16,128]{3,2,1,0:T(8,128)S(1)}, f32[5,2,16,128]{3,2,1,0:T(8,128)}, u32[]{:S(2)}) copy-start(f32[5,2,16,128]{3,2,1,0:T(8,128)} %get-tuple-element.34.refs_0_) | copy-start | bytes 245764
  11.3 28.3 %copy-start.2 = (f32[5,2,16,128]{3,2,1,0:T(8,128)S(1)}, f32[5,2,16,128]{3,2,1,0:T(8,128)}, u32[]{:S(2)}) copy-start(f32[5,2,16,128]{3,2,1,0:T(8,128)} %get-tuple-element.35.refs_1_) | copy-start | bytes 245764
  11.3 1.7 %collective-permute-start.2 = (f32[13,2,16,128]{3,2,1,0:T(8,128)}, f32[13,2,16,128]{3,2,1,0:T(8,128)S(1)}, u32[]{:S(2)}, u32[]{:S(2)}) collective-permute-start(f32[13,2,16,128]{3,2,1,0:T(8,128)} %get-tuple-element.39), channel_id=1, source_target_pairs={{0,1},{1,0},{2,3},{3,2},{4,5},{5,4},{6,7},{7,6},{8,9},{9,8},{10,11... | collective-permute-start | bytes 638984 | tf_op jit(solution)/shard_map/ppermute | solution.py:572
  11.7 1.7 %collective-permute-start.3 = (f32[13,2,16,128]{3,2,1,0:T(8,128)}, f32[13,2,16,128]{3,2,1,0:T(8,128)S(1)}, u32[]{:S(2)}, u32[]{:S(2)}) collective-permute-start(f32[13,2,16,128]{3,2,1,0:T(8,128)} %get-tuple-element.40), channel_id=1, source_target_pairs={{0,1},{1,0},{2,3},{3,2},{4,5},{5,4},{6,7},{7,6},{8,9},{9,8},{10,11... | collective-permute-start | bytes 638984 | tf_op jit(solution)/shard_map/ppermute | solution.py:572
  11.9 1.8 %collective-permute-start.4 = (f32[13,2,16,128]{3,2,1,0:T(8,128)}, f32[13,2,16,128]{3,2,1,0:T(8,128)S(1)}, u32[]{:S(2)}, u32[]{:S(2)}) collective-permute-start(f32[13,2,16,128]{3,2,1,0:T(8,128)} %get-tuple-element.41), channel_id=1, source_target_pairs={{0,1},{1,0},{2,3},{3,2},{4,5},{5,4},{6,7},{7,6},{8,9},{9,8},{10,11... | collective-permute-start | bytes 638984 | tf_op jit(solution)/shard_map/ppermute | solution.py:572
  13.7 37.1 %collective-permute-start.7 = (f32[9,2,16,128]{3,2,1,0:T(8,128)}, f32[9,2,16,128]{3,2,1,0:T(8,128)S(1)}, u32[]{:S(2)}, u32[]{:S(2)}) collective-permute-start(f32[9,2,16,128]{3,2,1,0:T(8,128)} %get-tuple-element.51), channel_id=1, source_target_pairs={{0,8},{1,9},{2,10},{3,11},{4,12},{5,13},{6,14},{7,15},{8,0},{9,1},... | collective-permute-start | bytes 442376 | tf_op jit(solution)/shard_map/ppermute | solution.py:572
  15.9 35.0 %collective-permute-start.8 = (f32[9,2,16,128]{3,2,1,0:T(8,128)}, f32[9,2,16,128]{3,2,1,0:T(8,128)S(1)}, u32[]{:S(2)}, u32[]{:S(2)}) collective-permute-start(f32[9,2,16,128]{3,2,1,0:T(8,128)} %get-tuple-element.52), channel_id=1, source_target_pairs={{0,9},{1,8},{2,11},{3,10},{4,13},{5,12},{6,15},{7,14},{8,1},{9,0},... | collective-permute-start | bytes 442376 | tf_op jit(solution)/shard_map/ppermute | solution.py:572
  16.6 1.1 %copy-start = (f32[35,2,16,128]{3,2,1,0:T(8,128)S(1)}, f32[35,2,16,128]{3,2,1,0:T(8,128)}, u32[]{:S(2)}) copy-start(f32[35,2,16,128]{3,2,1,0:T(8,128)} %get-tuple-element.37) | copy-start | bytes 1720324
  17.6 0.8 %copy-start.3 = (f32[3,32,128]{2,1,0:T(8,128)S(1)}, f32[3,32,128]{2,1,0:T(8,128)}, u32[]{:S(2)}) copy-start(f32[3,32,128]{2,1,0:T(8,128)} %get-tuple-element.38.par) | copy-start | bytes 147460
  39.6 14.4 %collective-permute-start.5 = (f32[5,2,16,128]{3,2,1,0:T(8,128)S(1)}, f32[5,2,16,128]{3,2,1,0:T(8,128)S(1)}, u32[]{:S(2)}, u32[]{:S(2)}) collective-permute-start(f32[5,2,16,128]{3,2,1,0:T(8,128)S(1)} %get-tuple-element.43), channel_id=1, source_target_pairs={{0,8},{1,9},{2,10},{3,11},{4,12},{5,13},{6,14},{7,15},{8,0},{9,1},... | collective-permute-start | bytes 245768 | tf_op jit(solution)/shard_map/ppermute | solution.py:572
  39.7 14.4 %collective-permute-start.6 = (f32[5,2,16,128]{3,2,1,0:T(8,128)S(1)}, f32[5,2,16,128]{3,2,1,0:T(8,128)S(1)}, u32[]{:S(2)}, u32[]{:S(2)}) collective-permute-start(f32[5,2,16,128]{3,2,1,0:T(8,128)S(1)} %get-tuple-element.44), channel_id=1, source_target_pairs={{0,9},{1,8},{2,11},{3,10},{4,13},{5,12},{6,15},{7,14},{8,1},{9,0},... | collective-permute-start | bytes 245768 | tf_op jit(solution)/shard_map/ppermute | solution.py:572
